TPU v7x, 128 devices: a whole 4x4x4 slice. The times are simulated.
128 devices in a mesh: row: 4 (over x_hi, core), col: 32 (over z, x_lo, y).
Axes of the slice: x: 4 (x_hi: 2, x_lo: 2; x = x_hi * 2 + x_lo), y: 4, z: 4, core: 2. Of those that a mesh axis runs over, the one named last changes fastest.
Arguments:
- tokens: bfloat16 [2, 2048, 1536], P(None, 'col'), may hold values from -6 to 6
- memory: bfloat16 [2, 192, 1536], P(None, None, 'col'), may hold values from -6 to 6
- clip_lengths: int32 [2, 3], replicated, may hold values from 1 to 2046, as said below
- out_grad: bfloat16 [2, 2048, 1536], P(None, 'col'), may hold values from -6 to 6
- norm_gain: bfloat16 [2, 3, 1536], P(None, None, 'col'), may hold values from 0.25 to 1.75
- norm_bias: bfloat16 [2, 3, 1536], P(None, None, 'col'), may hold values from -1.5 to 1.5
- self_in: bfloat16 [2, 3, 1536, 1536], P(None, None, 'col', 'row'), may hold values from -0.15625 to 0.15625
- self_out: bfloat16 [2, 1536, 1536], P(None, 'row', 'col'), may hold values from -1.5 to 1.5
- text_query: bfloat16 [2, 1536, 1536], P(None, 'col', 'row'), may hold values from -0.15625 to 0.15625
- text_kv: bfloat16 [2, 2, 1536, 1536], P(None, None, 'col', 'row'), may hold values from -0.15625 to 0.15625
- text_out: bfloat16 [2, 1536, 1536], P(None, 'row', 'col'), may hold values from -0.75 to 0.75
- mlp_up: bfloat16 [2, 1536, 6144], P(None, 'col', 'row'), may hold values from -0.15625 to 0.15625
- mlp_down: bfloat16 [2, 6144, 1536], P(None, 'row', 'col'), may hold values from -0.078125 to 0.078125
Outputs:
- output: bfloat16 [2, 2048, 1536], P(None, 'col')
- input_grad: float32 [2, 2048, 1536], P(None, 'col')
- memory_grad: float32 [2, 192, 1536], P(None, None, 'col')
- norm_gain_grad: float32 [2, 3, 1536], P(None, None, 'col')
- norm_bias_grad: float32 [2, 2, 1536], P(None, None, 'col')
- ff_norm_bias_grad: float32 [2, 1536], P(None, 'col')
- self_in_grad: float32 [2, 3, 1536, 1536], P(None, None, 'col', 'row')
- self_out_grad: float32 [2, 1536, 1536], P(None, 'row', 'col')
- text_query_grad: float32 [2, 1536, 1536], P(None, 'col', 'row')
- text_kv_grad: float32 [2, 2, 1536, 1536], P(None, None, 'col', 'row')
- text_out_grad: float32 [2, 1536, 1536], P(None, 'row', 'col')
- mlp_up_grad: float32 [2, 1536, 6144], P(None, 'col', 'row')
- mlp_down_grad: float32 [2, 6144, 1536], P(None, 'row', 'col')
Inputs may be any that keep to these rules, and one draw needn't show every extreme that they name: `clip_lengths`: row m holds the lengths of the 3 clips of micro-batch m in order and sums to 2048; the first and the last clip are shorter than 64; in one micro-batch both are exactly 1 frame long.
All inputs are finite; a program needn't handle non-finite values.
Results may differ from a plain program's by a relative error of at most 0.023.
Values may be sent and summed in bfloat16 or wider, within the bound.
No kernel may reach another device: no remote copies, remote signals or barrier semaphores. Data moves between devices by JAX's collectives and lax.ppermute only.
A program may use at most 384 MiB of HBM per device.

v0:
```python
from functools import partial
import math

import jax
import jax.numpy as jnp
from jax import lax
from jax.sharding import PartitionSpec as P

HEAD = 64


NEG_FILL = -1e30
NORM_EPS = 1e-05


def sent_to_all(x, axis):
    peers = lax.axis_size(axis)
    return lax.all_to_all(jnp.broadcast_to(x[None], (peers, *x.shape)), axis, 0, 0, tiled=True)


def of_everyone(x, axis):
    return sent_to_all(x, axis).sum(axis=0)


def turned_gather(arrays, axis, dims):
    turned = [jnp.moveaxis(a, dim, 0) for a, dim in zip(arrays, dims)]
    widths = [t[0].size for t in turned]
    both = jnp.concatenate([t.reshape(-1, w) for t, w in zip(turned, widths)], axis=1)
    whole = lax.all_gather(both, axis, axis=0, tiled=True)
    pieces = jnp.split(whole, [sum(widths[:k]) for k in range(1, len(widths))], axis=1)
    return tuple(
        (
            jnp.moveaxis(b.reshape(-1, *t.shape[1:]), 0, dim)
            for b, t, dim in zip(pieces, turned, dims)
        )
    )


def sent_together(arrays, axis, dim, along):
    both = jnp.concatenate(arrays, axis=along)
    whole, at, done = (lax.all_gather(both, axis, axis=dim, tiled=True), 0, [])
    for a in arrays:
        done.append(lax.slice_in_dim(whole, at, at + a.shape[along], axis=along))
        at += a.shape[along]
    return tuple(done)


def filled_up(lines, peers):
    spare = -len(lines) % peers
    return jnp.pad(lines, [(0, spare)] + [(0, 0)] * (lines.ndim - 1))


def total_of(x, axis):
    lines = x.reshape(-1, *x.shape[1:][-1:])
    padded = filled_up(lines, lax.axis_size(axis))
    own = lax.psum_scatter(padded, axis, scatter_dimension=0, tiled=True)
    whole = lax.all_gather(own, axis, axis=0, tiled=True)
    return whole[: len(lines)].reshape(x.shape)


def sent_together_2(arrays, axis, dim, along):
    ends, at = ([], 0)
    for a in arrays[:-1]:
        at += a.shape[along]
        ends.append(at)
    both = jnp.concatenate(arrays, axis=along)
    return tuple(
        jnp.split(lax.psum_scatter(both, axis, scatter_dimension=dim, tiled=True), ends, axis=along)
    )


def norm_forward(values, gain_row, shift_row):
    centre = jnp.mean(values, axis=-1, keepdims=True)
    centred = values - centre
    inverse = lax.rsqrt(jnp.mean(centred * centred, axis=-1, keepdims=True) + NORM_EPS)
    unit_rows = centred * inverse
    return ((unit_rows * gain_row + shift_row).astype(jnp.bfloat16), unit_rows, inverse)


def norm_backward(upstream, unit_rows, inverse, gain_row):
    scaled = upstream * gain_row
    inner = (
        scaled
        - jnp.mean(scaled, axis=-1, keepdims=True)
        - unit_rows * jnp.mean(scaled * unit_rows, axis=-1, keepdims=True)
    )
    return (inner * inverse, jnp.sum(upstream * unit_rows, axis=0), jnp.sum(upstream, axis=0))


def clip_index(positions, lengths):
    clip_ends = jnp.cumsum(lengths)
    return jnp.sum((positions[:, None] >= clip_ends[None, :-1]).astype(jnp.int32), axis=1)


def masked_scores(queries, key_rows, allowed, score_scale):
    raw_scores = (
        jnp.einsum("rhd,khd->hrk", queries, key_rows, preferred_element_type=jnp.float32)
        * score_scale
    )
    return jnp.where(allowed[None], raw_scores, NEG_FILL)


def attend_forward(queries, key_rows, value_rows, allowed, score_scale):
    masked = masked_scores(queries, key_rows, allowed, score_scale)
    highest = jnp.max(masked, axis=-1, keepdims=True)
    log_total = highest + jnp.log(jnp.sum(jnp.exp(masked - highest), axis=-1, keepdims=True))
    weights = jnp.exp(masked - log_total).astype(jnp.bfloat16)
    mixed_rows = jnp.einsum("hrk,khd->rhd", weights, value_rows, preferred_element_type=jnp.float32)
    return (mixed_rows.astype(jnp.bfloat16).reshape(queries.shape[0], -1), log_total)


def attend_backward(upstream, queries, key_rows, value_rows, allowed, log_total, score_scale):
    weights = jnp.exp(masked_scores(queries, key_rows, allowed, score_scale) - log_total)
    weights_low = weights.astype(jnp.bfloat16)
    weight_grad = jnp.einsum(
        "rhd,khd->hrk", upstream, value_rows, preferred_element_type=jnp.float32
    )
    inner = jnp.sum(weights * weight_grad, axis=-1, keepdims=True)
    score_grad = (weights * (weight_grad - inner)).astype(jnp.bfloat16)
    query_grad = (
        jnp.einsum("hrk,khd->rhd", score_grad, key_rows, preferred_element_type=jnp.float32)
        * score_scale
    )
    key_grad = (
        jnp.einsum("hrk,rhd->khd", score_grad, queries, preferred_element_type=jnp.float32)
        * score_scale
    )
    value_grad = jnp.einsum(
        "hrk,rhd->khd", weights_low, upstream, preferred_element_type=jnp.float32
    )
    return (query_grad, key_grad, value_grad)


def row_forward(partial_sum):
    return of_everyone(partial_sum, "row")


def row_backward(partial_sum):
    return of_everyone(partial_sum, "row")


def project_in(normed, full_weight):
    projected = jnp.einsum("rd,gdh->rgh", normed, full_weight, preferred_element_type=jnp.float32)
    return (projected, normed)


def project_in_back(upstream, kept_rows, full_weight):
    partial_sum = jnp.einsum(
        "rgh,gdh->rd", upstream, full_weight, preferred_element_type=jnp.float32
    )
    weight_grad = jnp.einsum("rd,rgh->gdh", kept_rows, upstream, preferred_element_type=jnp.float32)
    return (row_backward(partial_sum), weight_grad)


def local(
    tokens,
    memory,
    clip_lengths,
    out_grad,
    norm_gain,
    norm_bias,
    self_in,
    self_out,
    text_query,
    text_kv,
    text_out,
    mlp_up,
    mlp_down,
):
    layer_count = self_in.shape[0]
    batch_count, row_count, model_width = tokens.shape
    text_count = memory.shape[1]
    head_width = self_in.shape[3]
    head_count = head_width // HEAD
    score_scale = 1.0 / math.sqrt(HEAD)
    self_out_full, text_out_full, down_full, gain_full, shift_full = turned_gather(
        (self_out, text_out, mlp_down, norm_gain, norm_bias), "col", (2, 2, 2, 2, 2)
    )
    gain_all = gain_full.astype(jnp.float32)
    shift_all = shift_full.astype(jnp.float32)
    self_in_full, query_full, up_full = turned_gather(
        (self_in, text_query, mlp_up), "col", (2, 1, 1)
    )
    col_count = lax.axis_size("col")
    query_places = lax.axis_index("col") * row_count + jnp.arange(row_count, dtype=jnp.int32)
    key_places = jnp.arange(row_count * col_count, dtype=jnp.int32)
    text_clip = jnp.arange(text_count, dtype=jnp.int32) // (text_count // clip_lengths.shape[1])
    grad_self_in = jnp.zeros(self_in_full.shape, jnp.float32)
    grad_query = jnp.zeros(query_full.shape, jnp.float32)
    grad_up = jnp.zeros(up_full.shape, jnp.float32)
    grad_text_kv = jnp.zeros(text_kv.shape, jnp.float32)
    grad_self_out = jnp.zeros(self_out_full.shape, jnp.float32)
    grad_text_out = jnp.zeros(text_out_full.shape, jnp.float32)
    grad_down = jnp.zeros(down_full.shape, jnp.float32)
    grad_gain = jnp.zeros(gain_full.shape, jnp.float32)
    grad_shift = jnp.zeros(gain_full.shape, jnp.float32)
    outputs = []
    input_grads = []
    memory_grads = []
    for batch_index in range(batch_count):
        lengths = clip_lengths[batch_index]
        frame_clip = clip_index(query_places, lengths)
        key_clip = clip_index(key_places, lengths)
        self_allowed = (frame_clip[:, None] == key_clip[None, :]) & (
            key_places[None, :] <= query_places[:, None]
        )
        text_allowed = frame_clip[:, None] == text_clip[None, :]
        text_rows = memory[batch_index]
        residual = tokens[batch_index].astype(jnp.float32)
        kept_layers = []
        for layer_index in range(layer_count):
            normed_one, unit_one, inverse_one = norm_forward(
                residual, gain_all[layer_index, 0], shift_all[layer_index, 0]
            )
            projected, kept_self = project_in(normed_one, self_in_full[layer_index])
            projected = projected.astype(jnp.bfloat16)
            own_query = projected[:, 0].reshape(row_count, head_count, HEAD)
            keys_all, values_all = sent_together((projected[:, 1], projected[:, 2]), "col", 0, 1)
            keys_all = keys_all.reshape(-1, head_count, HEAD)
            values_all = values_all.reshape(-1, head_count, HEAD)
            self_mixed, self_total = attend_forward(
                own_query, keys_all, values_all, self_allowed, score_scale
            )
            residual_one = residual + row_forward(
                jnp.dot(self_mixed, self_out_full[layer_index], preferred_element_type=jnp.float32)
            )
            normed_two, unit_two, inverse_two = norm_forward(
                residual_one, gain_all[layer_index, 1], shift_all[layer_index, 1]
            )
            cross_proj, kept_cross = project_in(normed_two, query_full[layer_index][None])
            cross_query = cross_proj[:, 0].astype(jnp.bfloat16).reshape(row_count, head_count, HEAD)
            text_pair = lax.psum(
                jnp.einsum(
                    "md,gdh->mgh",
                    text_rows,
                    text_kv[layer_index],
                    preferred_element_type=jnp.float32,
                ),
                "col",
            ).astype(jnp.bfloat16)
            text_keys = text_pair[:, 0].reshape(text_count, head_count, HEAD)
            text_values = text_pair[:, 1].reshape(text_count, head_count, HEAD)
            cross_mixed, cross_total = attend_forward(
                cross_query, text_keys, text_values, text_allowed, score_scale
            )
            residual_two = residual_one + row_forward(
                jnp.dot(cross_mixed, text_out_full[layer_index], preferred_element_type=jnp.float32)
            )
            normed_three, unit_three, inverse_three = norm_forward(
                residual_two, gain_all[layer_index, 2], shift_all[layer_index, 2]
            )
            hidden_proj, kept_up = project_in(normed_three, up_full[layer_index][None])
            hidden = hidden_proj[:, 0]
            active = jax.nn.gelu(hidden, approximate=False).astype(jnp.bfloat16)
            residual = residual_two + row_forward(
                jnp.dot(active, down_full[layer_index], preferred_element_type=jnp.float32)
            )
            kept_layers.append(
                (
                    unit_one,
                    inverse_one,
                    kept_self,
                    own_query,
                    keys_all,
                    values_all,
                    self_mixed,
                    self_total,
                    unit_two,
                    inverse_two,
                    kept_cross,
                    cross_query,
                    text_keys,
                    text_values,
                    cross_mixed,
                    cross_total,
                    unit_three,
                    inverse_three,
                    kept_up,
                    hidden,
                    active,
                )
            )
        outputs.append(residual.astype(jnp.bfloat16))
        gradient = out_grad[batch_index].astype(jnp.float32)
        text_grad = jnp.zeros((text_count, text_rows.shape[1]), jnp.float32)
        for layer_index in reversed(range(layer_count)):
            (
                unit_one,
                inverse_one,
                kept_self,
                own_query,
                keys_all,
                values_all,
                self_mixed,
                self_total,
                unit_two,
                inverse_two,
                kept_cross,
                cross_query,
                text_keys,
                text_values,
                cross_mixed,
                cross_total,
                unit_three,
                inverse_three,
                kept_up,
                hidden,
                active,
            ) = kept_layers[layer_index]
            grad_low = gradient.astype(jnp.bfloat16)
            grad_down = grad_down.at[layer_index].add(
                jnp.einsum("rf,rd->fd", active, grad_low, preferred_element_type=jnp.float32)
            )
            grad_active = jnp.einsum(
                "rd,fd->rf", grad_low, down_full[layer_index], preferred_element_type=jnp.float32
            )
            gelu_value, gelu_pull = jax.vjp(partial(jax.nn.gelu, approximate=False), hidden)
            grad_hidden = gelu_pull(grad_active)[0].astype(jnp.bfloat16)
            grad_normed, up_grad = project_in_back(
                grad_hidden[:, None], kept_up, up_full[layer_index][None]
            )
            grad_up = grad_up.at[layer_index].add(up_grad[0])
            norm_grad, gain_grad, shift_grad = norm_backward(
                grad_normed, unit_three, inverse_three, gain_all[layer_index, 2]
            )
            grad_gain = grad_gain.at[layer_index, 2].add(gain_grad)
            grad_shift = grad_shift.at[layer_index, 2].add(shift_grad)
            gradient = gradient + norm_grad
            grad_low = gradient.astype(jnp.bfloat16)
            grad_text_out = grad_text_out.at[layer_index].add(
                jnp.einsum("rh,rd->hd", cross_mixed, grad_low, preferred_element_type=jnp.float32)
            )
            grad_mixed = (
                jnp.einsum(
                    "rd,hd->rh",
                    grad_low,
                    text_out_full[layer_index],
                    preferred_element_type=jnp.float32,
                )
                .astype(jnp.bfloat16)
                .reshape(row_count, head_count, HEAD)
            )
            query_grad, key_grad, value_grad = attend_backward(
                grad_mixed,
                cross_query,
                text_keys,
                text_values,
                text_allowed,
                cross_total,
                score_scale,
            )
            pair_term = jnp.stack(
                [
                    key_grad.reshape(text_count, head_width),
                    value_grad.reshape(text_count, head_width),
                ],
                axis=1,
            )
            pair_grad = total_of(pair_term, "col").astype(jnp.bfloat16)
            grad_text_kv = grad_text_kv.at[layer_index].add(
                jnp.einsum("md,mgh->gdh", text_rows, pair_grad, preferred_element_type=jnp.float32)
            )
            text_grad = text_grad + jnp.einsum(
                "mgh,gdh->md", pair_grad, text_kv[layer_index], preferred_element_type=jnp.float32
            )
            grad_normed, cross_grad = project_in_back(
                query_grad.astype(jnp.bfloat16).reshape(row_count, 1, head_width),
                kept_cross,
                query_full[layer_index][None],
            )
            grad_query = grad_query.at[layer_index].add(cross_grad[0])
            norm_grad, gain_grad, shift_grad = norm_backward(
                grad_normed, unit_two, inverse_two, gain_all[layer_index, 1]
            )
            grad_gain = grad_gain.at[layer_index, 1].add(gain_grad)
            grad_shift = grad_shift.at[layer_index, 1].add(shift_grad)
            gradient = gradient + norm_grad
            grad_low = gradient.astype(jnp.bfloat16)
            grad_self_out = grad_self_out.at[layer_index].add(
                jnp.einsum("rh,rd->hd", self_mixed, grad_low, preferred_element_type=jnp.float32)
            )
            grad_mixed = (
                jnp.einsum(
                    "rd,hd->rh",
                    grad_low,
                    self_out_full[layer_index],
                    preferred_element_type=jnp.float32,
                )
                .astype(jnp.bfloat16)
                .reshape(row_count, head_count, HEAD)
            )
            query_grad, key_grad, value_grad = attend_backward(
                grad_mixed, own_query, keys_all, values_all, self_allowed, self_total, score_scale
            )
            key_sum, value_sum = sent_together_2(
                (key_grad.reshape(-1, head_width), value_grad.reshape(-1, head_width)), "col", 0, 1
            )
            triple_grad = jnp.stack(
                [query_grad.reshape(row_count, head_width), key_sum, value_sum], axis=1
            ).astype(jnp.bfloat16)
            grad_normed, triple_weight = project_in_back(
                triple_grad, kept_self, self_in_full[layer_index]
            )
            grad_self_in = grad_self_in.at[layer_index].add(triple_weight)
            norm_grad, gain_grad, shift_grad = norm_backward(
                grad_normed, unit_one, inverse_one, gain_all[layer_index, 0]
            )
            grad_gain = grad_gain.at[layer_index, 0].add(gain_grad)
            grad_shift = grad_shift.at[layer_index, 0].add(shift_grad)
            gradient = gradient + norm_grad
        input_grads.append(gradient)
        memory_grads.append(row_backward(text_grad))
    self_out_grad, text_out_grad, down_grad, gain_out, shift_out = sent_together_2(
        (grad_self_out, grad_text_out, grad_down, grad_gain, grad_shift), "col", 2, 1
    )
    self_in_grad, query_grad_out, up_grad_out = (
        lax.psum_scatter(grad_self_in, "col", scatter_dimension=2, tiled=True),
        *sent_together_2((grad_query, grad_up), "col", 1, 2),
    )
    return (
        jnp.stack(outputs),
        jnp.stack(input_grads),
        jnp.stack(memory_grads),
        gain_out,
        shift_out[:, 0:2],
        shift_out[:, 2],
        self_in_grad,
        self_out_grad,
        query_grad_out,
        grad_text_kv,
        text_out_grad,
        up_grad_out,
        down_grad,
    )


def solution(mesh):
    return jax.shard_map(
        local,
        mesh=mesh,
        in_specs=(
            P(None, "col", None),
            P(None, None, "col"),
            P(),
            P(None, "col", None),
            P(None, None, "col"),
            P(None, None, "col"),
            P(None, None, "col", "row"),
            P(None, "row", "col"),
            P(None, "col", "row"),
            P(None, None, "col", "row"),
            P(None, "row", "col"),
            P(None, "col", "row"),
            P(None, "row", "col"),
        ),
        out_specs=(
            P(None, "col", None),
            P(None, "col", None),
            P(None, None, "col"),
            P(None, None, "col"),
            P(None, None, "col"),
            P(None, "col"),
            P(None, None, "col", "row"),
            P(None, "row", "col"),
            P(None, "col", "row"),
            P(None, None, "col", "row"),
            P(None, "row", "col"),
            P(None, "col", "row"),
            P(None, "row", "col"),
        ),
        check_vma=False,
    )
```

profile of v0, /device:TPU:1, one launch (start us, length us, event | category | flops | bytes accessed | tf_op | source)
XLA Modules:
  0.0 4199.1 jit_solution(3274039159420682373)
XLA Ops:
  16.7 166.9 %all-gather.11.cloned.1.call-done = bf16[1536,4620]{1,0:T(8,128)(2,1)} async-done(((bf16[48,4620]{1,0:T(8,128)(2,1)}), bf16[1536,4620]{1,0:T(8,128)(2,1)}) %all-gather.11.cloned.1.call-update) | async-done | bytes 14192656 | tf_op jit(solution)/shard_map/all_gather | solution.py:29
  186.8 225.0 %all-gather.13.cloned.1.call-done = bf16[1536,6144]{1,0:T(8,128)(2,1)} async-done(((bf16[48,6144]{1,0:T(8,128)(2,1)}), bf16[1536,6144]{1,0:T(8,128)(2,1)}) %all-gather.13.cloned.1.call-update) | async-done | bytes 18874384 | tf_op jit(solution)/shard_map/all_gather | solution.py:29
  411.9 6.3 split.99
  418.2 10.3 copy.623
  428.5 10.3 copy.624
  451.3 123.6 %all-gather.15.cloned.1.call-done = bf16[2048,768]{1,0:T(8,128)(2,1)} async-done(((bf16[64,768]{1,0:T(8,128)(2,1)}), bf16[2048,768]{1,0:T(8,128)(2,1)}) %all-gather.15.cloned.1.call-update) | async-done | bytes 3145744 | tf_op jit(solution)/shard_map/all_gather | solution.py:41
  588.7 45.1 %all_to_all.130 = f32[4,64,1536]{2,1,0:T(8,128)} all-to-all(f32[4,64,1536]{2,1,0:T(8,128)S(1)} %broadcast_in_dim.138), channel_id=1, replica_groups=mesh['row'=4,'col'=32] {'row'}, dimensions={0} | all-to-all | bytes 3145728 | tf_op jit(solution)/shard_map/all_to_all | solution.py:18
  645.0 170.2 %all-reduce.25 = (bf16[192,2,384]{2,0,1:T(8,128)(2,1)}, bf16[192,2,384]{2,0,1:T(8,128)(2,1)}, bf16[192,2,384]{2,0,1:T(8,128)(2,1)}, bf16[192,2,384]{2,0,1:T(8,128)(2,1)}) all-reduce(f32[192,2,384]{2,0,1:T(8,128)} %fusion.370, f32[192,2,384]{2,0,1:T(8,128)} %fusion.364, ...), channel_id=1, replica_groups=mesh['row'=4,'col'=32] {'col'}, use_global_device_ids=true, to_apply=%region_39.40 | all-reduce | flops 589824 | bytes 3538944 | tf_op jit(solution)/shard_map/psum | solution.py:232
  833.5 26.6 all-to-all-start.6
  903.9 13.7 all-to-all-done.1
  925.5 8.2 split.104
  933.7 12.7 copy.634
  946.4 8.1 split.103
  954.5 8.1 copy.756
  979.8 25.4 all_to_all.131
  1023.8 30.1 all_to_all.132
  1062.9 84.2 %all-gather.17.cloned.1.call-done = bf16[2048,768]{1,0:T(8,128)(2,1)} async-done(((bf16[64,768]{1,0:T(8,128)(2,1)}), bf16[2048,768]{1,0:T(8,128)(2,1)}) %all-gather.17.cloned.1.call-update) | async-done | bytes 3145744 | tf_op jit(solution)/shard_map/all_gather | solution.py:41
  1162.0 23.8 all-to-all-start.3
  1185.8 119.6 %all-gather.21.cloned.1.call-done = bf16[2048,768]{1,0:T(8,128)(2,1)} async-done(((bf16[64,768]{1,0:T(8,128)(2,1)}), bf16[2048,768]{1,0:T(8,128)(2,1)}) %all-gather.21.cloned.1.call-update) | async-done | bytes 3145744 | tf_op jit(solution)/shard_map/all_gather | solution.py:41
  1322.6 25.2 all-to-all-start.9
  1360.7 7.9 all-to-all-done.9
  1396.4 12.6 all-to-all-done.4
  1421.8 15.7 all-to-all-done.10
  1466.6 16.1 all-to-all-done.12
  1502.0 9.0 all-to-all-done.5
  1528.0 11.4 all-to-all-done.18
  1554.6 13.5 all-to-all-done.11
  1599.8 10.5 all-to-all-done.13
  1619.3 18.4 all-to-all-done.19
  1699.4 124.0 %reduce-scatter.13.cloned.1.call-done = f32[64,768]{1,0:T(8,128)} async-done(((f32[2048,768]{1,0:T(8,128)}), f32[64,768]{1,0:T(8,128)}) %reduce-scatter.13.cloned.1.call-update) | async-done | bytes 196624 | tf_op jit(solution)/shard_map/reduce_scatter | solution.py:68
  1829.5 27.1 all-to-all-start.14
  1858.7 139.3 %reduce-scatter.17.cloned.1.call-done = f32[64,768]{1,0:T(8,128)} async-done(((f32[2048,768]{1,0:T(8,128)}), f32[64,768]{1,0:T(8,128)}) %reduce-scatter.17.cloned.1.call-update) | async-done | bytes 196624 | tf_op jit(solution)/shard_map/reduce_scatter | solution.py:68
  2004.8 28.3 all-to-all-start.20
  2035.6 18.3 all-to-all-done.20
  2081.5 12.3 all-to-all-done.15
  2101.2 19.9 all-to-all-done.21
  2145.4 16.1 all-to-all-done.16
  2169.6 18.5 all-to-all-done.22
  2263.9 8.8 pad_maximum_fusion
  2272.7 34.9 copy.701
  2330.6 35.6 reduce-scatter.15.cloned.1.call-done
  2367.1 172.9 %reduce-scatter.19.cloned.1.call-done = f32[64,768]{1,0:T(8,128)} async-done(((f32[2048,768]{1,0:T(8,128)}), f32[64,768]{1,0:T(8,128)}) %reduce-scatter.19.cloned.1.call-update) | async-done | bytes 196624 | tf_op jit(solution)/shard_map/reduce_scatter | solution.py:68
  2545.8 12.9 pad_maximum_fusion.3
  2558.8 7.2 bitcast_dynamic-update-slice_fusion.1
  2566.0 7.1 fusion.7
  2573.1 22.0 copy.700
  2604.8 12.5 pad_maximum_fusion.1
  2623.5 10.1 fusion.5
  2654.8 27.1 all-to-all-start.17
  2700.8 18.6 all-to-all-done.17
  2738.1 25.7 all-to-all-done.23
  2793.2 66.4 %concatenate.164 = f32[2,2310,1536]{2,1,0:T(8,128)} concatenate(f32[2,384,1536]{2,1,0:T(8,128)} %fusion.35, f32[2,384,1536]{2,1,0:T(8,128)} %fusion.33, f32[2,1536,1536]{2,1,0:T(8,128)} %fusion.5, f32[2,3,1536]{2,1,0:T(4,128)S(1)} %scatter-add.184, f32[2,3,1536]{2,1,0:T(4,128)} %scatter-add.204), dimensions={1} | concatenate | bytes 56770560 | tf_op jit(solution)/shard_map/concatenate | solution.py:66
  2859.6 43.6 %copy.698 = f32[2,2310,1536]{1,0,2:T(2,128)} copy(f32[2,2310,1536]{2,1,0:T(8,128)} %concatenate.164) | data formatting | bytes 56770560 | tf_op jit(solution)/shard_map/concatenate | solution.py:66
  2927.0 113.6 %fusion.450 = (f32[16,384]{1,0:T(8,128)S(1)}, f32[16,384]{1,0:T(8,128)S(1)}, f32[16,384]{1,0:T(8,128)S(1)}, f32[16,384]{1,0:T(8,128)S(1)}) fusion(f32[384,384]{1,0:T(8,128)S(1)} %reshape.6384, f32[384,384]{1,0:T(8,128)} %reshape.6385, f32[384,384]{1,0:T(8,128)S(1)} %copy-done.110, f32[384,384]{1,0:T(8,128)} %reshape.6383), kind=kCustom, calls=%all-reduce-scatter.4 | all-reduce-scatter fusion | flops 786433 | bytes 2458112
  3053.0 8.0 collective-permute-start.17
  3064.5 9.0 collective-permute-start.30
  3094.0 130.9 %all-gather.2 = bf16[32,12,384]{2,1,0:T(8,128)(2,1)S(1)} all-gather(bf16[1,12,384]{2,1,0:T(8,128)(2,1)S(1)} %dynamic-slice_bitcast_fusion.1), channel_id=1, replica_groups=mesh['row'=4,'col'=32] {'col'}, dimensions={0}, use_global_device_ids=true | all-gather | bytes 304128 | tf_op jit(solution)/shard_map/all_gather | solution.py:57
  3239.5 74.0 %all-gather.3 = bf16[32,12,384]{2,1,0:T(8,128)(2,1)S(1)} all-gather(bf16[1,12,384]{2,1,0:T(8,128)(2,1)S(1)} %dynamic-slice_bitcast_fusion), channel_id=1, replica_groups=mesh['row'=4,'col'=32] {'col'}, dimensions={0}, use_global_device_ids=true | all-gather | bytes 304128 | tf_op jit(solution)/shard_map/all_gather | solution.py:57
  3318.8 56.3 %all-to-all-start.25 = ((f32[4,192,48]{1,2,0:T(8,128)}), f32[4,192,48]{1,2,0:T(8,128)}, u32[]{:S(2)}, u32[]{:S(2)}) async-start(f32[4,192,48]{1,2,0:T(8,128)} %broadcast_in_dim.167), calls=%async_computation.29 | async-start | bytes 393216 | tf_op jit(solution)/shard_map/all_to_all | solution.py:18
  3385.9 6.9 collective-permute-start.15
  3402.2 77.7 %all-gather = bf16[32,12,384]{2,1,0:T(8,128)(2,1)S(1)} all-gather(bf16[1,12,384]{2,1,0:T(8,128)(2,1)S(1)} %dynamic-slice_bitcast_fusion.3), channel_id=1, replica_groups=mesh['row'=4,'col'=32] {'col'}, dimensions={0}, use_global_device_ids=true | all-gather | bytes 304128 | tf_op jit(solution)/shard_map/all_gather | solution.py:57
  3481.5 70.4 %all-gather.1 = bf16[32,12,384]{2,1,0:T(8,128)(2,1)S(1)} all-gather(bf16[1,12,384]{2,1,0:T(8,128)(2,1)S(1)} %dynamic-slice_bitcast_fusion.2), channel_id=1, replica_groups=mesh['row'=4,'col'=32] {'col'}, dimensions={0}, use_global_device_ids=true | all-gather | bytes 304128 | tf_op jit(solution)/shard_map/all_gather | solution.py:57
  3558.5 25.9 all-to-all-start.24
  3604.7 577.7 %all-reduce.20.cloned.1.call-done = f32[2,2310,1536]{1,0,2:T(2,128)} async-done(((f32[2,2310,1536]{1,0,2:T(2,128)}), f32[2,2310,1536]{1,0,2:T(2,128)}) %all-reduce.20.cloned.1.call-update) | async-done | bytes 28385296
  (1346 shorter events, 859.8 us)
Async XLA Ops:
  7.2 176.4 %all-gather.11.cloned.1.call-start = ((), (), s32[]{:S(2)}) async-start(), calls=%async_computation.30 | async-start | bytes 15003648 | tf_op jit(solution)/shard_map/all_gather | solution.py:29
  12.6 399.2 %all-gather.13.cloned.1.call-start = ((), (), s32[]{:S(2)}) async-start(), calls=%async_computation.31 | async-start | bytes 19464192 | tf_op jit(solution)/shard_map/all_gather | solution.py:29
  15.7 559.1 %all-gather.15.cloned.1.call-start = ((), (), s32[]{:S(2)}) async-start(), calls=%async_computation.32 | async-start | bytes 3244032 | tf_op jit(solution)/shard_map/all_gather | solution.py:41
  442.4 375.8 %all-gather.19.cloned.1.call-start = ((), (), s32[]{:S(2)}) async-start(), calls=%async_computation.34 | async-start | bytes 3244032 | tf_op jit(solution)/shard_map/all_gather | solution.py:41
  833.5 49.9 %all-to-all-start.6 = ((f32[4,64,1536]{2,1,0:T(8,128)}), f32[4,64,1536]{2,1,0:T(8,128)}, u32[]{:S(2)}, u32[]{:S(2)}) async-start(f32[4,64,1536]{2,1,0:T(8,128)} %broadcast_in_dim.147), calls=%async_computation.6 | async-start | bytes 3145728 | tf_op jit(solution)/shard_map/all_to_all | solution.py:18
  892.0 25.6 all-to-all-start.1
  919.9 45.0 %all-to-all-start.7 = ((f32[4,64,1536]{2,1,0:T(8,128)}), f32[4,64,1536]{2,1,0:T(8,128)}, u32[]{:S(2)}, u32[]{:S(2)}) async-start(f32[4,64,1536]{2,1,0:T(8,128)} %broadcast_in_dim.149), calls=%async_computation.7 | async-start | bytes 3145728 | tf_op jit(solution)/shard_map/all_to_all | solution.py:18
  925.1 222.0 %all-gather.17.cloned.1.call-start = ((), (), s32[]{:S(2)}) async-start(), calls=%async_computation.33 | async-start | bytes 3244032 | tf_op jit(solution)/shard_map/all_gather | solution.py:41
  1013.1 292.4 %all-gather.21.cloned.1.call-start = ((), (), s32[]{:S(2)}) async-start(), calls=%async_computation.35 | async-start | bytes 3244032 | tf_op jit(solution)/shard_map/all_gather | solution.py:41
  1162.0 158.2 %all-to-all-start.3 = ((f32[4,64,1536]{2,1,0:T(8,128)}), f32[4,64,1536]{2,1,0:T(8,128)}, u32[]{:S(2)}, u32[]{:S(2)}) async-start(f32[4,64,1536]{2,1,0:T(8,128)} %broadcast_in_dim.143), calls=%async_computation.3 | async-start | bytes 3145728 | tf_op jit(solution)/shard_map/all_to_all | solution.py:18
  1322.6 46.0 %all-to-all-start.9 = ((f32[4,64,1536]{2,1,0:T(8,128)}), f32[4,64,1536]{2,1,0:T(8,128)}, u32[]{:S(2)}, u32[]{:S(2)}) async-start(f32[4,64,1536]{2,1,0:T(8,128)} %broadcast_in_dim.151), calls=%async_computation.9 | async-start | bytes 3145728 | tf_op jit(solution)/shard_map/all_to_all | solution.py:18
  1383.0 26.0 all-to-all-start.4
  1411.3 26.2 all-to-all-start.10
  1456.7 26.0 all-to-all-start.12
  1485.1 26.0 all-to-all-start.5
  1513.4 26.0 all-to-all-start.18
  1541.7 26.4 all-to-all-start.11
  1584.3 26.0 all-to-all-start.13
  1611.6 26.0 all-to-all-start.19
  1616.8 206.5 %reduce-scatter.13.cloned.1.call-start = ((), (), s32[]{:S(2)}) async-start(), calls=%async_computation.36 | async-start | bytes 6488064 | tf_op jit(solution)/shard_map/reduce_scatter | solution.py:68
  1672.8 325.1 %reduce-scatter.17.cloned.1.call-start = ((), (), s32[]{:S(2)}) async-start(), calls=%async_computation.38 | async-start | bytes 6488064 | tf_op jit(solution)/shard_map/reduce_scatter | solution.py:68
  1829.5 172.7 %all-to-all-start.14 = ((f32[4,64,1536]{2,1,0:T(8,128)}), f32[4,64,1536]{2,1,0:T(8,128)S(1)}, u32[]{:S(2)}, u32[]{:S(2)}) async-start(f32[4,64,1536]{2,1,0:T(8,128)} %broadcast_in_dim.156), calls=%async_computation.15 | async-start | bytes 3145728 | tf_op jit(solution)/shard_map/all_to_all | solution.py:18
  2004.8 49.2 %all-to-all-start.20 = ((f32[4,64,1536]{2,1,0:T(8,128)}), f32[4,64,1536]{2,1,0:T(8,128)}, u32[]{:S(2)}, u32[]{:S(2)}) async-start(f32[4,64,1536]{2,1,0:T(8,128)} %broadcast_in_dim.162), calls=%async_computation.23 | async-start | bytes 3145728 | tf_op jit(solution)/shard_map/all_to_all | solution.py:18
  2068.2 25.6 all-to-all-start.15
  2095.1 26.0 all-to-all-start.21
  2135.4 26.1 all-to-all-start.16
  2162.9 25.3 all-to-all-start.22
  2167.4 198.8 %reduce-scatter.15.cloned.1.call-start = ((), (), s32[]{:S(2)}) async-start(), calls=%async_computation.37 | async-start | bytes 6488064 | tf_op jit(solution)/shard_map/reduce_scatter | solution.py:68
  2219.0 321.1 %reduce-scatter.19.cloned.1.call-start = ((), (), s32[]{:S(2)}) async-start(), calls=%async_computation.39 | async-start | bytes 6488064 | tf_op jit(solution)/shard_map/reduce_scatter | solution.py:68
  2243.5 1354.9 %all-reduce.24.cloned.1.call-start = ((), (), s32[]{:S(2)}) async-start(), calls=%async_computation.42 | async-start | bytes 47185920
  2307.6 1295.1 %all-reduce.22.cloned.1.call-start = ((), (), s32[]{:S(2)}) async-start(), calls=%async_computation.41 | async-start | bytes 28311552
  2654.8 64.5 %all-to-all-start.17 = ((f32[4,64,1536]{2,1,0:T(8,128)}), f32[4,64,1536]{2,1,0:T(8,128)}, u32[]{:S(2)}, u32[]{:S(2)}) async-start(f32[4,64,1536]{2,1,0:T(8,128)} %broadcast_in_dim.159), calls=%async_computation.19 | async-start | bytes 3145728 | tf_op jit(solution)/shard_map/all_to_all | solution.py:18
  2720.8 43.1 %all-to-all-start.23 = ((f32[4,64,1536]{2,1,0:T(8,128)}), f32[4,64,1536]{2,1,0:T(8,128)}, u32[]{:S(2)}, u32[]{:S(2)}) async-start(f32[4,64,1536]{2,1,0:T(8,128)} %broadcast_in_dim.165), calls=%async_computation.27 | async-start | bytes 3145728 | tf_op jit(solution)/shard_map/all_to_all | solution.py:18
  2726.4 1456.0 %all-reduce.20.cloned.1.call-start = ((), (), s32[]{:S(2)}) async-start(), calls=%async_computation.40 | async-start | bytes 59768832
  3041.9 19.1 collective-permute-start.21
  3046.4 18.0 collective-permute-start.20
  3047.7 25.7 collective-permute-start.19
  3051.7 25.8 collective-permute-start.18
  3053.0 27.3 collective-permute-start.17
  3061.1 21.4 collective-permute-start.16
  3064.5 23.4 collective-permute-start.30
  3073.5 17.5 collective-permute-start.29
  3077.5 147.6 %collective-permute-start.28 = (bf16[16,384]{1,0:T(8,128)(2,1)S(1)}, bf16[16,384]{1,0:T(8,128)(2,1)S(1)}, u32[]{:S(2)}, u32[]{:S(2)}) collective-permute-start(bf16[16,384]{1,0:T(8,128)(2,1)S(1)} %convert.132), channel_id=1, source_target_pairs={{0,5},{1,6},{2,7},{3,8},{4,9},{5,10},{6,11},{7,12},{8,13},{9,14},{... | collective-permute-start | bytes 36872
  3080.3 146.1 %collective-permute-start.27 = (bf16[16,384]{1,0:T(8,128)(2,1)S(1)}, bf16[16,384]{1,0:T(8,128)(2,1)S(1)}, u32[]{:S(2)}, u32[]{:S(2)}) collective-permute-start(bf16[16,384]{1,0:T(8,128)(2,1)S(1)} %convert.132), channel_id=1, source_target_pairs={{0,4},{1,5},{2,6},{3,7},{4,8},{5,9},{6,10},{7,11},{8,12},{9,13},{1... | collective-permute-start | bytes 36872
  3085.1 142.6 %collective-permute-start.26 = (bf16[16,384]{1,0:T(8,128)(2,1)S(1)}, bf16[16,384]{1,0:T(8,128)(2,1)S(1)}, u32[]{:S(2)}, u32[]{:S(2)}) collective-permute-start(bf16[16,384]{1,0:T(8,128)(2,1)S(1)} %convert.132), channel_id=1, source_target_pairs={{0,3},{1,4},{2,5},{3,6},{4,7},{5,8},{6,9},{7,10},{8,11},{9,12},{10... | collective-permute-start | bytes 36872
  3087.9 141.1 %collective-permute-start.25 = (bf16[16,384]{1,0:T(8,128)(2,1)S(1)}, bf16[16,384]{1,0:T(8,128)(2,1)S(1)}, u32[]{:S(2)}, u32[]{:S(2)}) collective-permute-start(bf16[16,384]{1,0:T(8,128)(2,1)S(1)} %convert.132), channel_id=1, source_target_pairs={{0,2},{1,3},{2,4},{3,5},{4,6},{5,7},{6,8},{7,9},{8,10},{9,11},{10,... | collective-permute-start | bytes 36872
  3091.0 141.3 %collective-permute-start.24 = (bf16[16,384]{1,0:T(8,128)(2,1)S(1)}, bf16[16,384]{1,0:T(8,128)(2,1)S(1)}, u32[]{:S(2)}, u32[]{:S(2)}) collective-permute-start(bf16[16,384]{1,0:T(8,128)(2,1)S(1)} %convert.132), channel_id=1, source_target_pairs={{0,1},{1,2},{2,3},{3,4},{4,5},{5,6},{6,7},{7,8},{8,9},{9,10},{10,1... | collective-permute-start | bytes 36872
  3225.1 90.1 %collective-permute-start.6 = (bf16[16,384]{1,0:T(8,128)(2,1)S(1)}, bf16[16,384]{1,0:T(8,128)(2,1)S(1)}, u32[]{:S(2)}, u32[]{:S(2)}) collective-permute-start(bf16[16,384]{1,0:T(8,128)(2,1)S(1)} %convert.131), channel_id=1, source_target_pairs={{0,7},{1,8},{2,9},{3,10},{4,11},{5,12},{6,13},{7,14},{8,15},{9,16}... | collective-permute-start | bytes 36872
  3226.4 90.1 %collective-permute-start.5 = (bf16[16,384]{1,0:T(8,128)(2,1)S(1)}, bf16[16,384]{1,0:T(8,128)(2,1)S(1)}, u32[]{:S(2)}, u32[]{:S(2)}) collective-permute-start(bf16[16,384]{1,0:T(8,128)(2,1)S(1)} %convert.131), channel_id=1, source_target_pairs={{0,6},{1,7},{2,8},{3,9},{4,10},{5,11},{6,12},{7,13},{8,14},{9,15},... | collective-permute-start | bytes 36872
  3227.7 147.3 %collective-permute-start.4 = (bf16[16,384]{1,0:T(8,128)(2,1)S(1)}, bf16[16,384]{1,0:T(8,128)(2,1)S(1)}, u32[]{:S(2)}, u32[]{:S(2)}) collective-permute-start(bf16[16,384]{1,0:T(8,128)(2,1)S(1)} %convert.131), channel_id=1, source_target_pairs={{0,5},{1,6},{2,7},{3,8},{4,9},{5,10},{6,11},{7,12},{8,13},{9,14},{... | collective-permute-start | bytes 36872
  3229.0 147.3 %collective-permute-start.3 = (bf16[16,384]{1,0:T(8,128)(2,1)S(1)}, bf16[16,384]{1,0:T(8,128)(2,1)S(1)}, u32[]{:S(2)}, u32[]{:S(2)}) collective-permute-start(bf16[16,384]{1,0:T(8,128)(2,1)S(1)} %convert.131), channel_id=1, source_target_pairs={{0,4},{1,5},{2,6},{3,7},{4,8},{5,9},{6,10},{7,11},{8,12},{9,13},{1... | collective-permute-start | bytes 36872
  3232.3 81.6 %collective-permute-start.7 = (bf16[12,384]{1,0:T(8,128)(2,1)S(1)}, bf16[12,384]{1,0:T(8,128)(2,1)S(1)}, u32[]{:S(2)}, u32[]{:S(2)}) collective-permute-start(bf16[12,384]{1,0:T(8,128)(2,1)S(1)} %slice.1548), channel_id=1, source_target_pairs={{0,8},{1,9},{2,10},{3,11},{4,12},{5,13},{6,14},{7,15},{8,16},{9,17... | collective-permute-start | bytes 27656
  3314.0 63.7 %collective-permute-start.2 = (bf16[16,384]{1,0:T(8,128)(2,1)S(1)}, bf16[16,384]{1,0:T(8,128)(2,1)S(1)}, u32[]{:S(2)}, u32[]{:S(2)}) collective-permute-start(bf16[16,384]{1,0:T(8,128)(2,1)S(1)} %convert.131), channel_id=1, source_target_pairs={{0,3},{1,4},{2,5},{3,6},{4,7},{5,8},{6,9},{7,10},{8,11},{9,12},{10... | collective-permute-start | bytes 36872
  3315.3 64.4 %collective-permute-start.1 = (bf16[16,384]{1,0:T(8,128)(2,1)S(1)}, bf16[16,384]{1,0:T(8,128)(2,1)S(1)}, u32[]{:S(2)}, u32[]{:S(2)}) collective-permute-start(bf16[16,384]{1,0:T(8,128)(2,1)S(1)} %convert.131), channel_id=1, source_target_pairs={{0,2},{1,3},{2,4},{3,5},{4,6},{5,7},{6,8},{7,9},{8,10},{9,11},{10,... | collective-permute-start | bytes 36872
  3316.6 69.3 %collective-permute-start = (bf16[16,384]{1,0:T(8,128)(2,1)S(1)}, bf16[16,384]{1,0:T(8,128)(2,1)S(1)}, u32[]{:S(2)}, u32[]{:S(2)}) collective-permute-start(bf16[16,384]{1,0:T(8,128)(2,1)S(1)} %convert.131), channel_id=1, source_target_pairs={{0,1},{1,2},{2,3},{3,4},{4,5},{5,6},{6,7},{7,8},{8,9},{9,10},{10,1... | collective-permute-start | bytes 36872
  3318.8 239.0 %all-to-all-start.25 = ((f32[4,192,48]{1,2,0:T(8,128)}), f32[4,192,48]{1,2,0:T(8,128)}, u32[]{:S(2)}, u32[]{:S(2)}) async-start(f32[4,192,48]{1,2,0:T(8,128)} %broadcast_in_dim.167), calls=%async_computation.29 | async-start | bytes 393216 | tf_op jit(solution)/shard_map/all_to_all | solution.py:18
  3375.1 22.7 collective-permute-start.14
  3376.4 24.0 collective-permute-start.13
  3377.7 102.4 %collective-permute-start.12 = (bf16[16,384]{1,0:T(8,128)(2,1)S(1)}, bf16[16,384]{1,0:T(8,128)(2,1)S(1)}, u32[]{:S(2)}, u32[]{:S(2)}) collective-permute-start(bf16[16,384]{1,0:T(8,128)(2,1)S(1)} %convert.130), channel_id=1, source_target_pairs={{0,5},{1,6},{2,7},{3,8},{4,9},{5,10},{6,11},{7,12},{8,13},{9,14},{... | collective-permute-start | bytes 36872
  3379.6 100.5 %collective-permute-start.11 = (bf16[16,384]{1,0:T(8,128)(2,1)S(1)}, bf16[16,384]{1,0:T(8,128)(2,1)S(1)}, u32[]{:S(2)}, u32[]{:S(2)}) collective-permute-start(bf16[16,384]{1,0:T(8,128)(2,1)S(1)} %convert.130), channel_id=1, source_target_pairs={{0,4},{1,5},{2,6},{3,7},{4,8},{5,9},{6,10},{7,11},{8,12},{9,13},{1... | collective-permute-start | bytes 36872
  3394.1 86.0 %collective-permute-start.10 = (bf16[16,384]{1,0:T(8,128)(2,1)S(1)}, bf16[16,384]{1,0:T(8,128)(2,1)S(1)}, u32[]{:S(2)}, u32[]{:S(2)}) collective-permute-start(bf16[16,384]{1,0:T(8,128)(2,1)S(1)} %convert.130), channel_id=1, source_target_pairs={{0,3},{1,4},{2,5},{3,6},{4,7},{5,8},{6,9},{7,10},{8,11},{9,12},{10... | collective-permute-start | bytes 36872
  3397.8 82.3 %collective-permute-start.9 = (bf16[16,384]{1,0:T(8,128)(2,1)S(1)}, bf16[16,384]{1,0:T(8,128)(2,1)S(1)}, u32[]{:S(2)}, u32[]{:S(2)}) collective-permute-start(bf16[16,384]{1,0:T(8,128)(2,1)S(1)} %convert.130), channel_id=1, source_target_pairs={{0,2},{1,3},{2,4},{3,5},{4,6},{5,7},{6,8},{7,9},{8,10},{9,11},{10,... | collective-permute-start | bytes 36872
  3400.4 79.8 %collective-permute-start.8 = (bf16[16,384]{1,0:T(8,128)(2,1)S(1)}, bf16[16,384]{1,0:T(8,128)(2,1)S(1)}, u32[]{:S(2)}, u32[]{:S(2)}) collective-permute-start(bf16[16,384]{1,0:T(8,128)(2,1)S(1)} %convert.130), channel_id=1, source_target_pairs={{0,1},{1,2},{2,3},{3,4},{4,5},{5,6},{6,7},{7,8},{8,9},{9,10},{10,1... | collective-permute-start | bytes 36872
  3558.5 34.6 all-to-all-start.24
  (365 other events, 9589.2 us)
Sparse Core Ops, SparseCore 0:
  12.7 170.8 all-gather.10
  185.8 225.9 all-gather.12
  442.5 132.3 all-gather.14
  640.8 137.7 all-gather.18
  1013.2 133.8 all-gather.16
  1149.2 156.2 all-gather.20
  1673.0 150.3 reduce-scatter.12
  1825.8 172.1 reduce-scatter.16
  2219.1 147.0 reduce-scatter.14
  2368.5 171.5 reduce-scatter.18
  2542.6 604.8 all-reduce.23
  3150.0 364.7 all-reduce.21
  3517.3 664.9 all-reduce.19
where the time goes:
time: 4220 us; the launch traced here: 4200 us
  waiting for transfers between devices  2030 us (48%)
  blocking collectives  737 us (17%)
  local copies, waits for them, and re-layouts  490 us (12%)
  starting transfers between devices  409 us (10%)
  matrix products  270 us (6%)
  other arithmetic  238 us (6%)
    unnamed x48, waiting for transfers between devices  578 us
    reduce_scatter x4, waiting for transfers between devices, sent_together_2(): lax.psum_scatter(both, axis, scatter_dimension=dim, tiled=True)  472 us
    all_gather x2, waiting for transfers between devices, turned_gather(): whole = lax.all_gather(both, axis, axis=0, tiled=True)  392 us
    all_gather x4, blocking collectives, total_of(): whole = lax.all_gather(own, axis, axis=0, tiled=True)  353 us
    all_gather x4, waiting for transfers between devices, sent_together(): whole, at, done = (lax.all_gather(both, axis, axis=dim, tiled=True), 0, [])  327 us
    all_to_all x23, starting transfers between devices, sent_to_all(): lax.all_to_all(jnp.broadcast_to(x[None], (peers, *x.shape)), axis, 0, 0,...  318 us
    all_to_all x23, waiting for transfers between devices, sent_to_all(): lax.all_to_all(jnp.broadcast_to(x[None], (peers, *x.shape)), axis, 0, 0,...  264 us
    psum x1, blocking collectives, local(): lax.psum(jnp.einsum('md,gdh->mgh', text_rows, text_kv[layer_index], prefe...  170 us
  transfers between devices with their start and end apart: 68, of which 28 were waited for; matrix products, arithmetic and copies ran while one was open for 19% of the time, Pallas kernels for 0%

commit v1 on v0

v1 whole, which is shorter than its diff:
```python
import math

import jax
import jax.numpy as jnp
from jax import lax
from jax.sharding import Mesh, PartitionSpec as P

HEAD = 64
HEADS_HERE = 3
WIDE = HEAD * HEADS_HERE
NEG_FILL = -1e30
NORM_EPS = 1e-05
SCALE = 1.0 / math.sqrt(HEAD)
LOW = jnp.bfloat16
FULL = jnp.float32

FINE = ("xh", "core", "zh", "zl", "xl", "y")
FINE_SIZES = (2, 2, 2, 2, 2, 4)
ROW = ("xh", "core")
COL = ("zh", "zl", "xl", "y")
CHIPS = ("xh", "xl")
SPREAD = ("zh", "zl", "y")
KEYED = ("zl", "y")
SWAP = ((0, 1), (1, 0))


def flipped(size, mask):
    return [(i, i ^ mask) for i in range(size)]


def swapped(x, axis):
    return lax.ppermute(x, axis, SWAP)


def rows_of_all(rows):
    chips = [rows] + [lax.ppermute(rows, CHIPS, flipped(4, d)) for d in (1, 2, 3)]
    half = jnp.concatenate(chips, axis=0)
    return jnp.concatenate([half, swapped(half, "core")], axis=0)


def sum_to_rows(partial):
    count = partial.shape[0] // 8
    blocks = partial.reshape(2, 4, count, partial.shape[1])
    both = blocks[0].astype(FULL) + swapped(blocks[1].astype(LOW), "core").astype(FULL)
    low = both.astype(LOW)
    total = both[0]
    for d in (1, 2, 3):
        total = total + lax.ppermute(low[d], CHIPS, flipped(4, d)).astype(FULL)
    return total


def keys_of_all(block):
    parts = [block]
    for d in range(1, 8):
        parts.append(lax.ppermute(block, KEYED, flipped(8, d)))
    return jnp.concatenate(parts, axis=0)


def sum_to_keys(partial):
    blocks = partial.reshape(8, -1, partial.shape[1])
    low = blocks.astype(LOW)
    total = blocks[0].astype(FULL)
    for d in range(1, 8):
        total = total + lax.ppermute(low[d], KEYED, flipped(8, d)).astype(FULL)
    return total


def mm(a, b, dims):
    return lax.dot_general(a, b, (dims, ((), ())), preferred_element_type=FULL)


def nn(a, b):
    return mm(a, b, ((1,), (0,)))


def nt(a, b):
    return mm(a, b, ((1,), (1,)))


def tn(a, b):
    return mm(a, b, ((0,), (0,)))


def unit(values):
    centre = jnp.mean(values, axis=-1, keepdims=True)
    centred = values - centre
    inverse = lax.rsqrt(jnp.mean(centred * centred, axis=-1, keepdims=True) + NORM_EPS)
    return centred * inverse, inverse


def unit_back(upstream, unit_rows, inverse, gain_row):
    scaled = upstream * gain_row
    inner = (
        scaled
        - jnp.mean(scaled, axis=-1, keepdims=True)
        - unit_rows * jnp.mean(scaled * unit_rows, axis=-1, keepdims=True)
    )
    return inner * inverse


def heads_of(x):
    return x.reshape(x.shape[0], HEADS_HERE, HEAD)


def scores_of(q, k, allowed):
    raw = jnp.einsum("qhd,khd->hqk", heads_of(q), heads_of(k), preferred_element_type=FULL) * SCALE
    return jnp.where(allowed[None], raw, NEG_FILL)


def attend(q, k, v, allowed):
    s = scores_of(q, k, allowed)
    top = jnp.max(s, axis=-1, keepdims=True)
    lse = top + jnp.log(jnp.sum(jnp.exp(s - top), axis=-1, keepdims=True))
    p = jnp.exp(s - lse).astype(LOW)
    o = jnp.einsum("hqk,khd->qhd", p, heads_of(v), preferred_element_type=FULL)
    return o.reshape(q.shape).astype(LOW), lse


def attend_back(do, q, k, v, allowed, lse):
    p = jnp.exp(scores_of(q, k, allowed) - lse)
    dp = jnp.einsum("qhd,khd->hqk", heads_of(do), heads_of(v), preferred_element_type=FULL)
    ds = (p * (dp - jnp.sum(p * dp, axis=-1, keepdims=True))).astype(LOW)
    dq = jnp.einsum("hqk,khd->qhd", ds, heads_of(k), preferred_element_type=FULL) * SCALE
    dk = jnp.einsum("hqk,qhd->khd", ds, heads_of(q), preferred_element_type=FULL) * SCALE
    dv = jnp.einsum("hqk,qhd->khd", p.astype(LOW), heads_of(do), preferred_element_type=FULL)
    return dq.reshape(q.shape), dk.reshape(k.shape), dv.reshape(v.shape)


def gelu(z):
    return 0.5 * z * (1.0 + lax.erf(z * math.sqrt(0.5)))


def gelu_slope(z):
    half = 0.5 * (1.0 + lax.erf(z * math.sqrt(0.5)))
    return half + z * jnp.exp(-0.5 * z * z) * (1.0 / math.sqrt(2.0 * math.pi))


def width_mixed(x):
    lead = x.shape[:-1]
    parts = x.reshape(*lead, 4, 2, 4, -1)
    return jnp.swapaxes(parts, -2, -3).reshape(*lead, -1)


def width_restored(x):
    lead = x.shape[:-1]
    parts = x.reshape(*lead, 4, 4, 2, -1)
    return jnp.swapaxes(parts, -2, -3).reshape(*lead, -1)


def local(
    tokens,
    memory,
    clip_lengths,
    out_grad,
    norm_gain,
    norm_bias,
    self_in,
    self_out,
    text_query,
    text_kv,
    text_out,
    mlp_up,
    mlp_down,
):
    xh, core, zh = lax.axis_index("xh"), lax.axis_index("core"), lax.axis_index("zh")
    zl, xl, y = lax.axis_index("zl"), lax.axis_index("xl"), lax.axis_index("y")
    row = xh * 2 + core
    width = tokens.shape[2]
    strip = memory.shape[2]
    ff = mlp_up.shape[2] // 2

    def halves(x, axis):
        size = x.shape[axis] // 2
        a = lax.slice_in_dim(x, 0, size, axis=axis)
        b = lax.slice_in_dim(x, size, 2 * size, axis=axis)
        return a, b

    def joined(*pairs):
        return tuple(jnp.concatenate(side, axis=1) for side in zip(*pairs))

    def common(x):
        return x, x

    def spread(pair):
        first, second = pair
        mine = jnp.where(xl == 0, first, second)
        theirs = swapped(jnp.where(xl == 0, second, first), "xl")
        both = jnp.where(
            xl == 0, jnp.concatenate([mine, theirs]), jnp.concatenate([theirs, mine])
        )
        return lax.all_gather(both, SPREAD, axis=0, tiled=True)

    norms = jnp.concatenate([norm_gain.reshape(6, strip), norm_bias.reshape(6, strip)])
    norms = jnp.pad(norms.T, ((0, 0), (0, 52)))
    memory_t = memory.reshape(-1, strip).T

    def own_in(l):
        return joined(*[halves(self_in[l, k], 1) for k in range(3)])

    def own_out(w, l):
        return halves(w[l].T, 1)

    def own_text(l):
        return joined(*[halves(text_kv[l, k], 1) for k in range(2)])

    def own_ff(l):
        return joined(halves(mlp_up[l], 1), own_out(mlp_down, l))

    piece_0 = spread(joined(own_in(0), common(norms)))
    piece_1 = spread(
        joined(
            own_text(0),
            common(memory_t),
            own_out(self_out, 0),
            halves(text_query[0], 1),
            own_out(text_out, 0),
            common(jnp.zeros((strip, 64), LOW)),
        )
    )
    piece_2 = spread(own_ff(0))
    piece_3 = spread(
        joined(
            own_text(1),
            own_out(self_out, 1),
            halves(text_query[1], 1),
            own_out(text_out, 1),
            own_in(1),
        )
    )
    piece_4 = spread(own_ff(1))

    w_in = [piece_0[:, :576], piece_3[:, 960:1536]]
    norm_rows = piece_0[:, 576:588].astype(FULL).T
    gains = [norm_rows[0:3], norm_rows[3:6]]
    shifts = [norm_rows[6:9], norm_rows[9:12]]
    w_text = [piece_1[:, :384], piece_3[:, :384]]
    memory_all = piece_1[:, 384:768]
    w_out = [piece_1[:, 768:960], piece_3[:, 384:576]]
    w_query = [piece_1[:, 960:1152], piece_3[:, 576:768]]
    w_tout = [piece_1[:, 1152:1344], piece_3[:, 768:960]]
    w_up = [piece_2[:, :ff], piece_4[:, :ff]]
    w_down = [piece_2[:, ff:], piece_4[:, ff:]]

    def own_rows(x):
        here = width_mixed(lax.dynamic_slice_in_dim(x, row * 16, 16, axis=1))
        keep = jnp.where(zh == 0, here[0], here[1])
        send = jnp.where(zh == 0, here[1], here[0])
        return jnp.concatenate([keep, swapped(send, "zh")], axis=0)

    token_rows = own_rows(tokens)
    grad_rows = own_rows(out_grad)

    at = jnp.arange(2048, dtype=jnp.int32)
    d_z, d_y, d_c = at // 1024, (at // 256) % 4, (at // 128) % 2
    d_x, d_s, inner = (at // 32) % 4, (at // 16) % 2, at % 16
    block = (zh ^ d_s) * 16 + (zl ^ d_z) * 8 + (xl ^ (d_x & 1)) * 4 + (y ^ d_y)
    key_at = block * 64 + ((xh ^ (d_x >> 1)) * 2 + (core ^ d_c)) * 16 + inner
    lengths = jnp.where(zh == 0, clip_lengths[0], clip_lengths[1])
    end_0 = lengths[0]
    end_1 = lengths[0] + lengths[1]
    key_clip = (key_at >= end_0).astype(jnp.int32) + (key_at >= end_1).astype(jnp.int32)
    frame_at, frame_clip = key_at[:256], key_clip[:256]
    allowed = (frame_clip[:, None] == key_clip[None, :]) & (key_at[None, :] <= frame_at[:, None])
    text_allowed = frame_clip[:, None] == (jnp.arange(192, dtype=jnp.int32) // 64)[None, :]

    token_all = rows_of_all(token_rows)
    unit_all, _ = unit(token_all.astype(FULL))
    residual = token_rows.astype(FULL)
    kept = []
    for l in range(2):
        n_0, r_0 = unit(residual)
        if l == 0:
            a = (unit_all * gains[0][0] + shifts[0][0]).astype(LOW)
        else:
            a = rows_of_all((n_0 * gains[l][0] + shifts[l][0]).astype(LOW))
        qkv = nn(a, w_in[l]).astype(LOW)
        q = qkv[:, :WIDE]
        kv = keys_of_all(qkv[:, WIDE:])
        k, v = kv[:, :WIDE], kv[:, WIDE:]
        o, lse = attend(q, k, v, allowed)
        x1 = residual + sum_to_rows(nt(o, w_out[l]))
        n_1, r_1 = unit(x1)
        c = rows_of_all((n_1 * gains[l][1] + shifts[l][1]).astype(LOW))
        cq = nn(c, w_query[l]).astype(LOW)
        mkv = tn(memory_all, w_text[l]).astype(LOW)
        mkv = jnp.where(zh == 0, mkv[:192], mkv[192:])
        mk, mv = mkv[:, :WIDE], mkv[:, WIDE:]
        co, clse = attend(cq, mk, mv, text_allowed)
        x2 = x1 + sum_to_rows(nt(co, w_tout[l]))
        n_2, r_2 = unit(x2)
        e = rows_of_all((n_2 * gains[l][2] + shifts[l][2]).astype(LOW))
        u = nn(e, w_up[l])
        hmid = gelu(u).astype(LOW)
        residual = x2 + sum_to_rows(nt(hmid, w_down[l]))
        kept.append((n_0, r_0, a, q, k, v, o, lse, n_1, r_1, c, cq, mk, mv, co, clse, n_2, r_2, e, u, hmid))

    def frames_back(rows):
        pair = rows.reshape(2, 16, width)
        other = swapped(pair[1], "zh")
        mbs = jnp.where(zh == 0, jnp.stack([pair[0], other]), jnp.stack([other, pair[0]]))
        mbs = width_restored(mbs)
        both = jnp.stack([mbs, swapped(mbs, "core")])
        both = jnp.where(core == 0, both, both[::-1])
        four = jnp.stack([both, swapped(both, "xh")])
        four = jnp.where(xh == 0, four, four[::-1])
        return jnp.moveaxis(four.reshape(4, 2, 16, width), 0, 1).reshape(2, 64, width)

    output = frames_back(residual.astype(LOW))

    grad = grad_rows.astype(FULL)
    norm_sums = [[None] * 3, [None] * 3]
    reduced = []
    memory_partial = jnp.zeros((width, 384), FULL)

    def norm_step(l, k, grad, upstream, n, r):
        norm_sums[l][k] = (jnp.sum(upstream * n, axis=0), jnp.sum(upstream, axis=0))
        return grad + unit_back(upstream, n, r, gains[l][k])

    def gathered_sum(parts):
        both = jnp.concatenate([p.astype(LOW) for p in parts], axis=1)
        return lax.psum_scatter(both, SPREAD, scatter_dimension=0, tiled=True)

    for l in (1, 0):
        n_0, r_0, a, q, k, v, o, lse, n_1, r_1, c, cq, mk, mv, co, clse, n_2, r_2, e, u, hmid = kept[l]
        dy = rows_of_all(grad.astype(LOW))
        g_down = tn(dy, hmid)
        du = (nn(dy, w_down[l]) * gelu_slope(u)).astype(LOW)
        g_up = tn(e, du)
        reduced.append(gathered_sum([g_up, g_down]))
        grad = norm_step(l, 2, grad, sum_to_rows(nt(du, w_up[l])), n_2, r_2)

        dy = rows_of_all(grad.astype(LOW))
        g_tout = tn(dy, co)
        dco = nn(dy, w_tout[l]).astype(LOW)
        dcq, dmk, dmv = attend_back(dco, cq, mk, mv, text_allowed, clse)
        dcq = dcq.astype(LOW)
        dmkv = jnp.concatenate([dmk, dmv], axis=1).astype(LOW)
        none = jnp.zeros_like(dmkv)
        dmkv = jnp.where(
            zh == 0, jnp.concatenate([dmkv, none]), jnp.concatenate([none, dmkv])
        )
        g_text = nn(memory_all, dmkv)
        memory_partial = memory_partial + nt(w_text[l], dmkv)
        g_query = tn(c, dcq)
        grad = norm_step(l, 1, grad, sum_to_rows(nt(dcq, w_query[l])), n_1, r_1)

        dy = rows_of_all(grad.astype(LOW))
        g_out = tn(dy, o)
        do = nn(dy, w_out[l]).astype(LOW)
        dq, dk, dv = attend_back(do, q, k, v, allowed, lse)
        if l == 0:
            reduced.append(
                gathered_sum([g_text, memory_partial, g_out, g_query, g_tout, jnp.zeros((width, 64), LOW)])
            )
        dkv = sum_to_keys(jnp.concatenate([dk, dv], axis=1))
        dqkv = jnp.concatenate([dq, dkv], axis=1).astype(LOW)
        g_in = tn(a, dqkv)
        da = nt(dqkv, w_in[l])
        if l == 1:
            reduced.append(gathered_sum([g_text, g_out, g_query, g_tout, g_in]))
            grad = norm_step(l, 0, grad, sum_to_rows(da), n_0, r_0)
        else:
            norm_sums[0][0] = (jnp.sum(da * unit_all, axis=0), jnp.sum(da, axis=0))
            sums = jnp.stack(
                [norm_sums[i][j][0] for i in range(2) for j in range(3)]
                + [norm_sums[i][j][1] for i in range(2) for j in range(3)]
            )
            sums = jnp.pad(sums.T, ((0, 0), (0, 52)))
            reduced.append(gathered_sum([g_in, sums]))
            grad = grad + unit_back(sum_to_rows(da), n_0, r_0, gains[0][0])
    input_grad = frames_back(grad.astype(LOW)).astype(FULL)

    ff_1, rest_1, ff_0, rest_0, in_0 = reduced

    def strips(block):
        pair = block.reshape(2, strip, -1)
        mine = jnp.where(xl == 0, pair[0], pair[1])
        theirs = swapped(jnp.where(xl == 0, pair[1], pair[0]), "xl")
        return (
            jnp.where(xl == 0, mine, theirs).astype(FULL),
            jnp.where(xl == 0, theirs, mine).astype(FULL),
        )

    def cut(pair, start, size):
        return [x[:, start : start + size] for x in pair]

    def wide(pair, start, size):
        return jnp.concatenate(cut(pair, start, size), axis=1)

    def tall(pair, start, size):
        return wide(pair, start, size).T

    def everywhere(x):
        x = x + swapped(x.astype(LOW), "core").astype(FULL)
        return x + swapped(x.astype(LOW), "xh").astype(FULL)

    ff_1, rest_1, ff_0, rest_0, in_0 = [strips(b) for b in (ff_1, rest_1, ff_0, rest_0, in_0)]
    self_in_grad = jnp.stack(
        [
            jnp.stack([wide(in_0, k * WIDE, WIDE) for k in range(3)]),
            jnp.stack([wide(rest_1, 960 + k * WIDE, WIDE) for k in range(3)]),
        ]
    )
    text_kv_grad = jnp.stack(
        [jnp.stack([wide(p, k * WIDE, WIDE) for k in range(2)]) for p in (rest_0, rest_1)]
    )
    self_out_grad = jnp.stack([tall(rest_0, 768, WIDE), tall(rest_1, 384, WIDE)])
    text_query_grad = jnp.stack([wide(rest_0, 960, WIDE), wide(rest_1, 576, WIDE)])
    text_out_grad = jnp.stack([tall(rest_0, 1152, WIDE), tall(rest_1, 768, WIDE)])
    mlp_up_grad = jnp.stack([wide(ff_0, 0, ff), wide(ff_1, 0, ff)])
    mlp_down_grad = jnp.stack([tall(ff_0, ff, ff), tall(ff_1, ff, ff)])
    memory_grad = everywhere(sum(cut(rest_0, 384, 384))).T.reshape(2, 192, strip)
    norm_grads = everywhere(sum(cut(in_0, 576, 64)))[:, :12].T
    gain_grad = norm_grads[:6].reshape(2, 3, strip)
    shift_grad = norm_grads[6:].reshape(2, 3, strip)
    return (
        output,
        input_grad,
        memory_grad,
        gain_grad,
        shift_grad[:, 0:2],
        shift_grad[:, 2],
        self_in_grad,
        self_out_grad,
        text_query_grad,
        text_kv_grad,
        text_out_grad,
        mlp_up_grad,
        mlp_down_grad,
    )


def solution(mesh):
    fine = Mesh(mesh.devices.reshape(FINE_SIZES), FINE)
    frames = P(None, COL, None)
    strips = P(None, None, COL)
    return jax.shard_map(
        local,
        mesh=fine,
        in_specs=(
            frames,
            strips,
            P(),
            frames,
            strips,
            strips,
            P(None, None, COL, ROW),
            P(None, ROW, COL),
            P(None, COL, ROW),
            P(None, None, COL, ROW),
            P(None, ROW, COL),
            P(None, COL, ROW),
            P(None, ROW, COL),
        ),
        out_specs=(
            frames,
            frames,
            strips,
            strips,
            strips,
            P(None, COL),
            P(None, None, COL, ROW),
            P(None, ROW, COL),
            P(None, COL, ROW),
            P(None, None, COL, ROW),
            P(None, ROW, COL),
            P(None, COL, ROW),
            P(None, ROW, COL),
        ),
        check_vma=False,
    )
```

time: 4220 us -> 1030 us (0.24)
  waiting for transfers between devices: 2030 us -> 538 us
  blocking collectives: 737 us -> 0 us
  local copies, waits for them, and re-layouts: 490 us -> 112 us
  starting transfers between devices: 409 us -> 187 us
  matrix products: 270 us -> 96.1 us
  other arithmetic: 238 us -> 70.1 us
    all_gather x6 -> x5, waiting for transfers between devices: 719 us -> 52.7 us  [spread(): return lax.all_gather(both, SPREAD, axis=0, tiled=True)]
    unnamed x48 -> x10, waiting for transfers between devices: 578 us -> 0.16 us
    all_gather x4 -> x0, blocking collectives: 353 us -> none  [total_of(): whole = lax.all_gather(own, axis, axis=0, tiled=True)]
    all_to_all x23 -> x0, starting transfers between devices: 318 us -> none  [sent_to_all(): lax.all_to_all(jnp.broadcast_to(x[None], (peers, *x.shape)), axis, 0, 0,...]
    all_to_all x23 -> x0, waiting for transfers between devices: 264 us -> none  [sent_to_all(): lax.all_to_all(jnp.broadcast_to(x[None], (peers, *x.shape)), axis, 0, 0,...]
    ppermute x0 -> x146, waiting for transfers between devices: none -> 229 us  [the longest x36 64.9 us: sum_to_rows(): total = total + lax.ppermute(low[d], CHIPS, flipped(4, d)).astype(FULL)]
    reduce_scatter x4 -> x5, waiting for transfers between devices: 472 us -> 256 us  [gathered_sum(): return lax.psum_scatter(both, SPREAD, scatter_dimension=0, tiled=True)]
    ppermute x0 -> x146, starting transfers between devices: none -> 186 us  [the longest x46 61.2 us: swapped(): return lax.ppermute(x, axis, SWAP)]
  transfers between devices with their start and end apart: 68 -> 156, of which waited for: 28 -> 105; matrix products, arithmetic and copies ran while one was open for 19% -> 19% of each run, Pallas kernels for 0% -> 0%
where the time goes in v1:
time: 1030 us; the launch traced here: 1020 us
  waiting for transfers between devices  538 us (52%)
  starting transfers between devices  187 us (18%)
  local copies, waits for them, and re-layouts  112 us (11%)
  matrix products  96.1 us (9%)
  other arithmetic  70.1 us (7%)
  between operations  19.8 us (2%)
    reduce_scatter x5, waiting for transfers between devices, gathered_sum(): return lax.psum_scatter(both, SPREAD, scatter_dimension=0, tiled=True)  256 us
    dot_general x42, matrix products, mm(): return lax.dot_general(a, b, (dims, ((), ())), preferred_element_type=FULL)  68.9 us
    ppermute x36, waiting for transfers between devices, sum_to_rows(): total = total + lax.ppermute(low[d], CHIPS, flipped(4, d)).astype(FULL)  64.9 us
    ppermute x46, starting transfers between devices, swapped(): return lax.ppermute(x, axis, SWAP)  61.2 us
    unnamed x401, local copies, waits for them, and re-layouts  59.4 us
    ppermute x46, waiting for transfers between devices, swapped(): return lax.ppermute(x, axis, SWAP)  57.2 us
    all_gather x5, waiting for transfers between devices, spread(): return lax.all_gather(both, SPREAD, axis=0, tiled=True)  52.7 us
    ppermute x36, waiting for transfers between devices, rows_of_all(): lax.ppermute(rows, CHIPS, flipped(4, d))  51.1 us
  transfers between devices with their start and end apart: 156, of which 105 were waited for; matrix products, arithmetic and copies ran while one was open for 19% of the time, Pallas kernels for 0%

profile of v1, /device:TPU:1, one launch (start us, length us, event | category | flops | bytes accessed | tf_op | source)
XLA Modules:
  0.0 1022.4 jit_solution(650239729188450467)
XLA Ops:
  26.8 3.9 collective-permute-start
  42.3 3.9 collective-permute-done.2
  47.2 5.3 collective-permute-start.4
  54.4 8.0 all-gather.6.cloned.1.call-done
  63.5 5.1 slice_reduce_fusion.1
  77.7 6.2 collective-permute-done.7
  83.9 6.2 collective-permute-done.8
  90.8 3.3 collective-permute-done.11
  94.0 6.1 collective-permute-done.12
  106.2 22.2 %all-gather.8.cloned.1.call-done = bf16[1536,1408]{1,0:T(8,128)(2,1)} async-done(((bf16[96,1408]{1,0:T(8,128)(2,1)}), bf16[1536,1408]{1,0:T(8,128)(2,1)}) %all-gather.8.cloned.1.call-update) | async-done | bytes 4325392 | tf_op jit(solution)/shard_map/all_gather | solution.py:191
  136.4 4.2 collective-permute-done.16
  164.9 3.0 collective-permute-start.24
  169.4 3.4 collective-permute-done.24
  193.7 3.0 collective-permute-start.33
  213.1 3.0 collective-permute-start.38
  218.8 22.6 %all-gather.12.cloned.1.call-done = bf16[1536,1536]{1,0:T(8,128)(2,1)} async-done(((bf16[96,1536]{1,0:T(8,128)(2,1)}), bf16[1536,1536]{1,0:T(8,128)(2,1)}) %all-gather.12.cloned.1.call-update) | async-done | bytes 4718608 | tf_op jit(solution)/shard_map/all_gather | solution.py:191
  241.4 3.6 fusion.66
  254.3 2.9 collective-permute-done.41
  257.3 3.4 collective-permute-done.42
  263.1 3.0 collective-permute-done.44
  267.1 4.3 collective-permute-done.45
  271.4 3.9 collective-permute-done.46
  284.8 3.9 collective-permute-start.47
  297.2 3.0 collective-permute-start.49
  300.4 4.9 collective-permute-done.49
  330.3 3.6 collective-permute-start.57
  362.9 3.3 collective-permute-start.66
  367.0 3.3 collective-permute-start.78
  371.0 3.6 collective-permute-done.67
  394.9 3.0 collective-permute-start.86
  398.9 3.6 collective-permute-done.86
  420.7 3.1 bitcast_convert_fusion.2
  434.9 3.1 maximum_bitcast_fusion.17
  444.1 3.9 collective-permute-done.93
  456.2 4.5 collective-permute-done.98
  468.7 3.0 collective-permute-start.101
  472.7 3.6 collective-permute-done.101
  496.1 3.0 collective-permute-start.109
  500.1 3.6 collective-permute-done.109
  523.0 3.0 collective-permute-start.117
  527.0 3.6 collective-permute-done.117
  549.1 3.4 bitcast_convert_fusion
  563.1 3.0 maximum_bitcast_fusion.11
  572.6 3.3 collective-permute-start.128
  577.4 3.0 collective-permute-start.129
  586.9 4.0 collective-permute-done.129
  607.6 6.7 copy.243
  615.8 3.3 fusion.8
  622.6 3.3 fusion.5
  625.9 6.7 copy.239
  638.0 6.7 copy.241
  654.9 7.0 collective-permute-done.70
  665.5 3.2 fusion.9
  670.0 3.2 fusion.7
  674.6 3.0 collective-permute-start.132
  679.7 2.9 collective-permute-done.132
  694.0 6.5 copy.235
  701.1 8.0 collective-permute-done.136
  717.5 4.0 collective-permute-done.142
  721.5 32.1 %reduce-scatter.24.cloned.1.call-done = bf16[96,1536]{1,0:T(8,128)(2,1)} async-done(((bf16[1536,1536]{1,0:T(8,128)(2,1)}), bf16[96,1536]{1,0:T(8,128)(2,1)}) %reduce-scatter.24.cloned.1.call-update) | async-done | bytes 294928 | tf_op jit(solution)/shard_map/reduce_scatter | solution.py:321
  759.9 75.3 %reduce-scatter.20.cloned.1.call-done = bf16[96,1536]{1,0:T(8,128)(2,1)} async-done(((bf16[1536,1536]{1,0:T(8,128)(2,1)}), bf16[96,1536]{1,0:T(8,128)(2,1)}) %reduce-scatter.20.cloned.1.call-update) | async-done | bytes 294928 | tf_op jit(solution)/shard_map/reduce_scatter | solution.py:321
  842.1 74.5 %reduce-scatter.22.cloned.1.call-done = bf16[96,1536]{1,0:T(8,128)(2,1)} async-done(((bf16[1536,1536]{1,0:T(8,128)(2,1)}), bf16[96,1536]{1,0:T(8,128)(2,1)}) %reduce-scatter.22.cloned.1.call-update) | async-done | bytes 294928 | tf_op jit(solution)/shard_map/reduce_scatter | solution.py:321
  923.7 73.9 %reduce-scatter.16.cloned.1.call-done = bf16[96,1408]{1,0:T(8,128)(2,1)} async-done(((bf16[1536,1408]{1,0:T(8,128)(2,1)}), bf16[96,1408]{1,0:T(8,128)(2,1)}) %reduce-scatter.16.cloned.1.call-update) | async-done | bytes 270352 | tf_op jit(solution)/shard_map/reduce_scatter | solution.py:321
  1003.9 3.5 collective-permute-start.138
  (1074 shorter events, 465.1 us)
Async XLA Ops:
  7.2 55.2 %all-gather.6.cloned.1.call-start = ((), (), s32[]{:S(2)}) async-start(), calls=%async_computation.5 | async-start | bytes 2088960 | tf_op jit(solution)/shard_map/all_gather | solution.py:191
  14.4 113.9 %all-gather.8.cloned.1.call-start = ((), (), s32[]{:S(2)}) async-start(), calls=%async_computation.6 | async-start | bytes 4595712 | tf_op jit(solution)/shard_map/all_gather | solution.py:191
  24.0 163.4 %all-gather.10.cloned.1.call-start = ((), (), s32[]{:S(2)}) async-start(), calls=%async_computation.7 | async-start | bytes 5013504 | tf_op jit(solution)/shard_map/all_gather | solution.py:191
  26.8 11.0 %collective-permute-start = (bf16[16,1536]{1,0:T(8,128)(2,1)S(1)}, bf16[16,1536]{1,0:T(8,128)(2,1)S(1)}, u32[]{:S(2)}, u32[]{:S(2)}) collective-permute-start(bf16[16,1536]{1,0:T(8,128)(2,1)S(1)} %select_n.420), channel_id=1, source_target_pairs={{0,16},{16,0},{1,17},{17,1},{2,18},{18,2},{3,19},{19,3},{4,20},{20... | collective-permute-start | bytes 147464 | tf_op jit(solution)/shard_map/ppermute | solution.py:32
  32.2 42.0 %collective-permute-start.30 = (bf16[48,1536]{1,0:T(8,128)(2,1)S(1)}, bf16[48,1536]{1,0:T(8,128)(2,1)}, u32[]{:S(2)}, u32[]{:S(2)}) collective-permute-start(bf16[48,1536]{1,0:T(8,128)(2,1)S(1)} %get-tuple-element.265), channel_id=1, source_target_pairs={{0,4},{4,0},{1,5},{5,1},{2,6},{6,2},{3,7},{7,3},{8,12},{12,8},{9,1... | collective-permute-start | bytes 442376 | tf_op jit(solution)/shard_map/ppermute | solution.py:32
  34.6 126.9 %collective-permute-start.39 = (bf16[48,1536]{1,0:T(8,128)(2,1)}, bf16[48,1536]{1,0:T(8,128)(2,1)}, u32[]{:S(2)}, u32[]{:S(2)}) collective-permute-start(bf16[48,1536]{1,0:T(8,128)(2,1)} %get-tuple-element.263), channel_id=1, source_target_pairs={{0,4},{4,0},{1,5},{5,1},{2,6},{6,2},{3,7},{7,3},{8,12},{12,8},{9,1... | collective-permute-start | bytes 442376 | tf_op jit(solution)/shard_map/ppermute | solution.py:32
  71.8 12.1 %collective-permute-start.7 = (bf16[256,384]{0,1:T(8,128)(2,1)}, bf16[256,384]{0,1:T(8,128)(2,1)S(1)}, u32[]{:S(2)}, u32[]{:S(2)}) collective-permute-start(bf16[256,384]{0,1:T(8,128)(2,1)} %get-tuple-element.266), channel_id=1, source_target_pairs={{0,2},{1,3},{2,0},{3,1},{8,10},{9,11},{10,8},{11,9},{4,6},{5,7},{6... | collective-permute-start | bytes 589832 | tf_op jit(solution)/shard_map/ppermute | solution.py:55
  76.0 165.4 %all-gather.12.cloned.1.call-start = ((), (), s32[]{:S(2)}) async-start(), calls=%async_computation.8 | async-start | bytes 5013504 | tf_op jit(solution)/shard_map/all_gather | solution.py:191
  76.0 14.1 %collective-permute-start.8 = (bf16[256,384]{0,1:T(8,128)(2,1)}, bf16[256,384]{0,1:T(8,128)(2,1)S(1)}, u32[]{:S(2)}, u32[]{:S(2)}) collective-permute-start(bf16[256,384]{0,1:T(8,128)(2,1)} %get-tuple-element.266), channel_id=1, source_target_pairs={{0,3},{1,2},{2,1},{3,0},{8,11},{9,10},{10,9},{11,8},{4,7},{5,6},{6... | collective-permute-start | bytes 589832 | tf_op jit(solution)/shard_map/ppermute | solution.py:55
  76.7 14.0 %collective-permute-start.9 = (bf16[256,384]{0,1:T(8,128)(2,1)}, bf16[256,384]{0,1:T(8,128)(2,1)S(1)}, u32[]{:S(2)}, u32[]{:S(2)}) collective-permute-start(bf16[256,384]{0,1:T(8,128)(2,1)} %get-tuple-element.266), channel_id=1, source_target_pairs={{0,8},{1,9},{2,10},{3,11},{8,0},{9,1},{10,2},{11,3},{4,12},{5,13},... | collective-permute-start | bytes 589832 | tf_op jit(solution)/shard_map/ppermute | solution.py:55
  77.6 13.1 %collective-permute-start.10 = (bf16[256,384]{0,1:T(8,128)(2,1)}, bf16[256,384]{0,1:T(8,128)(2,1)S(1)}, u32[]{:S(2)}, u32[]{:S(2)}) collective-permute-start(bf16[256,384]{0,1:T(8,128)(2,1)} %get-tuple-element.266), channel_id=1, source_target_pairs={{0,9},{1,8},{2,11},{3,10},{8,1},{9,0},{10,3},{11,2},{4,13},{5,12},... | collective-permute-start | bytes 589832 | tf_op jit(solution)/shard_map/ppermute | solution.py:55
  83.9 10.1 collective-permute-start.11
  90.1 10.0 collective-permute-start.12
  163.5 191.2 %all-gather.14.cloned.1.call-start = ((), (), s32[]{:S(2)}) async-start(), calls=%async_computation.9 | async-start | bytes 5013504 | tf_op jit(solution)/shard_map/all_gather | solution.py:191
  164.9 7.9 collective-permute-start.24
  167.9 7.6 collective-permute-start.25
  193.6 9.3 collective-permute-start.32
  193.7 9.2 collective-permute-start.33
  198.3 90.4 %collective-permute-start.63 = (bf16[48,1536]{1,0:T(8,128)(2,1)}, bf16[48,1536]{1,0:T(8,128)(2,1)}, u32[]{:S(2)}, u32[]{:S(2)}) collective-permute-start(bf16[48,1536]{1,0:T(8,128)(2,1)} %get-tuple-element.255), channel_id=1, source_target_pairs={{0,4},{4,0},{1,5},{5,1},{2,6},{6,2},{3,7},{7,3},{8,12},{12,8},{9,1... | collective-permute-start | bytes 442376 | tf_op jit(solution)/shard_map/ppermute | solution.py:32
  199.2 49.7 %collective-permute-start.71 = (bf16[16,1536]{1,0:T(8,128)(2,1)}, bf16[16,1536]{1,0:T(8,128)(2,1)}, u32[]{:S(2)}, u32[]{:S(2)}) collective-permute-start(bf16[16,1536]{1,0:T(8,128)(2,1)} %select_n.468), channel_id=1, source_target_pairs={{0,16},{16,0},{1,17},{17,1},{2,18},{18,2},{3,19},{19,3},{4,20},{20... | collective-permute-start | bytes 147464 | tf_op jit(solution)/shard_map/ppermute | solution.py:32
  245.0 9.0 collective-permute-start.40
  246.3 11.0 %collective-permute-start.41 = (bf16[256,384]{0,1:T(8,128)(2,1)S(1)}, bf16[256,384]{0,1:T(8,128)(2,1)S(1)}, u32[]{:S(2)}, u32[]{:S(2)}) collective-permute-start(bf16[256,384]{0,1:T(8,128)(2,1)S(1)} %get-tuple-element.260), channel_id=1, source_target_pairs={{0,2},{1,3},{2,0},{3,1},{8,10},{9,11},{10,8},{11,9},{4,6},{5,7},{6... | collective-permute-start | bytes 589832 | tf_op jit(solution)/shard_map/ppermute | solution.py:55
  250.4 76.4 %collective-permute-start.72 = (bf16[32,1536]{1,0:T(8,128)(2,1)}, bf16[32,1536]{1,0:T(8,128)(2,1)}, u32[]{:S(2)}, u32[]{:S(2)}) collective-permute-start(bf16[32,1536]{1,0:T(8,128)(2,1)} %get-tuple-element.342), channel_id=1, source_target_pairs={{0,4},{4,0},{64,68},{68,64},{1,5},{5,1},{65,69},{69,65},{2,6},{6,2... | collective-permute-start | bytes 294920 | tf_op jit(solution)/shard_map/ppermute | solution.py:36
  251.6 76.8 %collective-permute-start.73 = (bf16[32,1536]{1,0:T(8,128)(2,1)}, bf16[32,1536]{1,0:T(8,128)(2,1)}, u32[]{:S(2)}, u32[]{:S(2)}) collective-permute-start(bf16[32,1536]{1,0:T(8,128)(2,1)} %get-tuple-element.342), channel_id=1, source_target_pairs={{0,64},{4,68},{64,0},{68,4},{1,65},{5,69},{65,1},{69,5},{2,66},{6,... | collective-permute-start | bytes 294920 | tf_op jit(solution)/shard_map/ppermute | solution.py:36
  262.1 9.3 collective-permute-start.45
  266.1 9.2 collective-permute-start.46
  284.8 8.3 collective-permute-start.47
  290.4 418.8 %reduce-scatter.18.cloned.1.call-start = ((), (), s32[]{:S(2)}) async-start(), calls=%async_computation.11 | async-start | bytes 2088960 | tf_op jit(solution)/shard_map/reduce_scatter | solution.py:321
  297.2 8.1 collective-permute-start.49
  300.2 7.6 collective-permute-start.50
  313.2 20.9 %collective-permute-start.74 = (bf16[32,1536]{1,0:T(8,128)(2,1)}, bf16[32,1536]{1,0:T(8,128)(2,1)S(1)}, u32[]{:S(2)}, u32[]{:S(2)}) collective-permute-start(bf16[32,1536]{1,0:T(8,128)(2,1)} %get-tuple-element.342), channel_id=1, source_target_pairs={{0,68},{4,64},{64,4},{68,0},{1,69},{5,65},{65,5},{69,1},{2,70},{6,... | collective-permute-start | bytes 294920 | tf_op jit(solution)/shard_map/ppermute | solution.py:36
  330.3 8.3 collective-permute-start.57
  333.9 7.4 collective-permute-start.58
  334.8 11.5 %collective-permute-start.75 = (bf16[128,1536]{1,0:T(8,128)(2,1)S(1)}, bf16[128,1536]{1,0:T(8,128)(2,1)S(1)}, u32[]{:S(2)}, u32[]{:S(2)}) collective-permute-start(bf16[128,1536]{1,0:T(8,128)(2,1)S(1)} %get-tuple-element.320), channel_id=1, source_target_pairs={{0,32},{32,0},{1,33},{33,1},{2,34},{34,2},{3,35},{35,3},{4,36},{36... | collective-permute-start | bytes 1179656 | tf_op jit(solution)/shard_map/ppermute | solution.py:32
  362.8 7.5 collective-permute-start.65
  362.9 8.1 collective-permute-start.66
  366.3 8.4 collective-permute-start.67
  366.9 7.7 collective-permute-start.77
  367.0 7.6 collective-permute-start.78
  394.9 7.6 collective-permute-start.86
  438.0 10.0 collective-permute-start.93
  439.3 16.1 %collective-permute-start.94 = (bf16[256,384]{1,0:T(8,128)(2,1)}, bf16[256,384]{1,0:T(8,128)(2,1)}, u32[]{:S(2)}, u32[]{:S(2)}) collective-permute-start(bf16[256,384]{1,0:T(8,128)(2,1)} %get-tuple-element.179), channel_id=1, source_target_pairs={{0,3},{1,2},{2,1},{3,0},{8,11},{9,10},{10,9},{11,8},{4,7},{5,6},{6... | collective-permute-start | bytes 589832 | tf_op jit(solution)/shard_map/ppermute | solution.py:64
  442.0 13.3 %collective-permute-start.95 = (bf16[256,384]{1,0:T(8,128)(2,1)}, bf16[256,384]{1,0:T(8,128)(2,1)}, u32[]{:S(2)}, u32[]{:S(2)}) collective-permute-start(bf16[256,384]{1,0:T(8,128)(2,1)} %get-tuple-element.178), channel_id=1, source_target_pairs={{0,8},{1,9},{2,10},{3,11},{8,0},{9,1},{10,2},{11,3},{4,12},{5,13},... | collective-permute-start | bytes 589832 | tf_op jit(solution)/shard_map/ppermute | solution.py:64
  442.0 13.3 %collective-permute-start.96 = (bf16[256,384]{1,0:T(8,128)(2,1)}, bf16[256,384]{1,0:T(8,128)(2,1)}, u32[]{:S(2)}, u32[]{:S(2)}) collective-permute-start(bf16[256,384]{1,0:T(8,128)(2,1)} %get-tuple-element.177), channel_id=1, source_target_pairs={{0,9},{1,8},{2,11},{3,10},{8,1},{9,0},{10,3},{11,2},{4,13},{5,12},... | collective-permute-start | bytes 589832 | tf_op jit(solution)/shard_map/ppermute | solution.py:64
  444.1 12.1 %collective-permute-start.97 = (bf16[256,384]{1,0:T(8,128)(2,1)}, bf16[256,384]{1,0:T(8,128)(2,1)}, u32[]{:S(2)}, u32[]{:S(2)}) collective-permute-start(bf16[256,384]{1,0:T(8,128)(2,1)} %get-tuple-element.176), channel_id=1, source_target_pairs={{0,10},{1,11},{2,8},{3,9},{8,2},{9,3},{10,0},{11,1},{4,14},{5,15},... | collective-permute-start | bytes 589832 | tf_op jit(solution)/shard_map/ppermute | solution.py:64
  448.0 12.7 %collective-permute-start.98 = (bf16[256,384]{1,0:T(8,128)(2,1)}, bf16[256,384]{1,0:T(8,128)(2,1)}, u32[]{:S(2)}, u32[]{:S(2)}) collective-permute-start(bf16[256,384]{1,0:T(8,128)(2,1)} %get-tuple-element.181), channel_id=1, source_target_pairs={{0,11},{1,10},{2,9},{3,8},{8,3},{9,2},{10,1},{11,0},{4,15},{5,14},... | collective-permute-start | bytes 589832 | tf_op jit(solution)/shard_map/ppermute | solution.py:64
  468.7 7.6 collective-permute-start.101
  496.1 7.6 collective-permute-start.109
  523.0 7.6 collective-permute-start.117
  566.1 10.6 %collective-permute-start.124 = (bf16[256,384]{1,0:T(8,128)(2,1)S(1)}, bf16[256,384]{1,0:T(8,128)(2,1)S(1)}, u32[]{:S(2)}, u32[]{:S(2)}) collective-permute-start(bf16[256,384]{1,0:T(8,128)(2,1)S(1)} %get-tuple-element.173), channel_id=1, source_target_pairs={{0,2},{1,3},{2,0},{3,1},{8,10},{9,11},{10,8},{11,9},{4,6},{5,7},{6... | collective-permute-start | bytes 589832 | tf_op jit(solution)/shard_map/ppermute | solution.py:64
  569.3 17.1 %collective-permute-start.125 = (bf16[256,384]{1,0:T(8,128)(2,1)}, bf16[256,384]{1,0:T(8,128)(2,1)}, u32[]{:S(2)}, u32[]{:S(2)}) collective-permute-start(bf16[256,384]{1,0:T(8,128)(2,1)} %get-tuple-element.172), channel_id=1, source_target_pairs={{0,3},{1,2},{2,1},{3,0},{8,11},{9,10},{10,9},{11,8},{4,7},{5,6},{6... | collective-permute-start | bytes 589832 | tf_op jit(solution)/shard_map/ppermute | solution.py:64
  571.4 14.9 %collective-permute-start.126 = (bf16[256,384]{1,0:T(8,128)(2,1)}, bf16[256,384]{1,0:T(8,128)(2,1)}, u32[]{:S(2)}, u32[]{:S(2)}) collective-permute-start(bf16[256,384]{1,0:T(8,128)(2,1)} %get-tuple-element.171), channel_id=1, source_target_pairs={{0,8},{1,9},{2,10},{3,11},{8,0},{9,1},{10,2},{11,3},{4,12},{5,13},... | collective-permute-start | bytes 589832 | tf_op jit(solution)/shard_map/ppermute | solution.py:64
  572.6 13.8 %collective-permute-start.127 = (bf16[256,384]{1,0:T(8,128)(2,1)}, bf16[256,384]{1,0:T(8,128)(2,1)}, u32[]{:S(2)}, u32[]{:S(2)}) collective-permute-start(bf16[256,384]{1,0:T(8,128)(2,1)} %get-tuple-element.170), channel_id=1, source_target_pairs={{0,9},{1,8},{2,11},{3,10},{8,1},{9,0},{10,3},{11,2},{4,13},{5,12},... | collective-permute-start | bytes 589832 | tf_op jit(solution)/shard_map/ppermute | solution.py:64
  572.6 14.3 %collective-permute-start.128 = (bf16[256,384]{1,0:T(8,128)(2,1)}, bf16[256,384]{1,0:T(8,128)(2,1)}, u32[]{:S(2)}, u32[]{:S(2)}) collective-permute-start(bf16[256,384]{1,0:T(8,128)(2,1)} %get-tuple-element.169), channel_id=1, source_target_pairs={{0,10},{1,11},{2,8},{3,9},{8,2},{9,3},{10,0},{11,1},{4,14},{5,15},... | collective-permute-start | bytes 589832 | tf_op jit(solution)/shard_map/ppermute | solution.py:64
  577.4 13.5 %collective-permute-start.129 = (bf16[256,384]{1,0:T(8,128)(2,1)}, bf16[256,384]{1,0:T(8,128)(2,1)}, u32[]{:S(2)}, u32[]{:S(2)}) collective-permute-start(bf16[256,384]{1,0:T(8,128)(2,1)} %get-tuple-element.174), channel_id=1, source_target_pairs={{0,11},{1,10},{2,9},{3,8},{8,3},{9,2},{10,1},{11,0},{4,15},{5,14},... | collective-permute-start | bytes 589832 | tf_op jit(solution)/shard_map/ppermute | solution.py:64
  601.0 152.7 %reduce-scatter.24.cloned.1.call-start = ((), (), s32[]{:S(2)}) async-start(), calls=%async_computation.14 | async-start | bytes 5013504 | tf_op jit(solution)/shard_map/reduce_scatter | solution.py:321
  614.3 220.8 %reduce-scatter.20.cloned.1.call-start = ((), (), s32[]{:S(2)}) async-start(), calls=%async_computation.12 | async-start | bytes 5013504 | tf_op jit(solution)/shard_map/reduce_scatter | solution.py:321
  632.6 284.0 %reduce-scatter.22.cloned.1.call-start = ((), (), s32[]{:S(2)}) async-start(), calls=%async_computation.13 | async-start | bytes 5013504 | tf_op jit(solution)/shard_map/reduce_scatter | solution.py:321
  644.7 352.9 %reduce-scatter.16.cloned.1.call-start = ((), (), s32[]{:S(2)}) async-start(), calls=%async_computation.10 | async-start | bytes 4595712 | tf_op jit(solution)/shard_map/reduce_scatter | solution.py:321
  654.2 7.7 collective-permute-start.70
  674.6 8.0 collective-permute-start.132
  677.6 7.5 collective-permute-start.133
  692.3 8.6 collective-permute-start.135
  701.0 8.1 collective-permute-start.136
  (262 other events, 2509.8 us)
Sparse Core Ops, SparseCore 0:
  14.5 47.7 all-gather.5
  65.1 63.2 all-gather.7
  131.1 53.6 all-gather.9
  187.4 53.9 all-gather.11
  290.6 53.4 all-gather.13
  601.1 71.1 reduce-scatter.17
  676.0 77.6 reduce-scatter.23
  757.4 77.6 reduce-scatter.19
  838.8 77.7 reduce-scatter.21
  920.2 77.4 reduce-scatter.15

commit v2 on v1

v2 whole, which is shorter than its diff:
```python
import math

import jax
import jax.numpy as jnp
from jax import lax
from jax.experimental import pallas as pl
from jax.experimental.pallas import tpu as pltpu
from jax.sharding import Mesh, PartitionSpec as P

HEAD = 64
HEADS_HERE = 3
WIDE = HEAD * HEADS_HERE
NEG_FILL = -1e30
NORM_EPS = 1e-05
SCALE = 1.0 / math.sqrt(HEAD)
LOW = jnp.bfloat16
FULL = jnp.float32

FINE = ("xh", "core", "zh", "zl", "xl", "y")
FINE_SIZES = (2, 2, 2, 2, 2, 4)
ROW = ("xh", "core")
COL = ("zh", "zl", "xl", "y")
CHIPS = ("xh", "xl")
SPREAD = ("y", "zh", "zl")
DEEP = ("zh", "zl")
KEYED = ("zl", "y")
SWAP = ((0, 1), (1, 0))


def flipped(size, mask):
    return [(i, i ^ mask) for i in range(size)]


def swapped(x, axis):
    return lax.ppermute(x, axis, SWAP)


def rows_of_all(rows):
    chips = [rows] + [lax.ppermute(rows, CHIPS, flipped(4, d)) for d in (1, 2, 3)]
    half = jnp.concatenate(chips, axis=0)
    return jnp.concatenate([half, swapped(half, "core")], axis=0)


def sum_to_rows(partial):
    count = partial.shape[0] // 8
    blocks = partial.reshape(2, 4, count, partial.shape[1])
    both = blocks[0].astype(FULL) + swapped(blocks[1].astype(LOW), "core").astype(FULL)
    low = both.astype(LOW)
    total = both[0]
    for d in (1, 2, 3):
        total = total + lax.ppermute(low[d], CHIPS, flipped(4, d)).astype(FULL)
    return total


def keys_of_all(block):
    parts = [block]
    for d in range(1, 8):
        parts.append(lax.ppermute(block, KEYED, flipped(8, d)))
    return jnp.concatenate(parts, axis=0)


def sum_to_keys(partial):
    blocks = partial.reshape(8, -1, partial.shape[1])
    low = blocks.astype(LOW)
    total = blocks[0].astype(FULL)
    for d in range(1, 8):
        total = total + lax.ppermute(low[d], KEYED, flipped(8, d)).astype(FULL)
    return total


def sum_to_strips(partial):
    y = lax.axis_index("y")
    z = lax.axis_index("zh") * 2 + lax.axis_index("zl")

    def level(values, axis, here, order):
        low = values.astype(LOW)
        count = values.shape[0] // 4

        def block(x, d):
            return lax.dynamic_slice_in_dim(x, (here ^ d) * count, count, axis=0)

        total = block(values, 0).astype(FULL)
        for d in order:
            total = total + lax.ppermute(block(low, d), axis, flipped(4, d)).astype(FULL)
        return total

    return level(level(partial, "y", y, (1, 3, 2)), DEEP, z, (1, 3, 2)).astype(LOW)


def tied(*arrays):
    return lax.optimization_barrier(arrays)


def mm(a, b, dims):
    return lax.dot_general(a, b, (dims, ((), ())), preferred_element_type=FULL)


def nn(a, b):
    return mm(a, b, ((1,), (0,)))


def nt(a, b):
    return mm(a, b, ((1,), (1,)))


def tn(a, b):
    return mm(a, b, ((0,), (0,)))


def unit(values):
    centre = jnp.mean(values, axis=-1, keepdims=True)
    centred = values - centre
    inverse = lax.rsqrt(jnp.mean(centred * centred, axis=-1, keepdims=True) + NORM_EPS)
    return centred * inverse, inverse


def unit_back(upstream, unit_rows, inverse, gain_row):
    scaled = upstream * gain_row
    inner = (
        scaled
        - jnp.mean(scaled, axis=-1, keepdims=True)
        - unit_rows * jnp.mean(scaled * unit_rows, axis=-1, keepdims=True)
    )
    return inner * inverse


def whole(x):
    return pl.BlockSpec(x.shape, lambda i: (0,) * x.ndim)


def window(columns, index, rows=None):
    return lambda x: pl.BlockSpec((x.shape[0], columns), lambda i: (0, index))


def kernel_call(body, args, outs, steps=1, specs=None, out_specs=None):
    shapes = [jax.ShapeDtypeStruct(shape, kind) for shape, kind in outs]
    placed = [(spec or whole)(x) for x, spec in zip(args, specs or [None] * len(args))]
    return pl.pallas_call(
        body,
        grid=(steps,),
        in_specs=placed,
        out_specs=out_specs or [whole(x) for x in shapes],
        out_shape=shapes,
        compiler_params=pltpu.CompilerParams(vmem_limit_bytes=48 * 2**20),
    )(*args)


def head(x, h, start=0):
    return x[:, start + h * HEAD : start + (h + 1) * HEAD]


def attend_into(q, kv, bias, o_ref, lse_ref):
    rows = []
    for h in range(HEADS_HERE):
        s = nt(head(kv, h), head(q, h)) * SCALE + bias
        top = jnp.max(s, axis=0, keepdims=True)
        lse = top + jnp.log(jnp.sum(jnp.exp(s - top), axis=0, keepdims=True))
        p = jnp.exp(s - lse).astype(LOW)
        lse_ref[h : h + 1, :] = lse
        rows.append(tn(head(kv, h, WIDE), p))
    lse_ref[HEADS_HERE:, :] = jnp.zeros((8 - HEADS_HERE, lse_ref.shape[1]), FULL)
    o = jnp.concatenate(rows, axis=0).T.astype(LOW)
    o_ref[...] = o
    return o


def attend_back(do, q, kv, bias, lse_ref):
    dqs, dks, dvs = [], [], []
    for h in range(HEADS_HERE):
        k, v, q_h, do_h = head(kv, h), head(kv, h, WIDE), head(q, h), head(do, h)
        p = jnp.exp(nt(k, q_h) * SCALE + bias - lse_ref[h : h + 1, :])
        dp = nt(v, do_h)
        inner = jnp.sum(p * dp, axis=0, keepdims=True)
        ds = (p * (dp - inner)).astype(LOW)
        dqs.append(tn(k, ds) * SCALE)
        dks.append(nn(ds, q_h) * SCALE)
        dvs.append(nn(p.astype(LOW), do_h))
    dq = jnp.concatenate(dqs, axis=0).T
    return dq, jnp.concatenate(dks + dvs, axis=1)


def self_forward(q_ref, kv_ref, bias_ref, w_ref, o_ref, lse_ref, out_ref):
    q = q_ref[...][:, :WIDE]
    o = attend_into(q, kv_ref[...], bias_ref[...], o_ref, lse_ref)
    out_ref[...] = nt(o, w_ref[...][:, :WIDE]).astype(LOW)


def cross_forward(c_ref, kv_ref, bias_ref, wq_ref, wo_ref, q_ref, o_ref, lse_ref, out_ref):
    q = nn(c_ref[...], wq_ref[...][:, WIDE : 2 * WIDE]).astype(LOW)
    q_ref[...] = q
    o = attend_into(q, kv_ref[...], bias_ref[...], o_ref, lse_ref)
    out_ref[...] = nt(o, wo_ref[...][:, :WIDE]).astype(LOW)


def self_backward(dy_ref, q_ref, kv_ref, bias_ref, lse_ref, w_ref, dq_ref, dkv_ref):
    do = nn(dy_ref[...], w_ref[...][:, :WIDE]).astype(LOW)
    dq, dkv = attend_back(do, q_ref[...][:, :WIDE], kv_ref[...], bias_ref[...], lse_ref)
    dq_ref[...] = dq.astype(LOW)
    dkv_ref[...] = dkv.astype(LOW)


def cross_backward(
    dy_ref, q_ref, kv_ref, bias_ref, lse_ref, wq_ref, wo_ref, dq_ref, dkv_ref, out_ref
):
    do = nn(dy_ref[...], wo_ref[...][:, :WIDE]).astype(LOW)
    dq, dkv = attend_back(do, q_ref[...], kv_ref[...], bias_ref[...], lse_ref)
    dq = dq.astype(LOW)
    dq_ref[...] = dq
    dkv_ref[...] = dkv.astype(LOW)
    out_ref[...] = nt(dq, wq_ref[...][:, WIDE : 2 * WIDE]).astype(LOW)


def ff_forward(e_ref, up_ref, down_ref, u_ref, hmid_ref, out_ref):
    u = nn(e_ref[...], up_ref[...])
    hmid = gelu(u).astype(LOW)
    u_ref[...] = u
    hmid_ref[...] = hmid
    out_ref[...] = nt(hmid, down_ref[...]).astype(LOW)


def ff_backward(dy_ref, u_ref, up_ref, down_ref, du_ref, out_ref):
    du = (nn(dy_ref[...], down_ref[...]) * gelu_slope(u_ref[...])).astype(LOW)
    du_ref[...] = du
    out_ref[...] = nt(du, up_ref[...]).astype(LOW)


def weight_sums(groups, width):
    steps, args, specs, plan, columns = 4, [], [], [], 0
    rows = width // steps

    def put(x, spec):
        args.append(x)
        specs.append(spec)
        return len(args) - 1

    for group in groups:
        terms = []
        size = 0
        for kind, a, b in group:
            if kind == "tn":
                at = put(a, lambda x: pl.BlockSpec((x.shape[0], rows), lambda i: (0, i)))
                size += b.shape[1]
            else:
                cut, index = a[1]
                at = put(a[0], lambda x, c=cut, k=index: pl.BlockSpec((rows, c), lambda i: (i, k)))
                size = b.shape[0] if kind == "nt" else b.shape[1]
            terms.append((kind, at, put(b, None)))
        plan.append((columns, size, terms))
        columns += size

    def body(*refs):
        out_ref = refs[-1]
        for start, size, terms in plan:
            if terms[0][0] == "tn":
                parts = [tn(refs[a][...], refs[b][...]) for _, a, b in terms]
                value = parts[0] if len(parts) == 1 else jnp.concatenate(parts, axis=1)
            else:
                product = nt if terms[0][0] == "nt" else nn
                value = sum(product(refs[a][...], refs[b][...]) for _, a, b in terms)
            out_ref[:, start : start + size] = value.astype(LOW)

    return kernel_call(
        body,
        args,
        [((width, columns), LOW)],
        steps,
        specs,
        [pl.BlockSpec((rows, columns), lambda i: (i, 0))],
    )[0]


def laid_out(parts, here, strip, ff):
    early, first, last = parts
    args = [here.reshape(1), *early, *first, *last]

    def body(*refs):
        lower = refs[0][0] == 0
        kept = []
        for mine, theirs in ((1, 2), (3, 4), (5, 6)):
            a, b = refs[mine][...].astype(FULL), refs[theirs][...].astype(FULL)
            kept.append((jnp.where(lower, a, b), jnp.where(lower, b, a)))
        early, first, last = kept
        g_in, g_out, g_query, g_text, g_tout, g_up, g_down = refs[7:]

        def wide(pair, start, size):
            return jnp.concatenate([x[:, start : start + size] for x in pair], axis=1)

        for k in range(3):
            g_in[0, k] = wide(last, k * WIDE, WIDE)
            g_in[1, k] = wide(first, 2688 + k * WIDE, WIDE)
        g_out[0] = wide(last, 576, WIDE)
        g_out[1] = wide(first, 3264, WIDE)
        for l, pair in enumerate((first, early)):
            g_up[l] = wide(pair, 0, ff)
            g_down[l] = wide(pair, ff, ff)
            for k in range(2):
                g_text[l, k] = wide(pair, 1536 + k * WIDE, WIDE)
            g_query[l] = wide(pair, 1920, WIDE)
            g_tout[l] = wide(pair, 2112, WIDE)

    outs = [
        ((2, 3, strip, 2 * WIDE), FULL),
        ((2, strip, 2 * WIDE), FULL),
        ((2, strip, 2 * WIDE), FULL),
        ((2, 2, strip, 2 * WIDE), FULL),
        ((2, strip, 2 * WIDE), FULL),
        ((2, strip, 2 * ff), FULL),
        ((2, strip, 2 * ff), FULL),
    ]
    specs = [lambda x: pl.BlockSpec(memory_space=pltpu.SMEM)] + [None] * 6
    return kernel_call(body, args, outs, 1, specs)


def gelu(z):
    return 0.5 * z * (1.0 + lax.erf(z * math.sqrt(0.5)))


def gelu_slope(z):
    half = 0.5 * (1.0 + lax.erf(z * math.sqrt(0.5)))
    return half + z * jnp.exp(-0.5 * z * z) * (1.0 / math.sqrt(2.0 * math.pi))


def width_mixed(x):
    lead = x.shape[:-1]
    parts = x.reshape(*lead, 8, 4, -1)
    return jnp.swapaxes(parts, -2, -3).reshape(*lead, -1)


def width_restored(x):
    lead = x.shape[:-1]
    parts = x.reshape(*lead, 4, 8, -1)
    return jnp.swapaxes(parts, -2, -3).reshape(*lead, -1)


def local(
    tokens,
    memory,
    clip_lengths,
    out_grad,
    norm_gain,
    norm_bias,
    self_in,
    self_out,
    text_query,
    text_kv,
    text_out,
    mlp_up,
    mlp_down,
):
    xh, core, zh = lax.axis_index("xh"), lax.axis_index("core"), lax.axis_index("zh")
    zl, xl, y = lax.axis_index("zl"), lax.axis_index("xl"), lax.axis_index("y")
    row = xh * 2 + core
    width = tokens.shape[2]
    strip = memory.shape[2]
    ff = mlp_up.shape[2] // 2

    def halves(x, axis):
        size = x.shape[axis] // 2
        a = lax.slice_in_dim(x, 0, size, axis=axis)
        b = lax.slice_in_dim(x, size, 2 * size, axis=axis)
        return a, b

    def joined(*pairs):
        return tuple(jnp.concatenate(side, axis=1) for side in zip(*pairs))

    def common(x):
        return x, x

    def strips_of_pair(pair):
        first, second = pair
        mine = jnp.where(xl == 0, first, second)
        theirs = swapped(jnp.where(xl == 0, second, first), "xl")
        return jnp.where(
            xl == 0, jnp.concatenate([mine, theirs]), jnp.concatenate([theirs, mine])
        )

    def spread(pair):
        return lax.all_gather(strips_of_pair(pair), SPREAD, axis=0, tiled=True)

    def spread_now(own):
        sent = jnp.broadcast_to(own[None], (16, *own.shape))
        return lax.all_to_all(sent, SPREAD, 0, 0, tiled=True).reshape(-1, own.shape[1])

    norms = jnp.concatenate([norm_gain.reshape(6, strip), norm_bias.reshape(6, strip)])
    norms = jnp.pad(norms.T, ((0, 0), (0, 52)))
    memory_t = memory.reshape(-1, strip).T

    def own_in(l):
        return joined(*[halves(self_in[l, k], 1) for k in range(3)])

    def own_out(w, l):
        return halves(w[l].T, 1)

    def own_text(l):
        return joined(*[halves(text_kv[l, k], 1) for k in range(2)])

    def own_ff(l):
        return joined(halves(mlp_up[l], 1), own_out(mlp_down, l))

    own_0 = strips_of_pair(joined(own_in(0), common(norms)))
    own_0, self_out, text_query, text_kv, text_out, memory_t = tied(
        own_0, self_out, text_query, text_kv, text_out, memory_t
    )
    piece_0 = spread_now(own_0)
    piece_1 = spread(
        joined(
            own_text(0),
            common(memory_t),
            own_out(self_out, 0),
            halves(text_query[0], 1),
            own_out(text_out, 0),
            common(jnp.zeros((strip, 192), LOW)),
        )
    )
    piece_2 = spread(
        joined(
            own_ff(0),
            own_text(1),
            own_out(self_out, 1),
            halves(text_query[1], 1),
            own_out(text_out, 1),
            own_in(1),
        )
    )
    piece_3 = spread(own_ff(1))

    w_in = [piece_0[:, :576], piece_2[:, 2496:3072]]
    norm_rows = piece_0[:, 576:588].astype(FULL).T
    gains = [norm_rows[0:3], norm_rows[3:6]]
    shifts = [norm_rows[6:9], norm_rows[9:12]]
    attn = [piece_1, piece_2]
    feed = [piece_2, piece_3]
    w_text = [piece_1[:, :384], piece_2[:, 1536:1920]]
    memory_all = piece_1[:, 384:768]
    up_window, down_window = window(ff, 0), window(ff, 1)
    mixed_window = [window(384, 2), window(384, 5)]
    tout_window = [window(384, 3), window(768, 3)]

    def own_rows(x):
        here = width_mixed(lax.dynamic_slice_in_dim(x, row * 16, 16, axis=1))
        keep = jnp.where(zh == 0, here[0], here[1])
        send = jnp.where(zh == 0, here[1], here[0])
        return jnp.concatenate([keep, swapped(send, "zh")], axis=0)

    token_rows = own_rows(tokens)
    grad_rows = own_rows(out_grad)

    at = jnp.arange(2048, dtype=jnp.int32)
    d_z, d_y, d_c = at // 1024, (at // 256) % 4, (at // 128) % 2
    d_x, d_s, inner = (at // 32) % 4, (at // 16) % 2, at % 16
    block = (zh ^ d_s) * 16 + (zl ^ d_z) * 8 + (xl ^ (d_x & 1)) * 4 + (y ^ d_y)
    key_at = block * 64 + ((xh ^ (d_x >> 1)) * 2 + (core ^ d_c)) * 16 + inner
    lengths = jnp.where(zh == 0, clip_lengths[0], clip_lengths[1])
    end_0 = lengths[0]
    end_1 = lengths[0] + lengths[1]
    key_clip = (key_at >= end_0).astype(jnp.int32) + (key_at >= end_1).astype(jnp.int32)
    frame_at, frame_clip = key_at[:256], key_clip[:256]
    allowed = (frame_clip[None, :] == key_clip[:, None]) & (key_at[:, None] <= frame_at[None, :])
    bias = jnp.where(allowed, 0.0, NEG_FILL).astype(FULL)
    text_clip = jnp.arange(192, dtype=jnp.int32) // 64
    text_bias = jnp.where(frame_clip[None, :] == text_clip[:, None], 0.0, NEG_FILL).astype(FULL)
    frames = bias.shape[1]
    low_frames = ((frames, WIDE), LOW)
    lse_rows = ((8, frames), FULL)
    partial_rows = ((frames, width), LOW)

    token_all = rows_of_all(token_rows)
    unit_all, _ = unit(token_all.astype(FULL))
    residual = token_rows.astype(FULL)
    kept = []
    for l in range(2):
        n_0, r_0 = unit(residual)
        if l == 0:
            a = (unit_all * gains[0][0] + shifts[0][0]).astype(LOW)
        else:
            a = rows_of_all((n_0 * gains[l][0] + shifts[l][0]).astype(LOW))
        qkv = nn(a, w_in[l]).astype(LOW)
        kv = keys_of_all(qkv[:, WIDE:])
        o, lse, part = kernel_call(
            self_forward,
            [qkv, kv, bias, attn[l]],
            [low_frames, lse_rows, partial_rows],
            specs=[None, None, None, mixed_window[l]],
        )
        x1 = residual + sum_to_rows(part)
        n_1, r_1 = unit(x1)
        c = rows_of_all((n_1 * gains[l][1] + shifts[l][1]).astype(LOW))
        mkv = tn(memory_all, w_text[l]).astype(LOW)
        mkv = jnp.where(zh == 0, mkv[:192], mkv[192:])
        cq, co, clse, part = kernel_call(
            cross_forward,
            [c, mkv, text_bias, attn[l], attn[l]],
            [low_frames, low_frames, lse_rows, partial_rows],
            specs=[None, None, None, mixed_window[l], tout_window[l]],
        )
        x2 = x1 + sum_to_rows(part)
        n_2, r_2 = unit(x2)
        e = rows_of_all((n_2 * gains[l][2] + shifts[l][2]).astype(LOW))
        u, hmid, part = kernel_call(
            ff_forward,
            [e, feed[l], feed[l]],
            [((frames, ff), FULL), ((frames, ff), LOW), partial_rows],
            specs=[None, up_window, down_window],
        )
        residual = x2 + sum_to_rows(part)
        kept.append((n_0, r_0, a, qkv, kv, o, lse, n_1, r_1, c, cq, mkv, co, clse, n_2, r_2, e, u, hmid))

    def frames_back(rows):
        pair = rows.reshape(2, 16, width)
        other = swapped(pair[1], "zh")
        mbs = jnp.where(zh == 0, jnp.stack([pair[0], other]), jnp.stack([other, pair[0]]))
        mbs = width_restored(mbs)
        both = jnp.stack([mbs, swapped(mbs, "core")])
        both = jnp.where(core == 0, both, both[::-1])
        four = jnp.stack([both, swapped(both, "xh")])
        four = jnp.where(xh == 0, four, four[::-1])
        return jnp.moveaxis(four.reshape(4, 2, 16, width), 0, 1).reshape(2, 64, width)

    output = frames_back(residual.astype(LOW))

    grad = grad_rows.astype(FULL)
    norm_sums = [[None] * 3, [None] * 3]
    memory_partial = jnp.zeros((width, 384), FULL)

    def norm_step(l, k, grad, upstream, n, r):
        norm_sums[l][k] = (jnp.sum(upstream * n, axis=0), jnp.sum(upstream, axis=0))
        return grad + unit_back(upstream, n, r, gains[l][k])

    def summed(both):
        return lax.psum_scatter(both, SPREAD, scatter_dimension=0, tiled=True)

    memory_terms = []
    for l in (1, 0):
        n_0, r_0, a, qkv, kv, o, lse, n_1, r_1, c, cq, mkv, co, clse, n_2, r_2, e, u, hmid = kept[l]
        dy = rows_of_all(grad.astype(LOW))
        du, part = kernel_call(
            ff_backward,
            [dy, u, feed[l], feed[l]],
            [((frames, ff), LOW), partial_rows],
            specs=[None, None, up_window, down_window],
        )
        de = sum_to_rows(part)
        groups = [[("tn", e, du)], [("tn", dy, hmid)]]
        grad = norm_step(l, 2, grad, de, n_2, r_2)

        dy = rows_of_all(grad.astype(LOW))
        dcq, dmkv, part = kernel_call(
            cross_backward,
            [dy, cq, mkv, text_bias, clse, attn[l], attn[l]],
            [low_frames, ((192, 2 * WIDE), LOW), partial_rows],
            specs=[None] * 5 + [mixed_window[l], tout_window[l]],
        )
        dc = sum_to_rows(part)
        none = jnp.zeros_like(dmkv)
        dmkv = jnp.where(
            zh == 0, jnp.concatenate([dmkv, none]), jnp.concatenate([none, dmkv])
        )
        memory_terms.append(("nt", (attn[l], (384, 4 * l)), dmkv))
        groups += [[("nn", (piece_1, (384, 1)), dmkv)], [("tn", c, dcq), ("tn", dy, co)]]
        if l == 0:
            groups += [memory_terms] + late
        first = weight_sums(groups, width)
        dc, first = tied(dc, first)
        first = summed(first)
        if l == 0:
            dc, early = tied(dc, early)
        grad = norm_step(l, 1, grad, dc, n_1, r_1)

        dy = rows_of_all(grad.astype(LOW))
        dq, dkv = kernel_call(
            self_backward,
            [dy, qkv, kv, bias, lse, attn[l]],
            [low_frames, ((kv.shape[0], 2 * WIDE), LOW)],
            specs=[None] * 5 + [mixed_window[l]],
        )
        dkv = sum_to_keys(dkv)
        dqkv = jnp.concatenate([dq, dkv.astype(LOW)], axis=1)
        da = nt(dqkv, w_in[l])
        late = [[("tn", a, dqkv), ("tn", dy, o)]]
        if l == 1:
            grad = norm_step(l, 0, grad, sum_to_rows(da), n_0, r_0)
            early = first
        else:
            norm_sums[0][0] = (jnp.sum(da * unit_all, axis=0), jnp.sum(da, axis=0))
            last = sum_to_strips(weight_sums(late, width))
            sums = jnp.stack(
                [norm_sums[i][j][0] for i in range(2) for j in range(3)]
                + [norm_sums[i][j][1] for i in range(2) for j in range(3)]
            )
            sums = jnp.pad(sums, ((0, 4), (0, 0)))
            extra = jnp.broadcast_to(sums[None], (8, *sums.shape))
            da = jnp.concatenate([da.reshape(8, -1, width), extra], axis=1)
            da = sum_to_rows(da.reshape(-1, width))
            norm_total = da[-16:].astype(LOW).reshape(16, 16, -1)
            norm_total = lax.all_to_all(jnp.swapaxes(norm_total, 0, 1), SPREAD, 0, 0, tiled=True)
            norm_total = jnp.sum(norm_total.astype(FULL), axis=0)
            grad = grad + unit_back(da[:-16], n_0, r_0, gains[0][0])
    input_grad = frames_back(grad.astype(LOW)).astype(FULL)

    def strips(block):
        mine = lax.dynamic_slice_in_dim(block, xl * strip, strip, axis=0)
        theirs = lax.dynamic_slice_in_dim(block, (1 - xl) * strip, strip, axis=0)
        return mine, swapped(theirs, "xl")

    def both(pair, start, size):
        return sum(x[:, start : start + size].astype(FULL) for x in pair)

    def everywhere(x):
        x = x + swapped(x.astype(LOW), "core").astype(FULL)
        return x + swapped(x.astype(LOW), "xh").astype(FULL)

    early, first, last = [strips(b) for b in (early, first, last)]
    laid = laid_out((early, first, last), xl, strip, ff)
    self_in_grad, self_out_grad, text_query_grad, text_kv_grad = laid[:4]
    text_out_grad, mlp_up_grad, mlp_down_grad = laid[4:]
    self_out_grad, text_out_grad, mlp_down_grad = [
        jnp.swapaxes(x, 1, 2) for x in (self_out_grad, text_out_grad, mlp_down_grad)
    ]
    memory_grad = everywhere(both(first, 2304, 384)).reshape(strip, 2, 192)
    memory_grad = jnp.transpose(memory_grad, (1, 2, 0))
    norm_grads = lax.dynamic_slice_in_dim(norm_total, xl * strip, strip, axis=1)
    gain_grad = norm_grads[:6].reshape(2, 3, strip)
    shift_grad = norm_grads[6:12].reshape(2, 3, strip)
    return (
        output,
        input_grad,
        memory_grad,
        gain_grad,
        shift_grad[:, 0:2],
        shift_grad[:, 2],
        self_in_grad,
        self_out_grad,
        text_query_grad,
        text_kv_grad,
        text_out_grad,
        mlp_up_grad,
        mlp_down_grad,
    )


def solution(mesh):
    fine = Mesh(mesh.devices.reshape(FINE_SIZES), FINE)
    frames = P(None, COL, None)
    strips = P(None, None, COL)
    return jax.shard_map(
        local,
        mesh=fine,
        in_specs=(
            frames,
            strips,
            P(),
            frames,
            strips,
            strips,
            P(None, None, COL, ROW),
            P(None, ROW, COL),
            P(None, COL, ROW),
            P(None, None, COL, ROW),
            P(None, ROW, COL),
            P(None, COL, ROW),
            P(None, ROW, COL),
        ),
        out_specs=(
            frames,
            frames,
            strips,
            strips,
            strips,
            P(None, COL),
            P(None, None, COL, ROW),
            P(None, ROW, COL),
            P(None, COL, ROW),
            P(None, None, COL, ROW),
            P(None, ROW, COL),
            P(None, COL, ROW),
            P(None, ROW, COL),
        ),
        check_vma=False,
    )
```

time: 1030 us -> 665 us (0.65)
  waiting for transfers between devices: 538 us -> 222 us
  matrix products: 96.1 us -> 10.3 us
  Pallas kernels: 0 us -> 82.5 us
  local copies, waits for them, and re-layouts: 112 us -> 47.1 us
  starting transfers between devices: 187 us -> 246 us
  other arithmetic: 70.1 us -> 28.5 us
    reduce_scatter x5 -> x2, waiting for transfers between devices: 256 us -> 0.02 us  [summed(): return lax.psum_scatter(both, SPREAD, scatter_dimension=0, tiled=True)]
    pallas_call x0 -> x16, Pallas kernels: none -> 82.5 us  [kernel_call(): pl.pallas_call(body, grid=(steps,), in_specs=placed, out_specs=out_specs...]
    dot_general x42 -> x6, matrix products: 68.9 us -> 10.3 us  [mm(): return lax.dot_general(a, b, (dims, ((), ())), preferred_element_type=FULL)]
    all_gather x5 -> x3, waiting for transfers between devices: 52.7 us -> 0.04 us  [spread(): return lax.all_gather(strips_of_pair(pair), SPREAD, axis=0, tiled=True)]
    unnamed x401 -> x273, local copies, waits for them, and re-layouts: 59.4 us -> 18.4 us
    ppermute x46 -> x41, starting transfers between devices: 61.2 us -> 101 us  [swapped(): return lax.ppermute(x, axis, SWAP)]
    ppermute x36, waiting for transfers between devices: 64.9 us -> 28.8 us  [sum_to_rows(): total = total + lax.ppermute(low[d], CHIPS, flipped(4, d)).astype(FULL)]
    ppermute x0 -> x6, waiting for transfers between devices: none -> 29.1 us  [level(): lax.ppermute(block(low, d), axis, flipped(4, d)).astype(FULL)]
  transfers between devices with their start and end apart: 156 -> 154, of which waited for: 105 -> 102; matrix products, arithmetic and copies ran while one was open for 19% -> 10% of each run, Pallas kernels for 0% -> 11%
where the time goes in v2:
time: 665 us; the launch traced here: 655 us
  starting transfers between devices  246 us (37%)
  waiting for transfers between devices  222 us (33%)
  Pallas kernels  82.5 us (12%)
  local copies, waits for them, and re-layouts  47.1 us (7%)
  other arithmetic  28.5 us (4%)
  between operations  18.4 us (3%)
  matrix products  10.3 us (2%)
    ppermute x41, starting transfers between devices, swapped(): return lax.ppermute(x, axis, SWAP)  101 us
    pallas_call x16, Pallas kernels, kernel_call(): pl.pallas_call(body, grid=(steps,), in_specs=placed, out_specs=out_specs...  82.5 us
    ppermute x41, waiting for transfers between devices, swapped(): return lax.ppermute(x, axis, SWAP)  44.8 us
    ppermute x36, starting transfers between devices, sum_to_rows(): total = total + lax.ppermute(low[d], CHIPS, flipped(4, d)).astype(FULL)  42.9 us
    ppermute x14, waiting for transfers between devices, sum_to_keys(): total = total + lax.ppermute(low[d], KEYED, flipped(8, d)).astype(FULL)  42.3 us
    ppermute x36, starting transfers between devices, rows_of_all(): lax.ppermute(rows, CHIPS, flipped(4, d))  38.4 us
    ppermute x36, waiting for transfers between devices, rows_of_all(): lax.ppermute(rows, CHIPS, flipped(4, d))  30.6 us
    ppermute x6, waiting for transfers between devices, level(): lax.ppermute(block(low, d), axis, flipped(4, d)).astype(FULL)  29.1 us
  transfers between devices with their start and end apart: 154, of which 102 were waited for; matrix products, arithmetic and copies ran while one was open for 10% of the time, Pallas kernels for 11%

profile of v2, /device:TPU:1, one launch (start us, length us, event | category | flops | bytes accessed | tf_op | source)
XLA Modules:
  0.0 654.9 jit_solution(14696426405399401246)
XLA Ops:
  16.2 2.5 collective-permute-done.13
  23.3 4.1 collective-permute-done.30
  31.0 3.9 collective-permute-start
  42.2 8.3 %all-to-all-start = ((bf16[16,96,640]{2,1,0:T(8,128)(2,1)}), bf16[16,96,640]{2,1,0:T(8,128)(2,1)S(1)}, u32[]{:S(2)}, u32[]{:S(2)}) async-start(bf16[16,96,640]{2,1,0:T(8,128)(2,1)} %broadcast_in_dim.22), calls=%async_computation | async-start | bytes 3932160 | tf_op jit(solution)/shard_map/all_to_all | solution.py:382
  52.6 5.9 collective-permute-start.4
  61.7 15.7 %all-to-all-done = bf16[16,96,640]{2,1,0:T(8,128)(2,1)S(1)} async-done(((bf16[16,96,640]{2,1,0:T(8,128)(2,1)}), bf16[16,96,640]{2,1,0:T(8,128)(2,1)S(1)}, u32[]{:S(2)}, u32[]{:S(2)}) %all-to-all-start) | async-done | bytes 1966112 | tf_op jit(solution)/shard_map/all_to_all | solution.py:382
  77.6 5.2 slice_reduce_fusion.1
  84.2 5.5 collective-permute-start.6
  90.3 3.1 collective-permute-start.7
  100.2 4.7 collective-permute-done.8
  104.9 3.6 collective-permute-done.9
  111.3 6.8 %shard_map.228 = (bf16[256,192]{1,0:T(8,128)(2,1)S(1)}, f32[8,256]{1,0:T(8,128)S(1)}, bf16[256,1536]{1,0:T(8,128)(2,1)S(1)}) custom-call(bf16[256,576]{1,0:T(8,128)(2,1)S(1)} %fusion.16.q_ref, bf16[2048,384]{1,0:T(8,128)(2,1)S(1)} %copy-done.6, f32[2048,256]{1,0:T(8,128)S(1)} %and_select_fusion.bias_ref, ...), custom_call_target="tpu_custom_call" | custom-call | tf_op jit(solution)/shard_map/pallas_call | solution.py:138
  118.1 22.6 %collective-permute-start.14 = (bf16[4,32,1536]{2,1,0:T(8,128)(2,1)S(1)}, bf16[4,32,1536]{2,1,0:T(8,128)(2,1)S(1)}, u32[]{:S(2)}, u32[]{:S(2)}) collective-permute-start(bf16[4,32,1536]{2,1,0:T(8,128)(2,1)S(1)} %bitcast.356), channel_id=1, source_target_pairs={{0,32},{32,0},{1,33},{33,1},{2,34},{34,2},{3,35},{35,3},{4,36},{36... | collective-permute-start | bytes 1179656 | tf_op jit(solution)/shard_map/ppermute | solution.py:35
  158.4 3.7 collective-permute-start.21
  163.5 4.1 shard_map.229
  184.1 3.4 collective-permute-start.29
  188.8 4.1 shard_map.230
  214.6 4.9 collective-permute-start.38
  223.9 2.8 fusion.19.q_ref
  230.6 6.7 %collective-permute-done.39 = bf16[256,384]{1,0:T(8,128)(2,1)S(1)} collective-permute-done((bf16[256,384]{1,0:T(8,128)(2,1)S(1)}, bf16[256,384]{1,0:T(8,128)(2,1)S(1)}, u32[]{:S(2)}, u32[]{:S(2)}) %collective-permute-start.39) | collective-permute-done | bytes 196640 | tf_op jit(solution)/shard_map/ppermute | solution.py:58
  239.7 4.5 collective-permute-done.41
  244.9 3.8 collective-permute-start.44
  249.8 5.9 collective-permute-done.44
  255.8 7.2 %shard_map.231 = (bf16[256,192]{1,0:T(8,128)(2,1)S(1)}, f32[8,256]{1,0:T(8,128)S(1)}, bf16[256,1536]{1,0:T(8,128)(2,1)S(1)}) custom-call(bf16[256,576]{1,0:T(8,128)(2,1)S(1)} %fusion.19.q_ref, bf16[2048,384]{1,0:T(8,128)(2,1)S(1)} %constant_dynamic-update-slice_fusion.36.kv_ref, f32[2048,256]{1,0:T(8,128)S(1)} %and_select_fusion.bias_ref, ...), custom_call_target="tpu_custom_call" | custom-call | tf_op jit(solution)/shard_map/pallas_call | solution.py:138
  263.1 3.0 collective-permute-start.46
  274.9 2.4 convolution_convert_fusion
  287.8 3.8 collective-permute-start.53
  293.1 4.1 shard_map.232
  313.9 2.8 collective-permute-start.61
  318.1 4.1 shard_map.233
  322.8 4.1 shard_map.234
  348.5 3.5 collective-permute-start.82
  353.4 4.1 shard_map.235
  364.7 6.5 shard_map.236
  381.2 2.5 collective-permute-start.90
  385.1 8.3 %shard_map.237 = (bf16[256,192]{1,0:T(8,128)(2,1)S(1)}, bf16[2048,384]{1,0:T(8,128)(2,1)S(1)}) custom-call(bf16[256,1536]{1,0:T(8,128)(2,1)S(1)} %constant_dynamic-update-slice_fusion.72.dy_ref.refs_16_, bf16[256,576]{1,0:T(8,128)(2,1)S(1)} %copy-done.19, bf16[2048,384]{1,0:T(8,128)(2,1)S(1)} %copy-done.4, f32[2048,256]{1,0:T(8,128)} %copy-done.2, ...), custom_call_target="tpu_custom_call" | custom-call | tf_op jit(solution)/shard_map/pallas_call | solution.py:138
  400.2 3.3 collective-permute-done.91
  403.5 3.2 collective-permute-start.93
  408.5 4.2 collective-permute-done.96
  412.7 3.5 collective-permute-done.95
  416.2 5.4 collective-permute-done.94
  423.5 2.6 fusion.4
  443.1 3.3 collective-permute-start.105
  447.8 4.1 shard_map.238
  468.3 3.4 collective-permute-start.113
  473.1 3.7 shard_map.239
  482.2 9.5 %shard_map.240 = bf16[1536,3456]{1,0:T(8,128)(2,1)} custom-call(bf16[256,1536]{1,0:T(8,128)(2,1)S(1)} %constant_dynamic-update-slice_fusion.26.e_ref.refs_0_, bf16[256,768]{1,0:T(8,128)(2,1)S(1)} %get-tuple-element.97.refs_1_, bf16[256,1536]{1,0:T(8,128)(2,1)S(1)} %constant_dynamic-update-slice_fusion.77.dy_ref.refs_2_, bf16[256,768]{1,0:T(8,128)(2,1)S(1)} %copy-done.26, ...), custom_call_target="tpu_custom_call" | custom-call | tf_op jit(solution)/shard_map/pallas_call | solution.py:138
  494.6 2.8 collective-permute-done.67
  510.7 2.5 collective-permute-start.121
  514.6 8.2 %shard_map.241 = (bf16[256,192]{1,0:T(8,128)(2,1)S(1)}, bf16[2048,384]{1,0:T(8,128)(2,1)S(1)}) custom-call(bf16[256,1536]{1,0:T(8,128)(2,1)S(1)} %constant_dynamic-update-slice_fusion.87.dy_ref.refs_2_, bf16[256,576]{1,0:T(8,128)(2,1)S(1)} %copy-done.17, bf16[2048,384]{1,0:T(8,128)(2,1)S(1)} %copy-done.7, f32[2048,256]{1,0:T(8,128)} %copy-done.2, ...), custom_call_target="tpu_custom_call" | custom-call | tf_op jit(solution)/shard_map/pallas_call | solution.py:138
  524.5 2.8 collective-permute-start.127
  528.5 5.0 collective-permute-done.122
  538.4 4.4 collective-permute-done.127
  542.8 3.8 collective-permute-done.126
  546.6 3.2 collective-permute-done.125
  549.8 5.1 collective-permute-done.123
  566.9 11.0 %collective-permute-done.140 = bf16[384,768]{1,0:T(8,128)(2,1)S(1)} collective-permute-done((bf16[384,768]{1,0:T(8,128)(2,1)S(1)}, bf16[384,768]{1,0:T(8,128)(2,1)S(1)}, u32[]{:S(2)}, u32[]{:S(2)}) %collective-permute-start.140) | collective-permute-done | bytes 589856 | tf_op jit(solution)/shard_map/ppermute | solution.py:84
  580.1 18.1 %collective-permute-done.142 = bf16[384,768]{1,0:T(8,128)(2,1)S(1)} collective-permute-done((bf16[384,768]{1,0:T(8,128)(2,1)S(1)}, bf16[384,768]{1,0:T(8,128)(2,1)S(1)}, u32[]{:S(2)}, u32[]{:S(2)}) %collective-permute-start.142) | collective-permute-done | bytes 589856 | tf_op jit(solution)/shard_map/ppermute | solution.py:84
  605.0 4.9 all-to-all-start.1
  609.9 2.9 collective-permute-start.133
  613.8 2.6 all-to-all-done.1
  617.3 4.9 collective-permute-start.134
  627.6 4.9 collective-permute-done.135
  632.6 6.0 collective-permute-done.136.refs_4_
  (807 shorter events, 305.0 us)
Async XLA Ops:
  7.2 102.6 %all-gather.4.cloned.1.call-start = ((), (), s32[]{:S(2)}) async-start(), calls=%async_computation.4 | async-start | bytes 5013504 | tf_op jit(solution)/shard_map/all_gather | solution.py:378
  19.5 169.3 %all-gather.6.cloned.1.call-start = ((), (), s32[]{:S(2)}) async-start(), calls=%async_computation.5 | async-start | bytes 10027008 | tf_op jit(solution)/shard_map/all_gather | solution.py:378
  37.4 13.2 %collective-permute-start.1 = (bf16[32,1536]{1,0:T(8,128)(2,1)S(1)}, bf16[32,1536]{1,0:T(8,128)(2,1)S(1)}, u32[]{:S(2)}, u32[]{:S(2)}) collective-permute-start(bf16[32,1536]{1,0:T(8,128)(2,1)S(1)} %get-tuple-element.410), channel_id=1, source_target_pairs={{0,4},{4,0},{64,68},{68,64},{1,5},{5,1},{65,69},{69,65},{2,6},{6,2... | collective-permute-start | bytes 294920 | tf_op jit(solution)/shard_map/ppermute | solution.py:39
  38.2 13.7 %collective-permute-start.3 = (bf16[32,1536]{1,0:T(8,128)(2,1)S(1)}, bf16[32,1536]{1,0:T(8,128)(2,1)S(1)}, u32[]{:S(2)}, u32[]{:S(2)}) collective-permute-start(bf16[32,1536]{1,0:T(8,128)(2,1)S(1)} %get-tuple-element.410), channel_id=1, source_target_pairs={{0,68},{4,64},{64,4},{68,0},{1,69},{5,65},{65,5},{69,1},{2,70},{6,... | collective-permute-start | bytes 294920 | tf_op jit(solution)/shard_map/ppermute | solution.py:39
  40.1 11.2 %collective-permute-start.2 = (bf16[32,1536]{1,0:T(8,128)(2,1)S(1)}, bf16[32,1536]{1,0:T(8,128)(2,1)S(1)}, u32[]{:S(2)}, u32[]{:S(2)}) collective-permute-start(bf16[32,1536]{1,0:T(8,128)(2,1)S(1)} %get-tuple-element.410), channel_id=1, source_target_pairs={{0,64},{4,68},{64,0},{68,4},{1,65},{5,69},{65,1},{69,5},{2,66},{6,... | collective-permute-start | bytes 294920 | tf_op jit(solution)/shard_map/ppermute | solution.py:39
  42.2 35.2 %all-to-all-start = ((bf16[16,96,640]{2,1,0:T(8,128)(2,1)}), bf16[16,96,640]{2,1,0:T(8,128)(2,1)S(1)}, u32[]{:S(2)}, u32[]{:S(2)}) async-start(bf16[16,96,640]{2,1,0:T(8,128)(2,1)} %broadcast_in_dim.22), calls=%async_computation | async-start | bytes 3932160 | tf_op jit(solution)/shard_map/all_to_all | solution.py:382
  50.5 267.6 %all-gather.8.cloned.1.call-start = ((), (), s32[]{:S(2)}) async-start(), calls=%async_computation.6 | async-start | bytes 5013504 | tf_op jit(solution)/shard_map/all_gather | solution.py:378
  52.6 8.5 %collective-permute-start.4 = (bf16[128,1536]{1,0:T(8,128)(2,1)}, bf16[128,1536]{1,0:T(8,128)(2,1)S(1)}, u32[]{:S(2)}, u32[]{:S(2)}) collective-permute-start(bf16[128,1536]{1,0:T(8,128)(2,1)} %get-tuple-element.390), channel_id=1, source_target_pairs={{0,32},{32,0},{1,33},{33,1},{2,34},{34,2},{3,35},{35,3},{4,36},{36... | collective-permute-start | bytes 1179656 | tf_op jit(solution)/shard_map/ppermute | solution.py:35
  84.2 12.9 %collective-permute-start.6 = (bf16[256,384]{1,0:T(8,128)(2,1)S(1)}, bf16[256,384]{1,0:T(8,128)(2,1)S(1)}, u32[]{:S(2)}, u32[]{:S(2)}) collective-permute-start(bf16[256,384]{1,0:T(8,128)(2,1)S(1)} %get-tuple-element.342), channel_id=1, source_target_pairs={{0,1},{1,0},{2,3},{3,2},{8,9},{9,8},{10,11},{11,10},{4,5},{5,4},{6... | collective-permute-start | bytes 589832 | tf_op jit(solution)/shard_map/ppermute | solution.py:58
  90.3 8.7 %collective-permute-start.7 = (bf16[256,384]{1,0:T(8,128)(2,1)S(1)}, bf16[256,384]{1,0:T(8,128)(2,1)S(1)}, u32[]{:S(2)}, u32[]{:S(2)}) collective-permute-start(bf16[256,384]{1,0:T(8,128)(2,1)S(1)} %get-tuple-element.342), channel_id=1, source_target_pairs={{0,2},{1,3},{2,0},{3,1},{8,10},{9,11},{10,8},{11,9},{4,6},{5,7},{6... | collective-permute-start | bytes 589832 | tf_op jit(solution)/shard_map/ppermute | solution.py:58
  93.4 15.3 %collective-permute-start.12 = (bf16[256,384]{1,0:T(8,128)(2,1)S(1)}, bf16[256,384]{1,0:T(8,128)(2,1)S(1)}, u32[]{:S(2)}, u32[]{:S(2)}) collective-permute-start(bf16[256,384]{1,0:T(8,128)(2,1)S(1)} %get-tuple-element.342), channel_id=1, source_target_pairs={{0,11},{1,10},{2,9},{3,8},{8,3},{9,2},{10,1},{11,0},{4,15},{5,14},... | collective-permute-start | bytes 589832 | tf_op jit(solution)/shard_map/ppermute | solution.py:58
  93.4 15.2 %collective-permute-start.11 = (bf16[256,384]{1,0:T(8,128)(2,1)S(1)}, bf16[256,384]{1,0:T(8,128)(2,1)S(1)}, u32[]{:S(2)}, u32[]{:S(2)}) collective-permute-start(bf16[256,384]{1,0:T(8,128)(2,1)S(1)} %get-tuple-element.342), channel_id=1, source_target_pairs={{0,10},{1,11},{2,8},{3,9},{8,2},{9,3},{10,0},{11,1},{4,14},{5,15},... | collective-permute-start | bytes 589832 | tf_op jit(solution)/shard_map/ppermute | solution.py:58
  95.5 13.1 %collective-permute-start.10 = (bf16[256,384]{1,0:T(8,128)(2,1)S(1)}, bf16[256,384]{1,0:T(8,128)(2,1)S(1)}, u32[]{:S(2)}, u32[]{:S(2)}) collective-permute-start(bf16[256,384]{1,0:T(8,128)(2,1)S(1)} %get-tuple-element.342), channel_id=1, source_target_pairs={{0,9},{1,8},{2,11},{3,10},{8,1},{9,0},{10,3},{11,2},{4,13},{5,12},... | collective-permute-start | bytes 589832 | tf_op jit(solution)/shard_map/ppermute | solution.py:58
  97.0 7.9 %collective-permute-start.8 = (bf16[256,384]{1,0:T(8,128)(2,1)S(1)}, bf16[256,384]{1,0:T(8,128)(2,1)S(1)}, u32[]{:S(2)}, u32[]{:S(2)}) collective-permute-start(bf16[256,384]{1,0:T(8,128)(2,1)S(1)} %get-tuple-element.342), channel_id=1, source_target_pairs={{0,3},{1,2},{2,1},{3,0},{8,11},{9,10},{10,9},{11,8},{4,7},{5,6},{6... | collective-permute-start | bytes 589832 | tf_op jit(solution)/shard_map/ppermute | solution.py:58
  99.0 9.5 %collective-permute-start.9 = (bf16[256,384]{1,0:T(8,128)(2,1)S(1)}, bf16[256,384]{1,0:T(8,128)(2,1)S(1)}, u32[]{:S(2)}, u32[]{:S(2)}) collective-permute-start(bf16[256,384]{1,0:T(8,128)(2,1)S(1)} %get-tuple-element.342), channel_id=1, source_target_pairs={{0,8},{1,9},{2,10},{3,11},{8,0},{9,1},{10,2},{11,3},{4,12},{5,13},... | collective-permute-start | bytes 589832 | tf_op jit(solution)/shard_map/ppermute | solution.py:58
  118.1 23.9 %collective-permute-start.14 = (bf16[4,32,1536]{2,1,0:T(8,128)(2,1)S(1)}, bf16[4,32,1536]{2,1,0:T(8,128)(2,1)S(1)}, u32[]{:S(2)}, u32[]{:S(2)}) collective-permute-start(bf16[4,32,1536]{2,1,0:T(8,128)(2,1)S(1)} %bitcast.356), channel_id=1, source_target_pairs={{0,32},{32,0},{1,33},{33,1},{2,34},{34,2},{3,35},{35,3},{4,36},{36... | collective-permute-start | bytes 1179656 | tf_op jit(solution)/shard_map/ppermute | solution.py:35
  200.7 67.3 %collective-permute-start.70 = (bf16[16,1536]{1,0:T(8,128)(2,1)}, bf16[16,1536]{1,0:T(8,128)(2,1)}, u32[]{:S(2)}, u32[]{:S(2)}) collective-permute-start(bf16[16,1536]{1,0:T(8,128)(2,1)} %select_n.396), channel_id=1, source_target_pairs={{0,16},{16,0},{1,17},{17,1},{2,18},{18,2},{3,19},{19,3},{4,20},{20... | collective-permute-start | bytes 147464 | tf_op jit(solution)/shard_map/ppermute | solution.py:35
  211.7 54.4 %collective-permute-start.62 = (bf16[48,1536]{1,0:T(8,128)(2,1)}, bf16[48,1536]{1,0:T(8,128)(2,1)}, u32[]{:S(2)}, u32[]{:S(2)}) collective-permute-start(bf16[48,1536]{1,0:T(8,128)(2,1)} %get-tuple-element.345), channel_id=1, source_target_pairs={{0,4},{4,0},{1,5},{5,1},{2,6},{6,2},{3,7},{7,3},{8,12},{12,8},{9,1... | collective-permute-start | bytes 442376 | tf_op jit(solution)/shard_map/ppermute | solution.py:35
  214.6 8.6 %collective-permute-start.38 = (bf16[128,1536]{1,0:T(8,128)(2,1)S(1)}, bf16[128,1536]{1,0:T(8,128)(2,1)S(1)}, u32[]{:S(2)}, u32[]{:S(2)}) collective-permute-start(bf16[128,1536]{1,0:T(8,128)(2,1)S(1)} %pad_maximum_fusion.3), channel_id=1, source_target_pairs={{0,32},{32,0},{1,33},{33,1},{2,34},{34,2},{3,35},{35,3},{4,36},{36... | collective-permute-start | bytes 1179656 | tf_op jit(solution)/shard_map/ppermute | solution.py:35
  226.9 12.7 %collective-permute-start.40 = (bf16[256,384]{1,0:T(8,128)(2,1)S(1)}, bf16[256,384]{1,0:T(8,128)(2,1)S(1)}, u32[]{:S(2)}, u32[]{:S(2)}) collective-permute-start(bf16[256,384]{1,0:T(8,128)(2,1)S(1)} %get-tuple-element.340), channel_id=1, source_target_pairs={{0,2},{1,3},{2,0},{3,1},{8,10},{9,11},{10,8},{11,9},{4,6},{5,7},{6... | collective-permute-start | bytes 589832 | tf_op jit(solution)/shard_map/ppermute | solution.py:58
  227.9 9.5 %collective-permute-start.39 = (bf16[256,384]{1,0:T(8,128)(2,1)S(1)}, bf16[256,384]{1,0:T(8,128)(2,1)S(1)}, u32[]{:S(2)}, u32[]{:S(2)}) collective-permute-start(bf16[256,384]{1,0:T(8,128)(2,1)S(1)} %get-tuple-element.340), channel_id=1, source_target_pairs={{0,1},{1,0},{2,3},{3,2},{8,9},{9,8},{10,11},{11,10},{4,5},{5,4},{6... | collective-permute-start | bytes 589832 | tf_op jit(solution)/shard_map/ppermute | solution.py:58
  228.7 27.0 %collective-permute-start.45 = (bf16[256,384]{1,0:T(8,128)(2,1)S(1)}, bf16[256,384]{1,0:T(8,128)(2,1)S(1)}, u32[]{:S(2)}, u32[]{:S(2)}) collective-permute-start(bf16[256,384]{1,0:T(8,128)(2,1)S(1)} %get-tuple-element.340), channel_id=1, source_target_pairs={{0,11},{1,10},{2,9},{3,8},{8,3},{9,2},{10,1},{11,0},{4,15},{5,14},... | collective-permute-start | bytes 589832 | tf_op jit(solution)/shard_map/ppermute | solution.py:58
  244.9 10.8 %collective-permute-start.44 = (bf16[256,384]{1,0:T(8,128)(2,1)S(1)}, bf16[256,384]{1,0:T(8,128)(2,1)S(1)}, u32[]{:S(2)}, u32[]{:S(2)}) collective-permute-start(bf16[256,384]{1,0:T(8,128)(2,1)S(1)} %get-tuple-element.340), channel_id=1, source_target_pairs={{0,10},{1,11},{2,8},{3,9},{8,2},{9,3},{10,0},{11,1},{4,14},{5,15},... | collective-permute-start | bytes 589832 | tf_op jit(solution)/shard_map/ppermute | solution.py:58
  263.1 8.2 %collective-permute-start.46 = (bf16[4,32,1536]{2,1,0:T(8,128)(2,1)S(1)}, bf16[4,32,1536]{2,1,0:T(8,128)(2,1)S(1)}, u32[]{:S(2)}, u32[]{:S(2)}) collective-permute-start(bf16[4,32,1536]{2,1,0:T(8,128)(2,1)S(1)} %bitcast.352), channel_id=1, source_target_pairs={{0,32},{32,0},{1,33},{33,1},{2,34},{34,2},{3,35},{35,3},{4,36},{36... | collective-permute-start | bytes 1179656 | tf_op jit(solution)/shard_map/ppermute | solution.py:35
  267.9 233.8 %reduce-scatter.3.cloned.1.call-start = ((), (), s32[]{:S(2)}) async-start(), calls=%async_computation.7 | async-start | bytes 7520256 | tf_op jit(solution)/shard_map/reduce_scatter | solution.py:530
  269.4 33.4 %collective-permute-start.73 = (bf16[32,1536]{1,0:T(8,128)(2,1)S(1)}, bf16[32,1536]{1,0:T(8,128)(2,1)S(1)}, u32[]{:S(2)}, u32[]{:S(2)}) collective-permute-start(bf16[32,1536]{1,0:T(8,128)(2,1)S(1)} %get-tuple-element.404), channel_id=1, source_target_pairs={{0,68},{4,64},{64,4},{68,0},{1,69},{5,65},{65,5},{69,1},{2,70},{6,... | collective-permute-start | bytes 294920 | tf_op jit(solution)/shard_map/ppermute | solution.py:39
  270.9 27.4 %collective-permute-start.72 = (bf16[32,1536]{1,0:T(8,128)(2,1)S(1)}, bf16[32,1536]{1,0:T(8,128)(2,1)S(1)}, u32[]{:S(2)}, u32[]{:S(2)}) collective-permute-start(bf16[32,1536]{1,0:T(8,128)(2,1)S(1)} %get-tuple-element.404), channel_id=1, source_target_pairs={{0,64},{4,68},{64,0},{68,4},{1,65},{5,69},{65,1},{69,5},{2,66},{6,... | collective-permute-start | bytes 294920 | tf_op jit(solution)/shard_map/ppermute | solution.py:39
  285.8 12.0 %collective-permute-start.71 = (bf16[32,1536]{1,0:T(8,128)(2,1)S(1)}, bf16[32,1536]{1,0:T(8,128)(2,1)S(1)}, u32[]{:S(2)}, u32[]{:S(2)}) collective-permute-start(bf16[32,1536]{1,0:T(8,128)(2,1)S(1)} %get-tuple-element.404), channel_id=1, source_target_pairs={{0,4},{4,0},{64,68},{68,64},{1,5},{5,1},{65,69},{69,65},{2,6},{6,2... | collective-permute-start | bytes 294920 | tf_op jit(solution)/shard_map/ppermute | solution.py:39
  361.0 10.9 %collective-permute-start.84 = (bf16[32,1536]{1,0:T(8,128)(2,1)}, bf16[32,1536]{1,0:T(8,128)(2,1)}, u32[]{:S(2)}, u32[]{:S(2)}) collective-permute-start(bf16[32,1536]{1,0:T(8,128)(2,1)} %get-tuple-element.316), channel_id=1, source_target_pairs={{0,4},{4,0},{64,68},{68,64},{1,5},{5,1},{65,69},{69,65},{2,6},{6,2... | collective-permute-start | bytes 294920 | tf_op jit(solution)/shard_map/ppermute | solution.py:51
  361.7 10.3 %collective-permute-start.86 = (bf16[32,1536]{1,0:T(8,128)(2,1)}, bf16[32,1536]{1,0:T(8,128)(2,1)}, u32[]{:S(2)}, u32[]{:S(2)}) collective-permute-start(bf16[32,1536]{1,0:T(8,128)(2,1)} %get-tuple-element.317), channel_id=1, source_target_pairs={{0,68},{4,64},{64,4},{68,0},{1,69},{5,65},{65,5},{69,1},{2,70},{6,... | collective-permute-start | bytes 294920 | tf_op jit(solution)/shard_map/ppermute | solution.py:51
  363.0 8.9 %collective-permute-start.85 = (bf16[32,1536]{1,0:T(8,128)(2,1)}, bf16[32,1536]{1,0:T(8,128)(2,1)}, u32[]{:S(2)}, u32[]{:S(2)}) collective-permute-start(bf16[32,1536]{1,0:T(8,128)(2,1)} %get-tuple-element.318), channel_id=1, source_target_pairs={{0,64},{4,68},{64,0},{68,4},{1,65},{5,69},{65,1},{69,5},{2,66},{6,... | collective-permute-start | bytes 294920 | tf_op jit(solution)/shard_map/ppermute | solution.py:51
  373.2 252.5 %reduce-scatter.5.cloned.1.call-start = ((), (), s32[]{:S(2)}) async-start(), calls=%async_computation.8 | async-start | bytes 11280384 | tf_op jit(solution)/shard_map/reduce_scatter | solution.py:530
  393.6 9.9 %collective-permute-start.91 = (bf16[256,384]{1,0:T(8,128)(2,1)S(1)}, bf16[256,384]{1,0:T(8,128)(2,1)S(1)}, u32[]{:S(2)}, u32[]{:S(2)}) collective-permute-start(bf16[256,384]{1,0:T(8,128)(2,1)S(1)} %get-tuple-element.248), channel_id=1, source_target_pairs={{0,1},{1,0},{2,3},{3,2},{8,9},{9,8},{10,11},{11,10},{4,5},{5,4},{6... | collective-permute-start | bytes 589832 | tf_op jit(solution)/shard_map/ppermute | solution.py:67
  394.9 13.2 %collective-permute-start.97 = (bf16[256,384]{1,0:T(8,128)(2,1)S(1)}, bf16[256,384]{1,0:T(8,128)(2,1)S(1)}, u32[]{:S(2)}, u32[]{:S(2)}) collective-permute-start(bf16[256,384]{1,0:T(8,128)(2,1)S(1)} %get-tuple-element.249), channel_id=1, source_target_pairs={{0,11},{1,10},{2,9},{3,8},{8,3},{9,2},{10,1},{11,0},{4,15},{5,14},... | collective-permute-start | bytes 589832 | tf_op jit(solution)/shard_map/ppermute | solution.py:67
  396.2 16.4 %collective-permute-start.96 = (bf16[256,384]{1,0:T(8,128)(2,1)S(1)}, bf16[256,384]{1,0:T(8,128)(2,1)S(1)}, u32[]{:S(2)}, u32[]{:S(2)}) collective-permute-start(bf16[256,384]{1,0:T(8,128)(2,1)S(1)} %get-tuple-element.250), channel_id=1, source_target_pairs={{0,10},{1,11},{2,8},{3,9},{8,2},{9,3},{10,0},{11,1},{4,14},{5,15},... | collective-permute-start | bytes 589832 | tf_op jit(solution)/shard_map/ppermute | solution.py:67
  397.8 18.4 %collective-permute-start.95 = (bf16[256,384]{1,0:T(8,128)(2,1)S(1)}, bf16[256,384]{1,0:T(8,128)(2,1)S(1)}, u32[]{:S(2)}, u32[]{:S(2)}) collective-permute-start(bf16[256,384]{1,0:T(8,128)(2,1)S(1)} %get-tuple-element.251), channel_id=1, source_target_pairs={{0,9},{1,8},{2,11},{3,10},{8,1},{9,0},{10,3},{11,2},{4,13},{5,12},... | collective-permute-start | bytes 589832 | tf_op jit(solution)/shard_map/ppermute | solution.py:67
  398.7 22.9 %collective-permute-start.94 = (bf16[256,384]{1,0:T(8,128)(2,1)S(1)}, bf16[256,384]{1,0:T(8,128)(2,1)S(1)}, u32[]{:S(2)}, u32[]{:S(2)}) collective-permute-start(bf16[256,384]{1,0:T(8,128)(2,1)S(1)} %get-tuple-element.252), channel_id=1, source_target_pairs={{0,8},{1,9},{2,10},{3,11},{8,0},{9,1},{10,2},{11,3},{4,12},{5,13},... | collective-permute-start | bytes 589832 | tf_op jit(solution)/shard_map/ppermute | solution.py:67
  403.5 18.1 %collective-permute-start.93 = (bf16[256,384]{1,0:T(8,128)(2,1)S(1)}, bf16[256,384]{1,0:T(8,128)(2,1)S(1)}, u32[]{:S(2)}, u32[]{:S(2)}) collective-permute-start(bf16[256,384]{1,0:T(8,128)(2,1)S(1)} %get-tuple-element.253), channel_id=1, source_target_pairs={{0,3},{1,2},{2,1},{3,0},{8,11},{9,10},{10,9},{11,8},{4,7},{5,6},{6... | collective-permute-start | bytes 589832 | tf_op jit(solution)/shard_map/ppermute | solution.py:67
  408.1 15.3 %collective-permute-start.92 = (bf16[256,384]{1,0:T(8,128)(2,1)S(1)}, bf16[256,384]{1,0:T(8,128)(2,1)S(1)}, u32[]{:S(2)}, u32[]{:S(2)}) collective-permute-start(bf16[256,384]{1,0:T(8,128)(2,1)S(1)} %get-tuple-element.254), channel_id=1, source_target_pairs={{0,2},{1,3},{2,0},{3,1},{8,10},{9,11},{10,8},{11,9},{4,6},{5,7},{6... | collective-permute-start | bytes 589832 | tf_op jit(solution)/shard_map/ppermute | solution.py:67
  478.8 12.9 %collective-permute-start.115 = (bf16[32,1536]{1,0:T(8,128)(2,1)S(1)}, bf16[32,1536]{1,0:T(8,128)(2,1)S(1)}, u32[]{:S(2)}, u32[]{:S(2)}) collective-permute-start(bf16[32,1536]{1,0:T(8,128)(2,1)S(1)} %get-tuple-element.307), channel_id=1, source_target_pairs={{0,4},{4,0},{64,68},{68,64},{1,5},{5,1},{65,69},{69,65},{2,6},{6,2... | collective-permute-start | bytes 294920 | tf_op jit(solution)/shard_map/ppermute | solution.py:51
  479.4 12.3 %collective-permute-start.117 = (bf16[32,1536]{1,0:T(8,128)(2,1)S(1)}, bf16[32,1536]{1,0:T(8,128)(2,1)S(1)}, u32[]{:S(2)}, u32[]{:S(2)}) collective-permute-start(bf16[32,1536]{1,0:T(8,128)(2,1)S(1)} %get-tuple-element.308), channel_id=1, source_target_pairs={{0,68},{4,64},{64,4},{68,0},{1,69},{5,65},{65,5},{69,1},{2,70},{6,... | collective-permute-start | bytes 294920 | tf_op jit(solution)/shard_map/ppermute | solution.py:51
  480.9 10.8 %collective-permute-start.116 = (bf16[32,1536]{1,0:T(8,128)(2,1)S(1)}, bf16[32,1536]{1,0:T(8,128)(2,1)S(1)}, u32[]{:S(2)}, u32[]{:S(2)}) collective-permute-start(bf16[32,1536]{1,0:T(8,128)(2,1)S(1)} %get-tuple-element.309), channel_id=1, source_target_pairs={{0,64},{4,68},{64,0},{68,4},{1,65},{5,69},{65,1},{69,5},{2,66},{6,... | collective-permute-start | bytes 294920 | tf_op jit(solution)/shard_map/ppermute | solution.py:51
  506.1 18.3 %collective-permute-start.69 = (bf16[2,2,16,1536]{3,2,1,0:T(8,128)(2,1)S(1)}, bf16[2,2,16,1536]{3,2,1,0:T(8,128)(2,1)S(1)}, u32[]{:S(2)}, u32[]{:S(2)}) collective-permute-start(bf16[2,2,16,1536]{3,2,1,0:T(8,128)(2,1)S(1)} %reverse_select_fusion.3), channel_id=1, source_target_pairs={{0,64},{64,0},{1,65},{65,1},{2,66},{66,2},{3,67},{67,3},{4,68},{68... | collective-permute-start | bytes 589832 | tf_op jit(solution)/shard_map/ppermute | solution.py:35
  522.9 10.6 %collective-permute-start.122 = (bf16[256,384]{1,0:T(8,128)(2,1)S(1)}, bf16[256,384]{1,0:T(8,128)(2,1)S(1)}, u32[]{:S(2)}, u32[]{:S(2)}) collective-permute-start(bf16[256,384]{1,0:T(8,128)(2,1)S(1)} %get-tuple-element.241), channel_id=1, source_target_pairs={{0,1},{1,0},{2,3},{3,2},{8,9},{9,8},{10,11},{11,10},{4,5},{5,4},{6... | collective-permute-start | bytes 589832 | tf_op jit(solution)/shard_map/ppermute | solution.py:67
  523.0 13.6 %collective-permute-start.128 = (bf16[256,384]{1,0:T(8,128)(2,1)S(1)}, bf16[256,384]{1,0:T(8,128)(2,1)S(1)}, u32[]{:S(2)}, u32[]{:S(2)}) collective-permute-start(bf16[256,384]{1,0:T(8,128)(2,1)S(1)} %get-tuple-element.242), channel_id=1, source_target_pairs={{0,11},{1,10},{2,9},{3,8},{8,3},{9,2},{10,1},{11,0},{4,15},{5,14},... | collective-permute-start | bytes 589832 | tf_op jit(solution)/shard_map/ppermute | solution.py:67
  524.5 18.3 %collective-permute-start.127 = (bf16[256,384]{1,0:T(8,128)(2,1)S(1)}, bf16[256,384]{1,0:T(8,128)(2,1)S(1)}, u32[]{:S(2)}, u32[]{:S(2)}) collective-permute-start(bf16[256,384]{1,0:T(8,128)(2,1)S(1)} %get-tuple-element.243), channel_id=1, source_target_pairs={{0,10},{1,11},{2,8},{3,9},{8,2},{9,3},{10,0},{11,1},{4,14},{5,15},... | collective-permute-start | bytes 589832 | tf_op jit(solution)/shard_map/ppermute | solution.py:67
  527.3 19.4 %collective-permute-start.126 = (bf16[256,384]{1,0:T(8,128)(2,1)S(1)}, bf16[256,384]{1,0:T(8,128)(2,1)S(1)}, u32[]{:S(2)}, u32[]{:S(2)}) collective-permute-start(bf16[256,384]{1,0:T(8,128)(2,1)S(1)} %get-tuple-element.244), channel_id=1, source_target_pairs={{0,9},{1,8},{2,11},{3,10},{8,1},{9,0},{10,3},{11,2},{4,13},{5,12},... | collective-permute-start | bytes 589832 | tf_op jit(solution)/shard_map/ppermute | solution.py:67
  527.3 22.6 %collective-permute-start.125 = (bf16[256,384]{1,0:T(8,128)(2,1)S(1)}, bf16[256,384]{1,0:T(8,128)(2,1)S(1)}, u32[]{:S(2)}, u32[]{:S(2)}) collective-permute-start(bf16[256,384]{1,0:T(8,128)(2,1)S(1)} %get-tuple-element.245), channel_id=1, source_target_pairs={{0,8},{1,9},{2,10},{3,11},{8,0},{9,1},{10,2},{11,3},{4,12},{5,13},... | collective-permute-start | bytes 589832 | tf_op jit(solution)/shard_map/ppermute | solution.py:67
  533.5 16.3 %collective-permute-start.124 = (bf16[256,384]{1,0:T(8,128)(2,1)S(1)}, bf16[256,384]{1,0:T(8,128)(2,1)S(1)}, u32[]{:S(2)}, u32[]{:S(2)}) collective-permute-start(bf16[256,384]{1,0:T(8,128)(2,1)S(1)} %get-tuple-element.246), channel_id=1, source_target_pairs={{0,3},{1,2},{2,1},{3,0},{8,11},{9,10},{10,9},{11,8},{4,7},{5,6},{6... | collective-permute-start | bytes 589832 | tf_op jit(solution)/shard_map/ppermute | solution.py:67
  536.6 18.4 %collective-permute-start.123 = (bf16[256,384]{1,0:T(8,128)(2,1)S(1)}, bf16[256,384]{1,0:T(8,128)(2,1)S(1)}, u32[]{:S(2)}, u32[]{:S(2)}) collective-permute-start(bf16[256,384]{1,0:T(8,128)(2,1)S(1)} %get-tuple-element.247), channel_id=1, source_target_pairs={{0,2},{1,3},{2,0},{3,1},{8,10},{9,11},{10,8},{11,9},{4,6},{5,7},{6... | collective-permute-start | bytes 589832 | tf_op jit(solution)/shard_map/ppermute | solution.py:67
  556.4 8.7 %collective-permute-start.129 = (bf16[4,48,1536]{2,1,0:T(8,128)(2,1)S(1)}, bf16[4,48,1536]{2,1,0:T(8,128)(2,1)S(1)}, u32[]{:S(2)}, u32[]{:S(2)}) collective-permute-start(bf16[4,48,1536]{2,1,0:T(8,128)(2,1)S(1)} %fusion.24), channel_id=1, source_target_pairs={{0,32},{32,0},{1,33},{33,1},{2,34},{34,2},{3,35},{35,3},{4,36},{36... | collective-permute-start | bytes 1769480 | tf_op jit(solution)/shard_map/ppermute | solution.py:35
  558.7 86.1 %collective-permute-start.139 = (bf16[48,2304]{1,0:T(8,128)(2,1)}, bf16[48,2304]{1,0:T(8,128)(2,1)S(1)}, u32[]{:S(2)}, u32[]{:S(2)}) collective-permute-start(bf16[48,2304]{1,0:T(8,128)(2,1)} %get-tuple-element.305), channel_id=1, source_target_pairs={{0,4},{4,0},{1,5},{5,1},{2,6},{6,2},{3,7},{7,3},{8,12},{12,8},{9,1... | collective-permute-start | bytes 663560 | tf_op jit(solution)/shard_map/ppermute | solution.py:35
  561.1 16.7 %collective-permute-start.140 = (bf16[384,768]{1,0:T(8,128)(2,1)S(1)}, bf16[384,768]{1,0:T(8,128)(2,1)S(1)}, u32[]{:S(2)}, u32[]{:S(2)}) collective-permute-start(bf16[384,768]{1,0:T(8,128)(2,1)S(1)} %get-tuple-element.238), channel_id=1, source_target_pairs={{0,1},{1,0},{2,3},{3,2},{4,5},{5,4},{6,7},{7,6},{8,9},{9,8},{10,11... | collective-permute-start | bytes 1769480 | tf_op jit(solution)/shard_map/ppermute | solution.py:84
  561.2 37.0 %collective-permute-start.142 = (bf16[384,768]{1,0:T(8,128)(2,1)S(1)}, bf16[384,768]{1,0:T(8,128)(2,1)S(1)}, u32[]{:S(2)}, u32[]{:S(2)}) collective-permute-start(bf16[384,768]{1,0:T(8,128)(2,1)S(1)} %get-tuple-element.239), channel_id=1, source_target_pairs={{0,2},{1,3},{2,0},{3,1},{4,6},{5,7},{6,4},{7,5},{8,10},{9,11},{10,... | collective-permute-start | bytes 1769480 | tf_op jit(solution)/shard_map/ppermute | solution.py:84
  563.1 36.3 %collective-permute-start.141 = (bf16[384,768]{1,0:T(8,128)(2,1)S(1)}, bf16[384,768]{1,0:T(8,128)(2,1)S(1)}, u32[]{:S(2)}, u32[]{:S(2)}) collective-permute-start(bf16[384,768]{1,0:T(8,128)(2,1)S(1)} %get-tuple-element.240), channel_id=1, source_target_pairs={{0,3},{1,2},{2,1},{3,0},{4,7},{5,6},{6,5},{7,4},{8,11},{9,10},{10,... | collective-permute-start | bytes 1769480 | tf_op jit(solution)/shard_map/ppermute | solution.py:84
  565.3 34.8 %collective-permute-start.130 = (bf16[48,1536]{1,0:T(8,128)(2,1)S(1)}, bf16[48,1536]{1,0:T(8,128)(2,1)S(1)}, u32[]{:S(2)}, u32[]{:S(2)}) collective-permute-start(bf16[48,1536]{1,0:T(8,128)(2,1)S(1)} %get-tuple-element.300), channel_id=1, source_target_pairs={{0,4},{4,0},{64,68},{68,64},{1,5},{5,1},{65,69},{69,65},{2,6},{6,2... | collective-permute-start | bytes 442376 | tf_op jit(solution)/shard_map/ppermute | solution.py:51
  577.9 23.6 %collective-permute-start.132 = (bf16[48,1536]{1,0:T(8,128)(2,1)S(1)}, bf16[48,1536]{1,0:T(8,128)(2,1)S(1)}, u32[]{:S(2)}, u32[]{:S(2)}) collective-permute-start(bf16[48,1536]{1,0:T(8,128)(2,1)S(1)} %get-tuple-element.301), channel_id=1, source_target_pairs={{0,68},{4,64},{64,4},{68,0},{1,69},{5,65},{65,5},{69,1},{2,70},{6,... | collective-permute-start | bytes 442376 | tf_op jit(solution)/shard_map/ppermute | solution.py:51
  599.8 13.0 %collective-permute-start.143 = (bf16[96,768]{1,0:T(8,128)(2,1)S(1)}, bf16[96,768]{1,0:T(8,128)(2,1)S(1)}, u32[]{:S(2)}, u32[]{:S(2)}) collective-permute-start(bf16[96,768]{1,0:T(8,128)(2,1)S(1)} %get-tuple-element.297), channel_id=1, source_target_pairs={{0,8},{8,0},{16,24},{24,16},{1,9},{9,1},{17,25},{25,17},{2,10},{10... | collective-permute-start | bytes 442376 | tf_op jit(solution)/shard_map/ppermute | solution.py:84
  600.1 12.7 %collective-permute-start.145 = (bf16[96,768]{1,0:T(8,128)(2,1)S(1)}, bf16[96,768]{1,0:T(8,128)(2,1)S(1)}, u32[]{:S(2)}, u32[]{:S(2)}) collective-permute-start(bf16[96,768]{1,0:T(8,128)(2,1)S(1)} %get-tuple-element.298), channel_id=1, source_target_pairs={{0,16},{8,24},{16,0},{24,8},{1,17},{9,25},{17,1},{25,9},{2,18},{10... | collective-permute-start | bytes 442376 | tf_op jit(solution)/shard_map/ppermute | solution.py:84
  601.4 11.4 %collective-permute-start.144 = (bf16[96,768]{1,0:T(8,128)(2,1)S(1)}, bf16[96,768]{1,0:T(8,128)(2,1)S(1)}, u32[]{:S(2)}, u32[]{:S(2)}) collective-permute-start(bf16[96,768]{1,0:T(8,128)(2,1)S(1)} %get-tuple-element.299), channel_id=1, source_target_pairs={{0,24},{8,16},{16,8},{24,0},{1,25},{9,17},{17,9},{25,1},{2,26},{10... | collective-permute-start | bytes 442376 | tf_op jit(solution)/shard_map/ppermute | solution.py:84
  605.0 11.4 %all-to-all-start.1 = ((bf16[16,16,96]{2,1,0:T(8,128)(2,1)}), bf16[16,16,96]{2,1,0:T(8,128)(2,1)S(1)}, u32[]{:S(2)}, u32[]{:S(2)}) async-start(bf16[16,16,96]{2,1,0:T(8,128)(2,1)} %bitcast.329), calls=%async_computation.3 | async-start | bytes 131072 | tf_op jit(solution)/shard_map/all_to_all | solution.py:595
  613.2 31.6 %collective-permute-start.146 = (bf16[48,768]{1,0:T(8,128)(2,1)S(1)}, bf16[48,768]{1,0:T(8,128)(2,1)S(1)}, u32[]{:S(2)}, u32[]{:S(2)}) collective-permute-start(bf16[48,768]{1,0:T(8,128)(2,1)S(1)} %get-tuple-element.365), channel_id=1, source_target_pairs={{0,4},{4,0},{1,5},{5,1},{2,6},{6,2},{3,7},{7,3},{8,12},{12,8},{9,1... | collective-permute-start | bytes 221192 | tf_op jit(solution)/shard_map/ppermute | solution.py:35
  624.4 8.1 %collective-permute-start.135 = (bf16[2,2,16,1536]{3,2,1,0:T(8,128)(2,1)S(1)}, bf16[2,2,16,1536]{3,2,1,0:T(8,128)(2,1)S(1)}, u32[]{:S(2)}, u32[]{:S(2)}) collective-permute-start(bf16[2,2,16,1536]{3,2,1,0:T(8,128)(2,1)S(1)} %reverse_select_fusion.2), channel_id=1, source_target_pairs={{0,64},{64,0},{1,65},{65,1},{2,66},{66,2},{3,67},{67,3},{4,68},{68... | collective-permute-start | bytes 589832 | tf_op jit(solution)/shard_map/ppermute | solution.py:35
  626.8 11.7 %collective-permute-start.136 = (bf16[48,3456]{1,0:T(8,128)(2,1)S(1)}, bf16[48,3456]{1,0:T(8,128)(2,1)S(1)}, u32[]{:S(2)}, u32[]{:S(2)}) collective-permute-start(bf16[48,3456]{1,0:T(8,128)(2,1)S(1)} %get-tuple-element.296), channel_id=1, source_target_pairs={{0,4},{4,0},{1,5},{5,1},{2,6},{6,2},{3,7},{7,3},{8,12},{12,8},{9,1... | collective-permute-start | bytes 995336 | tf_op jit(solution)/shard_map/ppermute | solution.py:35
  (199 other events, 2084.6 us)
Sparse Core Ops, SparseCore 0:
  19.6 76.2 all-gather.3
  98.7 80.5 all-gather.5
  268.0 49.8 all-gather.7
  373.3 94.6 reduce-scatter.2
  491.9 114.0 reduce-scatter.4

commit v3 on v2

v3 whole, which is shorter than its diff:
```python
import math

import jax
import jax.numpy as jnp
from jax import lax
from jax.experimental import pallas as pl
from jax.experimental.pallas import tpu as pltpu
from jax.sharding import Mesh, PartitionSpec as P

HEAD = 64
HEADS_HERE = 3
WIDE = HEAD * HEADS_HERE
NEG_FILL = -1e30
NORM_EPS = 1e-05
SCALE = 1.0 / math.sqrt(HEAD)
LOW = jnp.bfloat16
FULL = jnp.float32

FINE = ("xh", "core", "zh", "zl", "xl", "y")
FINE_SIZES = (2, 2, 2, 2, 2, 4)
ROW = ("xh", "core")
COL = ("zh", "zl", "xl", "y")
CHIPS = ("xh", "xl")
SPREAD = ("y", "zh", "zl")
DEEP = ("zh", "zl")
KEYED = ("zl", "y")
SWAP = ((0, 1), (1, 0))


def flipped(size, mask):
    return [(i, i ^ mask) for i in range(size)]


def swapped(x, axis):
    return lax.ppermute(x, axis, SWAP)


def rows_of_all(rows):
    chips = [rows] + [lax.ppermute(rows, CHIPS, flipped(4, d)) for d in (1, 2, 3)]
    half = jnp.concatenate(chips, axis=0)
    return [half, swapped(half, "core")]


def sum_to_rows(partial):
    count = partial.shape[0] // 8
    blocks = partial.reshape(2, 4, count, partial.shape[1])
    both = blocks[0].astype(FULL) + swapped(blocks[1].astype(LOW), "core").astype(FULL)
    low = both.astype(LOW)
    total = both[0]
    for d in (1, 2, 3):
        total = total + lax.ppermute(low[d], CHIPS, flipped(4, d)).astype(FULL)
    return total


def keys_pair(block):
    return jnp.concatenate([block, swapped(block, "zl")], axis=0)


def keys_of_all(pair):
    return [pair] + [lax.ppermute(pair, "y", flipped(4, d)) for d in (1, 2, 3)]


def keyed_mask(d):
    return (d & 1) * 4 + d // 2


def keyed_of_all(block):
    return [block] + [
        lax.ppermute(block, KEYED, flipped(8, keyed_mask(d))) for d in range(1, 8)
    ]


def strips_of_all(own):
    y = lax.axis_index("y")
    z = lax.axis_index("zh") * 2 + lax.axis_index("zl")
    places = {"y": (0, y), DEEP: (1, z)}
    rows = own.shape[0] // 2

    def level(x, axis):
        at, here = places[axis]
        shape = list(x.shape)
        shape[at] = 4
        out = jnp.zeros(shape, x.dtype)
        out = lax.dynamic_update_slice_in_dim(out, x, here, axis=at)
        for d in (1, 3, 2):
            part = lax.ppermute(x, axis, flipped(4, d))
            out = lax.dynamic_update_slice_in_dim(out, part, here ^ d, axis=at)
        return out

    halves = own.reshape(1, 1, 2, rows, -1)
    first = level(level(halves[:, :, 0], DEEP), "y")
    second = level(level(halves[:, :, 1], "y"), DEEP)
    return jnp.stack([first, second], axis=2).reshape(32 * rows, -1)


def strip_blocks(partial):
    return partial.reshape(4, 4, partial.shape[0] // 16, -1)


def sum_along(values, axis):
    if axis == "y":
        at, here = 0, lax.axis_index("y")
    else:
        at, here = 1, lax.axis_index("zh") * 2 + lax.axis_index("zl")
    low = values.astype(LOW)

    def block(x, d):
        return lax.dynamic_slice_in_dim(x, here ^ d, 1, axis=at)

    total = block(values, 0).astype(FULL)
    for d in (1, 3, 2):
        total = total + lax.ppermute(block(low, d), axis, flipped(4, d)).astype(FULL)
    return total


def strip_of(total):
    return total.reshape(-1, total.shape[-1]).astype(LOW)


def tied(*arrays):
    return lax.optimization_barrier(arrays)


def mm(a, b, dims):
    return lax.dot_general(a, b, (dims, ((), ())), preferred_element_type=FULL)


def nn(a, b):
    return mm(a, b, ((1,), (0,)))


def nt(a, b):
    return mm(a, b, ((1,), (1,)))


def tn(a, b):
    return mm(a, b, ((0,), (0,)))


def unit(values):
    centre = jnp.mean(values, axis=-1, keepdims=True)
    centred = values - centre
    inverse = lax.rsqrt(jnp.mean(centred * centred, axis=-1, keepdims=True) + NORM_EPS)
    return centred * inverse, inverse


def unit_back(upstream, unit_rows, inverse, gain_row):
    scaled = upstream * gain_row
    inner = (
        scaled
        - jnp.mean(scaled, axis=-1, keepdims=True)
        - unit_rows * jnp.mean(scaled * unit_rows, axis=-1, keepdims=True)
    )
    return inner * inverse


def whole(x):
    return pl.BlockSpec(x.shape, lambda i: (0,) * x.ndim)


def window(columns, index, rows=None):
    return lambda x: pl.BlockSpec((x.shape[0], columns), lambda i: (0, index))


def kernel_call(body, args, outs, steps=1, specs=None, out_specs=None, room=16):
    shapes = [jax.ShapeDtypeStruct(shape, kind) for shape, kind in outs]
    placed = [(spec or whole)(x) for x, spec in zip(args, specs or [None] * len(args))]
    return pl.pallas_call(
        body,
        grid=(steps,),
        in_specs=placed,
        out_specs=out_specs or [whole(x) for x in shapes],
        out_shape=shapes,
        compiler_params=pltpu.CompilerParams(vmem_limit_bytes=room * 2**20),
    )(*args)


def stacked(refs):
    return jnp.concatenate([ref[...] for ref in refs], axis=0)


def head(x, h, start=0):
    return x[:, start + h * HEAD : start + (h + 1) * HEAD]


def attend_into(q, kv, bias, o_ref, lse_ref):
    rows = []
    for h in range(HEADS_HERE):
        s = nt(head(kv, h), head(q, h)) * SCALE + bias
        top = jnp.max(s, axis=0, keepdims=True)
        lse = top + jnp.log(jnp.sum(jnp.exp(s - top), axis=0, keepdims=True))
        p = jnp.exp(s - lse).astype(LOW)
        lse_ref[h : h + 1, :] = lse
        rows.append(tn(head(kv, h, WIDE), p))
    lse_ref[HEADS_HERE:, :] = jnp.zeros((8 - HEADS_HERE, lse_ref.shape[1]), FULL)
    o = jnp.concatenate(rows, axis=0).T.astype(LOW)
    o_ref[...] = o
    return o


def packed(values, stats):
    columns = stats.T
    high = columns.astype(LOW)
    rest = columns - high.astype(FULL)
    middle = rest.astype(LOW)
    low = (rest - middle.astype(FULL)).astype(LOW)
    spare = jnp.zeros((values.shape[0], 256 - values.shape[1] - 3 * 8), LOW)
    return jnp.concatenate([values, high, middle, low, spare], axis=1)


def stats_of(pack):
    turned = pack[:, 128:256].astype(FULL).T
    return turned[64:72] + turned[72:80] + turned[80:88]


def attend_back(do, q, kv, bias, lse_ref):
    dqs, dks, dvs = [], [], []
    for h in range(HEADS_HERE):
        k, v, q_h, do_h = head(kv, h), head(kv, h, WIDE), head(q, h), head(do, h)
        p = jnp.exp(nt(k, q_h) * SCALE + bias - lse_ref[h : h + 1, :])
        dp = nt(v, do_h)
        inner = jnp.sum(p * dp, axis=0, keepdims=True)
        ds = (p * (dp - inner)).astype(LOW)
        dqs.append(tn(k, ds) * SCALE)
        dks.append(nn(ds, q_h) * SCALE)
        dvs.append(nn(p.astype(LOW), do_h))
    dq = jnp.concatenate(dqs, axis=0).T
    return dq, jnp.concatenate(dks + dvs, axis=1)


def project(a0_ref, a1_ref, w_ref, out_ref):
    out_ref[...] = nn(stacked((a0_ref, a1_ref)), w_ref[...][:, WIDE:]).astype(LOW)


def self_forward(q_ref, kv0, kv1, kv2, kv3, bias_ref, w_ref, o_ref, lse_ref, pack_ref, out_ref):
    q = q_ref[...][:, :WIDE]
    o = attend_into(q, stacked((kv0, kv1, kv2, kv3)), bias_ref[...], o_ref, lse_ref)
    pack_ref[...] = packed(q, lse_ref[...])
    out_ref[...] = nt(o, w_ref[...][:, :WIDE]).astype(LOW)


def cross_forward(c0_ref, c1_ref, kv_ref, bias_ref, w_ref, q_ref, o_ref, lse_ref, out_ref):
    q = nn(stacked((c0_ref, c1_ref)), w_ref[...][:, :WIDE]).astype(LOW)
    q_ref[...] = q
    o = attend_into(q, kv_ref[...], bias_ref[...], o_ref, lse_ref)
    out_ref[...] = nt(o, w_ref[...][:, WIDE:]).astype(LOW)


def self_upstream(dy0_ref, dy1_ref, o_ref, w_ref, pack_ref, delta_ref):
    do = nn(stacked((dy0_ref, dy1_ref)), w_ref[...][:, :WIDE]).astype(LOW)
    product = (do.astype(FULL) * o_ref[...].astype(FULL)).T
    sums = [
        jnp.sum(product[h * HEAD : (h + 1) * HEAD], axis=0, keepdims=True)
        for h in range(HEADS_HERE)
    ]
    sums.append(jnp.zeros((8 - HEADS_HERE, do.shape[0]), FULL))
    delta = jnp.concatenate(sums, axis=0)
    delta_ref[...] = delta
    pack_ref[...] = packed(do, delta)


def self_query_grad(q_ref, kv0, kv1, kv2, kv3, bias_ref, lse_ref, pack_ref, delta_ref, dq_ref):
    q, kv, bias = q_ref[...][:, :WIDE], stacked((kv0, kv1, kv2, kv3)), bias_ref[...]
    do = pack_ref[...]
    rows = []
    for h in range(HEADS_HERE):
        k = head(kv, h)
        p = jnp.exp(nt(k, head(q, h)) * SCALE + bias - lse_ref[h : h + 1, :])
        dp = nt(head(kv, h, WIDE), head(do, h))
        ds = (p * (dp - delta_ref[h : h + 1, :])).astype(LOW)
        rows.append(tn(k, ds) * SCALE)
    dq_ref[...] = jnp.concatenate(rows, axis=0).T.astype(LOW)


def self_key_grad(order_ref, qkv_ref, bias_ref, pack_ref, *refs):
    do_refs, out_ref = refs[:-1], refs[-1]
    kv, bias = qkv_ref[...][:, WIDE:], bias_ref[...]
    count = qkv_ref.shape[0]
    packs = [
        pack_ref[pl.ds(pl.multiple_of(order_ref[d] * count, count), count), :] for d in range(8)
    ]
    lse = jnp.concatenate([stats_of(x) for x in packs], axis=1)
    delta = jnp.concatenate([stats_of(ref[...]) for ref in do_refs], axis=1)
    q, do = jnp.concatenate(packs, axis=0), stacked(do_refs)
    dks, dvs = [], []
    for h in range(HEADS_HERE):
        q_h, do_h = head(q, h), head(do, h)
        p = jnp.exp(nt(head(kv, h), q_h) * SCALE + bias - lse[h : h + 1])
        dp = nt(head(kv, h, WIDE), do_h)
        ds = (p * (dp - delta[h : h + 1])).astype(LOW)
        dks.append(nn(ds, q_h) * SCALE)
        dvs.append(nn(p.astype(LOW), do_h))
    out_ref[...] = jnp.concatenate(dks + dvs, axis=1).astype(LOW)


def cross_backward(
    dy0_ref, dy1_ref, q_ref, kv_ref, bias_ref, lse_ref, w_ref, dq_ref, dkv_ref, out_ref
):
    do = nn(stacked((dy0_ref, dy1_ref)), w_ref[...][:, WIDE:]).astype(LOW)
    dq, dkv = attend_back(do, q_ref[...], kv_ref[...], bias_ref[...], lse_ref)
    dq = dq.astype(LOW)
    dq_ref[...] = dq
    dkv_ref[...] = dkv.astype(LOW)
    out_ref[...] = nt(dq, w_ref[...][:, :WIDE]).astype(LOW)


NORMS = [(l, k) for l in range(2) for k in range(3)]


def norm_sums(*refs):
    out_ref = refs[-1]
    out_ref[...] = jnp.zeros(out_ref.shape, FULL)
    for at in range(len(NORMS)):
        upstream, n = refs[2 * at][...], refs[2 * at + 1][...]
        out_ref[at : at + 1, :] = jnp.sum(upstream * n, axis=0, keepdims=True)
        out_ref[6 + at : 7 + at, :] = jnp.sum(upstream, axis=0, keepdims=True)


def ff_forward(e0_ref, e1_ref, up_ref, down_ref, u_ref, hmid_ref, out_ref):
    u = nn(stacked((e0_ref, e1_ref)), up_ref[...])
    hmid = gelu(u).astype(LOW)
    u_ref[...] = u
    hmid_ref[...] = hmid
    out_ref[...] = nt(hmid, down_ref[...]).astype(LOW)


def ff_backward(dy0_ref, dy1_ref, u_ref, up_ref, down_ref, du_ref, out_ref):
    du = (nn(stacked((dy0_ref, dy1_ref)), down_ref[...]) * gelu_slope(u_ref[...])).astype(LOW)
    du_ref[...] = du
    out_ref[...] = nt(du, up_ref[...]).astype(LOW)


def weight_sums(groups, width):
    steps, args, specs, plan, columns = 4, [], [], [], 0
    rows = width // steps

    def put(x, spec):
        args.append(x)
        specs.append(spec)
        return len(args) - 1

    for group in groups:
        terms = []
        size = 0
        for kind, a, b in group:
            if kind == "tn":
                at = [put(x, lambda x: pl.BlockSpec((x.shape[0], rows), lambda i: (0, i))) for x in a]
                size += b.shape[1]
            else:
                cut, index = a[1]
                at = put(a[0], lambda x, c=cut, k=index: pl.BlockSpec((rows, c), lambda i: (i, k)))
                size = b.shape[0] if kind == "nt" else b.shape[1]
            terms.append((kind, at, put(b, None)))
        plan.append((columns, size, terms))
        columns += size

    def body(*refs):
        out_ref = refs[-1]
        for start, size, terms in plan:
            if terms[0][0] == "tn":
                parts = [tn(stacked([refs[k] for k in a]), refs[b][...]) for _, a, b in terms]
                value = parts[0] if len(parts) == 1 else jnp.concatenate(parts, axis=1)
            else:
                product = nt if terms[0][0] == "nt" else nn
                value = sum(product(refs[a][...], refs[b][...]) for _, a, b in terms)
            out_ref[:, start : start + size] = value.astype(LOW)

    return kernel_call(
        body,
        args,
        [((width, columns), LOW)],
        steps,
        specs,
        [pl.BlockSpec((rows, columns), lambda i: (i, 0))],
        room=24,
    )[0]


def halved(lower, out_refs, columns):
    sides = []
    for side in range(2):
        parts = []
        for x, split in columns:
            size = x.shape[1] // 2
            parts.append(x[:, side * size : (side + 1) * size] if split else x)
        sides.append(jnp.concatenate(parts, axis=1))
    mine, theirs = out_refs

    @pl.when(lower)
    def _():
        mine[...], theirs[...] = sides[0], sides[1]

    @pl.when(jnp.logical_not(lower))
    def _():
        mine[...], theirs[...] = sides[1], sides[0]


def first_columns(here_ref, in_ref, norm_ref, mine, theirs):
    columns = [(in_ref[0, k], True) for k in range(3)] + [(norm_ref[...], False)]
    halved(here_ref[0] == 0, (mine, theirs), columns)


def other_columns(here_ref, in_ref, out_ref, query_ref, text_ref, tout_ref, up_ref, down_ref, memory_ref, *outs):
    lower = here_ref[0] == 0
    spare = jnp.zeros((out_ref.shape[1], WIDE), LOW)

    def text(l):
        pair = [(text_ref[l, k], True) for k in range(2)]
        return pair, [(query_ref[l], True), (tout_ref[l], True)]

    pair, cross = text(0)
    both = [(memory_ref[m], False) for m in range(2)]
    halved(lower, outs[0:2], pair + both + cross + [(out_ref[0], True), (spare, False)])
    feed = [(up_ref[0], True), (down_ref[0], True)]
    pair, cross = text(1)
    own = [(out_ref[1], True)] + [(in_ref[0, k], True) for k in range(3)]
    halved(lower, outs[2:4], feed + pair + cross + own)
    halved(lower, outs[4:6], [(up_ref[1], True), (down_ref[1], True)])


def laid_out(parts, here, strip, ff):
    args = [here.reshape(1)] + [x for pair in parts for x in pair]

    def body(*refs):
        lower = refs[0][0] == 0
        kept = []
        for mine, theirs in ((1, 2), (3, 4), (5, 6)):
            a, b = refs[mine][...].astype(FULL), refs[theirs][...].astype(FULL)
            kept.append((jnp.where(lower, a, b), jnp.where(lower, b, a)))
        early, second, last = kept
        g_in, g_out, g_query, g_text, g_tout, g_up, g_down = refs[7:]

        def wide(pair, start, size):
            return jnp.concatenate([x[:, start : start + size] for x in pair], axis=1)

        for k in range(3):
            g_in[0, k] = wide(last, k * WIDE, WIDE)
            g_in[1, k] = wide(second, 2 * ff + k * WIDE, WIDE)
        g_out[0] = wide(last, 576, WIDE)
        g_out[1] = wide(second, 2 * ff + 576, WIDE)
        for l, pair in enumerate((second, early)):
            g_up[l] = wide(pair, 0, ff)
            g_down[l] = wide(pair, ff, ff)
        for l, (pair, start, next_start) in enumerate(
            ((second, 2304, 2688), (early, 2 * ff, 2 * ff + 384))
        ):
            for k in range(2):
                g_text[l, k] = wide(pair, start + k * WIDE, WIDE)
            g_query[l] = wide(pair, next_start, WIDE)
            g_tout[l] = wide(pair, next_start + WIDE, WIDE)

    outs = [
        ((2, 3, strip, 2 * WIDE), FULL),
        ((2, strip, 2 * WIDE), FULL),
        ((2, strip, 2 * WIDE), FULL),
        ((2, 2, strip, 2 * WIDE), FULL),
        ((2, strip, 2 * WIDE), FULL),
        ((2, strip, 2 * ff), FULL),
        ((2, strip, 2 * ff), FULL),
    ]
    specs = [lambda x: pl.BlockSpec(memory_space=pltpu.SMEM)] + [None] * 6
    return kernel_call(body, args, outs, 1, specs, room=24)


def gelu(z):
    return 0.5 * z * (1.0 + lax.erf(z * math.sqrt(0.5)))


def gelu_slope(z):
    half = 0.5 * (1.0 + lax.erf(z * math.sqrt(0.5)))
    return half + z * jnp.exp(-0.5 * z * z) * (1.0 / math.sqrt(2.0 * math.pi))


def width_mixed(x):
    lead = x.shape[:-1]
    parts = x.reshape(*lead, 8, 4, -1)
    return jnp.swapaxes(parts, -2, -3).reshape(*lead, -1)


def width_restored(x):
    lead = x.shape[:-1]
    parts = x.reshape(*lead, 4, 8, -1)
    return jnp.swapaxes(parts, -2, -3).reshape(*lead, -1)


def local(
    tokens,
    memory,
    clip_lengths,
    out_grad,
    norm_gain,
    norm_bias,
    self_in,
    self_out,
    text_query,
    text_kv,
    text_out,
    mlp_up,
    mlp_down,
):
    xh, core, zh = lax.axis_index("xh"), lax.axis_index("core"), lax.axis_index("zh")
    zl, xl, y = lax.axis_index("zl"), lax.axis_index("xl"), lax.axis_index("y")
    row = xh * 2 + core
    width = tokens.shape[2]
    strip = memory.shape[2]
    ff = mlp_up.shape[2] // 2

    def spread_pair(pair):
        mine, theirs = pair
        theirs = swapped(theirs, "xl")
        return jnp.where(
            xl == 0, jnp.concatenate([mine, theirs]), jnp.concatenate([theirs, mine])
        )

    def spread(both):
        return lax.all_gather(both, SPREAD, axis=0, tiled=True)

    def columns(body, args, sizes, layer):
        scalar = lambda x: pl.BlockSpec(memory_space=pltpu.SMEM)
        one = lambda x: pl.BlockSpec((1, *x.shape[1:]), lambda i: (layer, 0, 0, 0))
        outs = [((strip, size), LOW) for size in sizes for _ in range(2)]
        specs = [scalar, one] + [None] * (len(args) - 1)
        done = kernel_call(body, [xl.reshape(1), *args], outs, specs=specs)
        return [done[k : k + 2] for k in range(0, len(done), 2)]

    norms = jnp.concatenate([norm_gain.reshape(6, strip), norm_bias.reshape(6, strip)])
    norms = jnp.pad(norms.T, ((0, 0), (0, 52)))
    turned = [jnp.swapaxes(x, 1, 2) for x in (self_out, text_out, mlp_down, memory)]

    own_0 = columns(first_columns, [self_in, norms], [640], 0)[0]
    *own_0, tokens, out_grad = tied(*own_0, tokens, out_grad)
    own_0 = spread_pair(own_0)
    here = jnp.concatenate([tokens, out_grad], axis=2)
    here = lax.dynamic_slice_in_dim(here, row * 16, 16, axis=1)
    keep = jnp.where(zh == 0, here[0], here[1])
    send = jnp.where(zh == 0, here[1], here[0])
    own_rows = jnp.concatenate([keep, swapped(send, "zh")], axis=0)
    token_rows = width_mixed(own_rows[:, :width])
    grad_rows = width_mixed(own_rows[:, width:])

    own_0, token_rows, norm_free = tied(own_0, token_rows, turned[0])
    piece_0, token_all = tied(strips_of_all(own_0), jnp.concatenate(rows_of_all(token_rows)))
    pairs = columns(
        other_columns,
        [self_in, norm_free, text_query, text_kv, turned[1], mlp_up, turned[2], turned[3]],
        [1536, 2 * ff + 1536, 2 * ff],
        1,
    )
    piece_1 = spread(spread_pair(pairs[0]))
    piece_2 = spread(spread_pair(pairs[1]))
    w_in_0 = piece_0[:, :576]
    norm_rows = nt(jnp.eye(64, dtype=LOW)[:16], piece_0[:, 576:640])
    gains = [norm_rows[0:3], norm_rows[3:6]]
    shifts = [norm_rows[6:9], norm_rows[9:12]]
    unit_all, _ = unit(token_all.astype(FULL))
    first_normed = (unit_all * gains[0][0] + shifts[0][0]).astype(LOW)
    first_qkv = nn(first_normed, w_in_0).astype(LOW)
    first_normed = [first_normed]
    first_pair = keys_pair(first_qkv[:, WIDE:])
    w_in = [w_in_0, piece_2[:, 2496:]]
    attn, feed = [piece_1, piece_2], [piece_2]
    w_text = [piece_1[:, :384], piece_2[:, 1536:1920]]
    out_window = [window(384, 3), window(384, 6)]
    memory_all = piece_1[:, 384:768]
    up_window, down_window = window(ff, 0), window(ff, 1)
    cross_window = [window(384, 2), window(384, 5)]

    at = jnp.arange(2048, dtype=jnp.int32)
    d_y, d_z, d_c = at // 512, (at // 256) % 2, (at // 128) % 2
    d_x, d_s, inner = (at // 32) % 4, (at // 16) % 2, at % 16
    block = (zh ^ d_s) * 16 + (zl ^ d_z) * 8 + (xl ^ (d_x & 1)) * 4 + (y ^ d_y)
    key_at = block * 64 + ((xh ^ (d_x >> 1)) * 2 + (core ^ d_c)) * 16 + inner
    lengths = jnp.where(zh == 0, clip_lengths[0], clip_lengths[1])
    end_0 = lengths[0]
    end_1 = lengths[0] + lengths[1]
    key_clip = (key_at >= end_0).astype(jnp.int32) + (key_at >= end_1).astype(jnp.int32)
    frame_at, frame_clip = key_at[:256], key_clip[:256]
    allowed = (frame_clip[None, :] == key_clip[:, None]) & (key_at[:, None] <= frame_at[None, :])
    bias = jnp.where(allowed, 0.0, NEG_FILL).astype(FULL)
    back = (key_clip[None, :] == frame_clip[:, None]) & (frame_at[:, None] <= key_at[None, :])
    back_bias = jnp.where(back, 0.0, NEG_FILL).astype(FULL)
    d_block = jnp.arange(8, dtype=jnp.int32)
    keyed_order = (zl ^ (d_block % 2)) * 4 + (y ^ (d_block // 2))
    text_clip = jnp.arange(192, dtype=jnp.int32) // 64
    text_bias = jnp.where(frame_clip[None, :] == text_clip[:, None], 0.0, NEG_FILL).astype(FULL)
    frames = bias.shape[1]
    low_frames = ((frames, WIDE), LOW)
    lse_rows = ((8, frames), FULL)
    partial_rows = ((frames, width), LOW)
    pack_rows = ((frames, 256), LOW)
    packs = []

    residual = token_rows.astype(FULL)
    kept = []
    for l in range(2):
        n_0, r_0 = unit(residual)
        if l == 0:
            a, qkv, pair = first_normed, first_qkv, first_pair
        else:
            a = rows_of_all((n_0 * gains[l][0] + shifts[l][0]).astype(LOW))
            qkv = kernel_call(
                project,
                [*a, attn[l]],
                [((frames, 3 * WIDE), LOW)],
                specs=[None, None, window(768, 3)],
            )[0]
            pair = keys_pair(qkv[:, WIDE:])
        kv = keys_of_all(pair)
        o, lse, pack, part = kernel_call(
            self_forward,
            [qkv, *kv, bias, attn[l]],
            [low_frames, lse_rows, pack_rows, partial_rows],
            specs=[None] * 6 + [out_window[l]],
            room=24,
        )
        if l == 0:
            part, *rest = tied(part, *pairs[2])
            feed_strips = spread_pair(rest)
        else:
            part, feed_strips = tied(part, feed_strips)
            feed.append(spread(feed_strips))
        packs.append(pack)
        x1 = residual + sum_to_rows(part)
        n_1, r_1 = unit(x1)
        c = rows_of_all((n_1 * gains[l][1] + shifts[l][1]).astype(LOW))
        mkv = tn(memory_all, w_text[l]).astype(LOW)
        mkv = jnp.where(zh == 0, mkv[:192], mkv[192:])
        cq, co, clse, part = kernel_call(
            cross_forward,
            [*c, mkv, text_bias, attn[l]],
            [low_frames, low_frames, lse_rows, partial_rows],
            specs=[None] * 4 + [cross_window[l]],
        )
        x2 = x1 + sum_to_rows(part)
        n_2, r_2 = unit(x2)
        e = rows_of_all((n_2 * gains[l][2] + shifts[l][2]).astype(LOW))
        u, hmid, part = kernel_call(
            ff_forward,
            [*e, feed[l], feed[l]],
            [((frames, ff), FULL), ((frames, ff), LOW), partial_rows],
            specs=[None, None, up_window, down_window],
        )
        residual = x2 + sum_to_rows(part)
        kept.append((n_0, r_0, a, qkv, kv, o, lse, n_1, r_1, c, cq, mkv, co, clse, n_2, r_2, e, u, hmid))

    def frames_back(rows):
        pair = rows.reshape(2, 16, -1)
        other = swapped(pair[1], "zh")
        mbs = jnp.where(zh == 0, jnp.stack([pair[0], other]), jnp.stack([other, pair[0]]))
        both = jnp.stack([mbs, swapped(mbs, "core")])
        both = jnp.where(core == 0, both, both[::-1])
        four = jnp.stack([both, swapped(both, "xh")])
        four = jnp.where(xh == 0, four, four[::-1])
        return jnp.moveaxis(four.reshape(4, 2, 16, -1), 0, 1).reshape(2, 64, -1)

    packs = lax.all_gather(jnp.concatenate(packs, axis=1), KEYED, axis=0, tiled=True)
    grad = grad_rows.astype(FULL)
    norm_terms = {}

    def norm_step(l, k, grad, upstream, n, r):
        norm_terms[l, k] = (upstream, n)
        return grad + unit_back(upstream, n, r, gains[l][k])

    def summed(both):
        return lax.psum_scatter(both, SPREAD, scatter_dimension=0, tiled=True)

    memory_terms = []
    for l in (1, 0):
        n_0, r_0, a, qkv, kv, o, lse, n_1, r_1, c, cq, mkv, co, clse, n_2, r_2, e, u, hmid = kept[l]
        dy = rows_of_all(grad.astype(LOW))
        du, part = kernel_call(
            ff_backward,
            [*dy, u, feed[l], feed[l]],
            [((frames, ff), LOW), partial_rows],
            specs=[None] * 3 + [up_window, down_window],
        )
        de = sum_to_rows(part)
        groups = [[("tn", e, du)], [("tn", dy, hmid)]]
        grad = norm_step(l, 2, grad, de, n_2, r_2)

        dy = rows_of_all(grad.astype(LOW))
        dcq, dmkv, part = kernel_call(
            cross_backward,
            [*dy, cq, mkv, text_bias, clse, attn[l]],
            [low_frames, ((192, 2 * WIDE), LOW), partial_rows],
            specs=[None] * 6 + [cross_window[l]],
        )
        if l == 1:
            part, packs = tied(part, packs)
        dc = sum_to_rows(part)
        none = jnp.zeros_like(dmkv)
        dmkv = jnp.where(
            zh == 0, jnp.concatenate([dmkv, none]), jnp.concatenate([none, dmkv])
        )
        memory_terms.append(("nt", (attn[l], (384, 4 * l)), dmkv))
        cross = [[("nn", (piece_1, (384, 1)), dmkv)], [("tn", c, dcq), ("tn", dy, co)]]
        if l == 1:
            early = weight_sums(groups + cross, width)
            dc, early = tied(dc, early)
            early = summed(early)
        else:
            second = weight_sums(groups + late + cross + [memory_terms], width)
            dc, second, early = tied(dc, second, early)
            second = summed(second)
        grad = norm_step(l, 1, grad, dc, n_1, r_1)

        dy = rows_of_all(grad.astype(LOW))
        do_pack, delta = kernel_call(
            self_upstream,
            [*dy, o, attn[l]],
            [pack_rows, lse_rows],
            specs=[None] * 3 + [out_window[l]],
        )
        do_packs = keyed_of_all(do_pack)
        dq = kernel_call(
            self_query_grad,
            [qkv, *kv, bias, lse, do_pack, delta],
            [low_frames],
            room=32,
        )[0]
        dkv = kernel_call(
            self_key_grad,
            [keyed_order, qkv, back_bias, packs, *do_packs],
            [((frames, 2 * WIDE), LOW)],
            specs=[lambda x: pl.BlockSpec(memory_space=pltpu.SMEM), None, None, window(256, l)]
            + [None] * 8,
            room=32,
        )[0]
        dqkv = jnp.concatenate([dq, dkv], axis=1)
        da = nt(dqkv, w_in[l])
        late = [[("tn", a, dqkv), ("tn", dy, o)]]
        if l == 1:
            grad = norm_step(l, 0, grad, sum_to_rows(da), n_0, r_0)
        else:
            norm_terms[0, 0] = (da, unit_all)
            last = weight_sums(late, width)
            sums = kernel_call(
                norm_sums,
                [x for l, k in NORMS for x in norm_terms[l, k]],
                [((16, width), FULL)],
            )[0]
            extra = jnp.broadcast_to(sums[None], (8, *sums.shape))
            da = jnp.concatenate([da.reshape(8, -1, width), extra], axis=1)
            da = sum_to_rows(da.reshape(-1, width))
            da, last = tied(da, last)
            last = strip_of(sum_along(sum_along(strip_blocks(last), "y"), DEEP))
            norm_total = da[-16:].astype(LOW).reshape(16, 16, -1)
            norm_total = lax.all_to_all(jnp.swapaxes(norm_total, 0, 1), SPREAD, 0, 0, tiled=True)
            norm_total = jnp.sum(norm_total.astype(FULL), axis=0)
            grad = grad + unit_back(da[:-16], n_0, r_0, gains[0][0])
    ends = jnp.concatenate(
        [width_restored(residual.astype(LOW)), width_restored(grad.astype(LOW))], axis=1
    )
    ends = frames_back(ends)
    output, input_grad = ends[:, :, :width], ends[:, :, width:].astype(FULL)

    def strips(block):
        mine = lax.dynamic_slice_in_dim(block, xl * strip, strip, axis=0)
        theirs = lax.dynamic_slice_in_dim(block, (1 - xl) * strip, strip, axis=0)
        return mine, swapped(theirs, "xl")

    def both(pair, start, size):
        return sum(x[:, start : start + size].astype(FULL) for x in pair)

    def everywhere(x):
        x = x + swapped(x.astype(LOW), "core").astype(FULL)
        return x + swapped(x.astype(LOW), "xh").astype(FULL)

    early, second, last = [strips(b) for b in (early, second, last)]
    laid = laid_out((early, second, last), xl, strip, ff)
    self_in_grad, self_out_grad, text_query_grad, text_kv_grad = laid[:4]
    text_out_grad, mlp_up_grad, mlp_down_grad = laid[4:]
    self_out_grad, text_out_grad, mlp_down_grad = [
        jnp.swapaxes(x, 1, 2) for x in (self_out_grad, text_out_grad, mlp_down_grad)
    ]
    memory_grad = everywhere(both(second, 3072, 384)).reshape(strip, 2, 192)
    memory_grad = jnp.transpose(memory_grad, (1, 2, 0))
    norm_grads = lax.dynamic_slice_in_dim(norm_total, xl * strip, strip, axis=1)
    gain_grad = norm_grads[:6].reshape(2, 3, strip)
    shift_grad = norm_grads[6:12].reshape(2, 3, strip)
    return (
        output,
        input_grad,
        memory_grad,
        gain_grad,
        shift_grad[:, 0:2],
        shift_grad[:, 2],
        self_in_grad,
        self_out_grad,
        text_query_grad,
        text_kv_grad,
        text_out_grad,
        mlp_up_grad,
        mlp_down_grad,
    )


def solution(mesh):
    fine = Mesh(mesh.devices.reshape(FINE_SIZES), FINE)
    frames = P(None, COL, None)
    strips = P(None, None, COL)
    return jax.shard_map(
        local,
        mesh=fine,
        in_specs=(
            frames,
            strips,
            P(),
            frames,
            strips,
            strips,
            P(None, None, COL, ROW),
            P(None, ROW, COL),
            P(None, COL, ROW),
            P(None, None, COL, ROW),
            P(None, ROW, COL),
            P(None, COL, ROW),
            P(None, ROW, COL),
        ),
        out_specs=(
            frames,
            frames,
            strips,
            strips,
            strips,
            P(None, COL),
            P(None, None, COL, ROW),
            P(None, ROW, COL),
            P(None, COL, ROW),
            P(None, None, COL, ROW),
            P(None, ROW, COL),
            P(None, COL, ROW),
            P(None, ROW, COL),
        ),
        check_vma=False,
    )
```

time: 665 us -> 657 us (0.988)
  local copies, waits for them, and re-layouts: 47.1 us -> 81.3 us
  starting transfers between devices: 246 us -> 213 us
  other arithmetic: 28.5 us -> 42.1 us
  Pallas kernels: 82.5 us -> 69.2 us
    unnamed x273 -> x367, local copies, waits for them, and re-layouts: 18.4 us -> 57.2 us
    ppermute x41 -> x39, starting transfers between devices: 101 us -> 81.2 us  [swapped(): return lax.ppermute(x, axis, SWAP)]
    all_to_all x1 -> x0, waiting for transfers between devices: 15.7 us -> none  [spread_now(): lax.all_to_all(sent, SPREAD, 0, 0, tiled=True).reshape(-1, own.shape[1])]
    pallas_call x16 -> x24, Pallas kernels: 82.5 us -> 69.2 us  [kernel_call(): pl.pallas_call(body, grid=(steps,), in_specs=placed, out_specs=out_specs...]
    convert_element_type x7 -> x15, other arithmetic: 1.36 us -> 13.1 us  [the longest x5 4.68 us: local(): dy = rows_of_all(grad.astype(LOW))]
    ppermute x34 -> x38, waiting for transfers between devices: 99.5 us -> 89.8 us  [the longest x6 29.3 us: keys_of_all(): return [pair] + [lax.ppermute(pair, 'y', flipped(4, d)) for d in (1, 2, 3)]]
    ppermute x41 -> x39, waiting for transfers between devices: 44.8 us -> 53.8 us  [swapped(): return lax.ppermute(x, axis, SWAP)]
    all_gather x3 -> x4, waiting for transfers between devices: 0.04 us -> 8.42 us  [the longest x3 8.42 us: spread(): return lax.all_gather(both, SPREAD, axis=0, tiled=True)]
  transfers between devices with their start and end apart: 154 -> 156, of which waited for: 102 -> 95; matrix products, arithmetic and copies ran while one was open for 10% -> 10% of each run, Pallas kernels for 11% -> 9%
where the time goes in v3:
time: 657 us; the launch traced here: 647 us
  waiting for transfers between devices  216 us (33%)
  starting transfers between devices  213 us (32%)
  local copies, waits for them, and re-layouts  81.3 us (12%)
  Pallas kernels  69.2 us (11%)
  other arithmetic  42.1 us (6%)
  between operations  18.7 us (3%)
    ppermute x39, starting transfers between devices, swapped(): return lax.ppermute(x, axis, SWAP)  81.2 us
    pallas_call x24, Pallas kernels, kernel_call(): pl.pallas_call(body, grid=(steps,), in_specs=placed, out_specs=out_specs...  69.2 us
    unnamed x367, local copies, waits for them, and re-layouts  57.2 us
    ppermute x39, waiting for transfers between devices, swapped(): return lax.ppermute(x, axis, SWAP)  53.8 us
    ppermute x36, starting transfers between devices, sum_to_rows(): total = total + lax.ppermute(low[d], CHIPS, flipped(4, d)).astype(FULL)  41.1 us
    ppermute x36, starting transfers between devices, rows_of_all(): lax.ppermute(rows, CHIPS, flipped(4, d))  39.8 us
    ppermute x36, waiting for transfers between devices, rows_of_all(): lax.ppermute(rows, CHIPS, flipped(4, d))  33.1 us
    ppermute x36, waiting for transfers between devices, sum_to_rows(): total = total + lax.ppermute(low[d], CHIPS, flipped(4, d)).astype(FULL)  31.1 us
  transfers between devices with their start and end apart: 156, of which 95 were waited for; matrix products, arithmetic and copies ran while one was open for 10% of the time, Pallas kernels for 9%

profile of v3, /device:TPU:1, one launch (start us, length us, event | category | flops | bytes accessed | tf_op | source)
XLA Modules:
  0.0 647.0 jit_solution(5049731811934624173)
XLA Ops:
  13.1 3.7 collective-permute-start.1
  20.8 3.7 collective-permute-done.22
  25.7 5.3 collective-permute-done.39
  34.0 3.2 collective-permute-start.3
  38.5 2.7 collective-permute-start.9
  44.8 2.4 collective-permute-start.16
  48.3 2.7 collective-permute-start.13
  52.9 2.5 collective-permute-start.6
  55.5 2.8 collective-permute-done.11
  58.7 9.5 %collective-permute-start.17 = (bf16[128,1536]{1,0:T(8,128)(2,1)S(1)}, bf16[128,1536]{1,0:T(8,128)(2,1)S(1)}, u32[]{:S(2)}, u32[]{:S(2)}) collective-permute-start(bf16[128,1536]{1,0:T(8,128)(2,1)S(1)} %pad_maximum_fusion.3), channel_id=1, source_target_pairs={{0,32},{32,0},{1,33},{33,1},{2,34},{34,2},{3,35},{35,3},{4,36},{36... | collective-permute-start | bytes 1179656 | tf_op jit(solution)/shard_map/ppermute | solution.py:35
  74.6 8.2 %collective-permute-done.18 = bf16[256,384]{1,0:T(8,128)(2,1)S(1)} collective-permute-done((bf16[256,384]{1,0:T(8,128)(2,1)S(1)}, bf16[256,384]{1,0:T(8,128)(2,1)S(1)}, u32[]{:S(2)}, u32[]{:S(2)}) %collective-permute-start.18) | collective-permute-done | bytes 196640 | tf_op jit(solution)/shard_map/ppermute | solution.py:35
  82.9 3.0 collective-permute-start.20
  87.0 18.1 %collective-permute-done.21.kv3 = bf16[512,384]{1,0:T(8,128)(2,1)S(1)} collective-permute-done((bf16[512,384]{1,0:T(8,128)(2,1)S(1)}, bf16[512,384]{1,0:T(8,128)(2,1)S(1)}, u32[]{:S(2)}, u32[]{:S(2)}) %collective-permute-start.21) | collective-permute-done | bytes 393248 | tf_op jit(solution)/shard_map/ppermute | solution.py:60
  106.7 2.7 copy-done.4
  111.4 5.3 shard_map.230
  135.9 3.3 collective-permute-start.30
  160.2 3.3 collective-permute-start.38
  165.7 8.4 %all-gather.7.cloned.1.call-done.up_ref.down_ref.w_ref.refs_20_ = bf16[1536,3072]{1,0:T(8,128)(2,1)} async-done(((bf16[96,3072]{1,0:T(8,128)(2,1)}), bf16[1536,3072]{1,0:T(8,128)(2,1)}) %all-gather.7.cloned.1.call-update) | async-done | bytes 9437200 | tf_op jit(solution)/shard_map/all_gather | solution.py:516
  174.1 3.7 copy-done
  199.8 3.4 collective-permute-start.47
  207.0 5.1 collective-permute-done.48
  212.9 2.5 collective-permute-start.51
  216.7 3.9 collective-permute-done.52
  221.4 11.0 %collective-permute-done.51.kv3 = bf16[512,384]{1,0:T(8,128)(2,1)} collective-permute-done((bf16[512,384]{1,0:T(8,128)(2,1)}, bf16[512,384]{1,0:T(8,128)(2,1)}, u32[]{:S(2)}, u32[]{:S(2)}) %collective-permute-start.51) | collective-permute-done | bytes 393248 | tf_op jit(solution)/shard_map/ppermute | solution.py:60
  232.6 3.7 copy-done.1
  236.3 6.7 %shard_map.234 = (bf16[256,192]{1,0:T(8,128)(2,1)S(1)}, f32[8,256]{1,0:T(8,128)S(1)}, bf16[256,256]{1,0:T(8,128)(2,1)S(1)}, bf16[256,1536]{1,0:T(8,128)(2,1)S(1)}) custom-call(bf16[256,576]{1,0:T(8,128)(2,1)S(1)} %shard_map.233.q_ref.qkv_ref, bf16[512,384]{1,0:T(8,128)(2,1)} %pad_maximum_fusion.8.kv0, bf16[512,384]{1,0:T(8,128)(2,1)} %collective-permute-done.49.kv1, ...), custom_call_target="tpu_custom_call" | custom-call | tf_op jit(solution)/shard_map/pallas_call | solution.py:168
  246.4 2.4 collective-permute-start.53
  265.5 3.3 collective-permute-start.60
  268.8 2.4 convolution_convert_fusion
  271.3 3.7 copy-done.2
  305.6 4.3 collective-permute-start.68
  313.9 3.0 shard_map.236
  320.9 3.0 shard_map.237
  341.2 3.2 collective-permute-start.84
  362.4 4.8 shard_map.239
  367.3 2.9 copy-done.9
  380.0 2.5 collective-permute-done.90
  382.5 2.8 collective-permute-start.92
  386.6 3.8 copy-done.3
  397.8 4.9 collective-permute-done.99.refs_7_
  402.8 8.1 %collective-permute-done.98.refs_6_ = bf16[256,256]{1,0:T(8,128)(2,1)S(1)} collective-permute-done((bf16[256,256]{1,0:T(8,128)(2,1)S(1)}, bf16[256,256]{1,0:T(8,128)(2,1)S(1)}, u32[]{:S(2)}, u32[]{:S(2)}) %collective-permute-start.98) | collective-permute-done | bytes 131104 | tf_op jit(solution)/shard_map/ppermute | solution.py:69
  412.8 4.7 shard_map.241
  418.3 4.9 shard_map.242
  441.6 4.1 collective-permute-start.107
  465.5 3.7 collective-permute-start.115
  479.1 8.1 %shard_map.245 = bf16[1536,3456]{1,0:T(8,128)(2,1)} custom-call(bf16[128,1536]{1,0:T(8,128)(2,1)S(1)} %copy-done.26, bf16[128,1536]{1,0:T(8,128)(2,1)S(1)} %copy-done.65, bf16[256,768]{1,0:T(8,128)(2,1)S(1)} %get-tuple-element.139.refs_2_, bf16[128,1536]{1,0:T(8,128)(2,1)S(1)} %pad_maximum_fusion.13.dy0_ref.refs_3_, ...), custom_call_target="tpu_custom_call" | custom-call | tf_op jit(solution)/shard_map/pallas_call | solution.py:168
  498.5 2.5 collective-permute-start.123
  502.5 2.4 copy-done.6
  506.7 2.8 collective-permute-start.130
  517.7 10.9 %collective-permute-done.129.refs_6_ = bf16[256,256]{1,0:T(8,128)(2,1)S(1)} collective-permute-done((bf16[256,256]{1,0:T(8,128)(2,1)S(1)}, bf16[256,256]{1,0:T(8,128)(2,1)S(1)}, u32[]{:S(2)}, u32[]{:S(2)}) %collective-permute-start.129) | collective-permute-done | bytes 131104 | tf_op jit(solution)/shard_map/ppermute | solution.py:69
  528.7 2.6 shard_map.247
  536.3 4.9 shard_map.248
  555.9 3.4 shard_map.250
  561.5 3.8 all-to-all-start
  566.5 2.9 collective-permute-start.135
  569.4 2.7 constant_dynamic-slice_fusion.5
  573.3 2.4 collective-permute-start.144
  577.8 4.0 collective-permute-start.136
  584.8 12.1 %collective-permute-done.142 = bf16[1,4,96,768]{3,2,1,0:T(8,128)(2,1)} collective-permute-done((bf16[1,4,96,768]{3,2,1,0:T(8,128)(2,1)}, bf16[1,4,96,768]{3,2,1,0:T(8,128)(2,1)}, u32[]{:S(2)}, u32[]{:S(2)}) %collective-permute-start.142) | collective-permute-done | bytes 589856 | tf_op jit(solution)/shard_map/ppermute | solution.py:112
  596.9 14.2 %collective-permute-done.144 = bf16[1,4,96,768]{3,2,1,0:T(8,128)(2,1)} collective-permute-done((bf16[1,4,96,768]{3,2,1,0:T(8,128)(2,1)}, bf16[1,4,96,768]{3,2,1,0:T(8,128)(2,1)}, u32[]{:S(2)}, u32[]{:S(2)}) %collective-permute-start.144) | collective-permute-done | bytes 589856 | tf_op jit(solution)/shard_map/ppermute | solution.py:112
  611.1 2.9 fusion.126
  624.3 2.4 collective-permute-done.138.refs_4_
  627.5 3.5 collective-permute-start.139
  633.2 2.6 collective-permute-start.140
  (866 shorter events, 333.7 us)
Async XLA Ops:
  7.2 99.5 %all-gather.5.cloned.1.call-start = ((), (), s32[]{:S(2)}) async-start(), calls=%async_computation.3 | async-start | bytes 5013504 | tf_op jit(solution)/shard_map/all_gather | solution.py:516
  9.8 6.9 %collective-permute-start = (bf16[48,640]{1,0:T(8,128)(2,1)S(1)}, bf16[48,640]{1,0:T(8,128)(2,1)S(1)}, u32[]{:S(2)}, u32[]{:S(2)}) collective-permute-start(bf16[48,640]{1,0:T(8,128)(2,1)S(1)} %get-tuple-element.90), channel_id=1, source_target_pairs={{0,4},{4,0},{1,5},{5,1},{2,6},{6,2},{3,7},{7,3},{8,12},{12,8},{9,1... | collective-permute-start | bytes 184328 | tf_op jit(solution)/shard_map/ppermute | solution.py:35
  25.3 148.8 %all-gather.7.cloned.1.call-start = ((), (), s32[]{:S(2)}) async-start(), calls=%async_computation.4 | async-start | bytes 10027008 | tf_op jit(solution)/shard_map/all_gather | solution.py:516
  32.0 279.6 %all-gather.9.cloned.1.call-start = ((), (), s32[]{:S(2)}) async-start(), calls=%async_computation.5 | async-start | bytes 5013504 | tf_op jit(solution)/shard_map/all_gather | solution.py:516
  34.0 14.3 %collective-permute-start.3 = (bf16[1,1,48,640]{3,2,1,0:T(8,128)(2,1)S(1)}, bf16[1,1,48,640]{3,2,1,0:T(8,128)(2,1)S(1)}, u32[]{:S(2)}, u32[]{:S(2)}) collective-permute-start(bf16[1,1,48,640]{3,2,1,0:T(8,128)(2,1)S(1)} %get-tuple-element.349), channel_id=1, source_target_pairs={{0,24},{8,16},{16,8},{24,0},{1,25},{9,17},{17,9},{25,1},{2,26},{10... | collective-permute-start | bytes 184328 | tf_op jit(solution)/shard_map/ppermute | solution.py:86
  37.2 13.8 %collective-permute-start.4 = (bf16[1,1,48,640]{3,2,1,0:T(8,128)(2,1)S(1)}, bf16[1,1,48,640]{3,2,1,0:T(8,128)(2,1)S(1)}, u32[]{:S(2)}, u32[]{:S(2)}) collective-permute-start(bf16[1,1,48,640]{3,2,1,0:T(8,128)(2,1)S(1)} %get-tuple-element.349), channel_id=1, source_target_pairs={{0,16},{8,24},{16,0},{24,8},{1,17},{9,25},{17,1},{25,9},{2,18},{10... | collective-permute-start | bytes 184328 | tf_op jit(solution)/shard_map/ppermute | solution.py:86
  38.5 8.8 %collective-permute-start.9 = (bf16[1,1,48,640]{3,2,0,1:T(8,128)(2,1)S(1)}, bf16[1,1,48,640]{3,2,0,1:T(8,128)(2,1)S(1)}, u32[]{:S(2)}, u32[]{:S(2)}) collective-permute-start(bf16[1,1,48,640]{3,2,0,1:T(8,128)(2,1)S(1)} %get-tuple-element.350), channel_id=1, source_target_pairs={{0,3},{1,2},{2,1},{3,0},{4,7},{5,6},{6,5},{7,4},{8,11},{9,10},{10,... | collective-permute-start | bytes 184328 | tf_op jit(solution)/shard_map/ppermute | solution.py:86
  44.8 8.0 %collective-permute-start.16 = (bf16[32,1536]{1,0:T(8,128)(2,1)S(1)}, bf16[32,1536]{1,0:T(8,128)(2,1)S(1)}, u32[]{:S(2)}, u32[]{:S(2)}) collective-permute-start(bf16[32,1536]{1,0:T(8,128)(2,1)S(1)} %reshape.664), channel_id=1, source_target_pairs={{0,68},{4,64},{64,4},{68,0},{1,69},{5,65},{65,5},{69,1},{2,70},{6,... | collective-permute-start | bytes 294920 | tf_op jit(solution)/shard_map/ppermute | solution.py:39
  48.3 19.9 %collective-permute-start.13 = (bf16[4,1,48,640]{3,2,0,1:T(8,128)(2,1)S(1)}, bf16[4,1,48,640]{3,2,0,1:T(8,128)(2,1)S(1)}, u32[]{:S(2)}, u32[]{:S(2)}) collective-permute-start(bf16[4,1,48,640]{3,2,0,1:T(8,128)(2,1)S(1)} %constant_dynamic-update-slice_fusion.11), channel_id=1, source_target_pairs={{0,16},{8,24},{16,0},{24,8},{1,17},{9,25},{17,1},{25,9},{2,18},{10... | collective-permute-start | bytes 737288 | tf_op jit(solution)/shard_map/ppermute | solution.py:86
  51.1 7.7 %collective-permute-start.12 = (bf16[4,1,48,640]{3,2,0,1:T(8,128)(2,1)S(1)}, bf16[4,1,48,640]{3,2,0,1:T(8,128)(2,1)S(1)}, u32[]{:S(2)}, u32[]{:S(2)}) collective-permute-start(bf16[4,1,48,640]{3,2,0,1:T(8,128)(2,1)S(1)} %constant_dynamic-update-slice_fusion.11), channel_id=1, source_target_pairs={{0,24},{8,16},{16,8},{24,0},{1,25},{9,17},{17,9},{25,1},{2,26},{10... | collective-permute-start | bytes 737288 | tf_op jit(solution)/shard_map/ppermute | solution.py:86
  52.8 15.6 %collective-permute-start.7 = (bf16[1,4,48,640]{3,2,1,0:T(8,128)(2,1)S(1)}, bf16[1,4,48,640]{3,2,1,0:T(8,128)(2,1)S(1)}, u32[]{:S(2)}, u32[]{:S(2)}) collective-permute-start(bf16[1,4,48,640]{3,2,1,0:T(8,128)(2,1)S(1)} %constant_dynamic-update-slice_fusion.15), channel_id=1, source_target_pairs={{0,2},{1,3},{2,0},{3,1},{4,6},{5,7},{6,4},{7,5},{8,10},{9,11},{10,... | collective-permute-start | bytes 737288 | tf_op jit(solution)/shard_map/ppermute | solution.py:86
  52.9 15.4 %collective-permute-start.6 = (bf16[1,4,48,640]{3,2,1,0:T(8,128)(2,1)S(1)}, bf16[1,4,48,640]{3,2,1,0:T(8,128)(2,1)S(1)}, u32[]{:S(2)}, u32[]{:S(2)}) collective-permute-start(bf16[1,4,48,640]{3,2,1,0:T(8,128)(2,1)S(1)} %constant_dynamic-update-slice_fusion.15), channel_id=1, source_target_pairs={{0,3},{1,2},{2,1},{3,0},{4,7},{5,6},{6,5},{7,4},{8,11},{9,10},{10,... | collective-permute-start | bytes 737288 | tf_op jit(solution)/shard_map/ppermute | solution.py:86
  58.4 9.9 %collective-permute-start.5 = (bf16[1,4,48,640]{3,2,1,0:T(8,128)(2,1)S(1)}, bf16[1,4,48,640]{3,2,1,0:T(8,128)(2,1)S(1)}, u32[]{:S(2)}, u32[]{:S(2)}) collective-permute-start(bf16[1,4,48,640]{3,2,1,0:T(8,128)(2,1)S(1)} %constant_dynamic-update-slice_fusion.15), channel_id=1, source_target_pairs={{0,1},{1,0},{2,3},{3,2},{4,5},{5,4},{6,7},{7,6},{8,9},{9,8},{10,11... | collective-permute-start | bytes 737288 | tf_op jit(solution)/shard_map/ppermute | solution.py:86
  58.7 10.8 %collective-permute-start.17 = (bf16[128,1536]{1,0:T(8,128)(2,1)S(1)}, bf16[128,1536]{1,0:T(8,128)(2,1)S(1)}, u32[]{:S(2)}, u32[]{:S(2)}) collective-permute-start(bf16[128,1536]{1,0:T(8,128)(2,1)S(1)} %pad_maximum_fusion.3), channel_id=1, source_target_pairs={{0,32},{32,0},{1,33},{33,1},{2,34},{34,2},{3,35},{35,3},{4,36},{36... | collective-permute-start | bytes 1179656 | tf_op jit(solution)/shard_map/ppermute | solution.py:35
  73.7 9.1 %collective-permute-start.18 = (bf16[256,384]{1,0:T(8,128)(2,1)S(1)}, bf16[256,384]{1,0:T(8,128)(2,1)S(1)}, u32[]{:S(2)}, u32[]{:S(2)}) collective-permute-start(bf16[256,384]{1,0:T(8,128)(2,1)S(1)} %slice.552), channel_id=1, source_target_pairs={{0,8},{8,0},{1,9},{9,1},{2,10},{10,2},{3,11},{11,3},{4,12},{12,4},... | collective-permute-start | bytes 589832 | tf_op jit(solution)/shard_map/ppermute | solution.py:35
  82.8 22.2 %collective-permute-start.21 = (bf16[512,384]{1,0:T(8,128)(2,1)S(1)}, bf16[512,384]{1,0:T(8,128)(2,1)S(1)}, u32[]{:S(2)}, u32[]{:S(2)}) collective-permute-start(bf16[512,384]{1,0:T(8,128)(2,1)S(1)} %pad_maximum_fusion.4.kv0), channel_id=1, source_target_pairs={{0,3},{1,2},{2,1},{3,0},{4,7},{5,6},{6,5},{7,4},{8,11},{9,10},{10,... | collective-permute-start | bytes 1179656 | tf_op jit(solution)/shard_map/ppermute | solution.py:60
  82.9 22.1 %collective-permute-start.20 = (bf16[512,384]{1,0:T(8,128)(2,1)S(1)}, bf16[512,384]{1,0:T(8,128)(2,1)S(1)}, u32[]{:S(2)}, u32[]{:S(2)}) collective-permute-start(bf16[512,384]{1,0:T(8,128)(2,1)S(1)} %pad_maximum_fusion.4.kv0), channel_id=1, source_target_pairs={{0,2},{1,3},{2,0},{3,1},{4,6},{5,7},{6,4},{7,5},{8,10},{9,11},{10,... | collective-permute-start | bytes 1179656 | tf_op jit(solution)/shard_map/ppermute | solution.py:60
  85.9 20.0 %collective-permute-start.19 = (bf16[512,384]{1,0:T(8,128)(2,1)S(1)}, bf16[512,384]{1,0:T(8,128)(2,1)S(1)}, u32[]{:S(2)}, u32[]{:S(2)}) collective-permute-start(bf16[512,384]{1,0:T(8,128)(2,1)S(1)} %pad_maximum_fusion.4.kv0), channel_id=1, source_target_pairs={{0,1},{1,0},{2,3},{3,2},{4,5},{5,4},{6,7},{7,6},{8,9},{9,8},{10,11... | collective-permute-start | bytes 1179656 | tf_op jit(solution)/shard_map/ppermute | solution.py:60
  212.9 19.6 %collective-permute-start.51 = (bf16[512,384]{1,0:T(8,128)(2,1)}, bf16[512,384]{1,0:T(8,128)(2,1)}, u32[]{:S(2)}, u32[]{:S(2)}) collective-permute-start(bf16[512,384]{1,0:T(8,128)(2,1)} %pad_maximum_fusion.8.kv0), channel_id=1, source_target_pairs={{0,3},{1,2},{2,1},{3,0},{4,7},{5,6},{6,5},{7,4},{8,11},{9,10},{10,... | collective-permute-start | bytes 1179656 | tf_op jit(solution)/shard_map/ppermute | solution.py:60
  215.4 17.1 %collective-permute-start.50 = (bf16[512,384]{1,0:T(8,128)(2,1)}, bf16[512,384]{1,0:T(8,128)(2,1)}, u32[]{:S(2)}, u32[]{:S(2)}) collective-permute-start(bf16[512,384]{1,0:T(8,128)(2,1)} %pad_maximum_fusion.8.kv0), channel_id=1, source_target_pairs={{0,2},{1,3},{2,0},{3,1},{4,6},{5,7},{6,4},{7,5},{8,10},{9,11},{10,... | collective-permute-start | bytes 1179656 | tf_op jit(solution)/shard_map/ppermute | solution.py:60
  215.8 16.8 %collective-permute-start.49 = (bf16[512,384]{1,0:T(8,128)(2,1)}, bf16[512,384]{1,0:T(8,128)(2,1)}, u32[]{:S(2)}, u32[]{:S(2)}) collective-permute-start(bf16[512,384]{1,0:T(8,128)(2,1)} %pad_maximum_fusion.8.kv0), channel_id=1, source_target_pairs={{0,1},{1,0},{2,3},{3,2},{4,5},{5,4},{6,7},{7,6},{8,9},{9,8},{10,11... | collective-permute-start | bytes 1179656 | tf_op jit(solution)/shard_map/ppermute | solution.py:60
  245.2 106.4 %all-gather.11.cloned.1.call-start = ((), (), s32[]{:S(2)}) async-start(), calls=%async_computation.6 | async-start | bytes 2359296 | tf_op jit(solution)/shard_map/all_gather | solution.py:656
  278.1 10.5 %collective-permute-start.61 = (bf16[4,32,1536]{2,1,0:T(8,128)(2,1)}, bf16[4,32,1536]{2,1,0:T(8,128)(2,1)}, u32[]{:S(2)}, u32[]{:S(2)}) collective-permute-start(bf16[4,32,1536]{2,1,0:T(8,128)(2,1)} %bitcast.54), channel_id=1, source_target_pairs={{0,32},{32,0},{1,33},{33,1},{2,34},{34,2},{3,35},{35,3},{4,36},{36... | collective-permute-start | bytes 1179656 | tf_op jit(solution)/shard_map/ppermute | solution.py:35
  283.7 26.2 %collective-permute-start.75 = (bf16[32,1536]{1,0:T(8,128)(2,1)}, bf16[32,1536]{1,0:T(8,128)(2,1)S(1)}, u32[]{:S(2)}, u32[]{:S(2)}) collective-permute-start(bf16[32,1536]{1,0:T(8,128)(2,1)} %reshape.670), channel_id=1, source_target_pairs={{0,68},{4,64},{64,4},{68,0},{1,69},{5,65},{65,5},{69,1},{2,70},{6,... | collective-permute-start | bytes 294920 | tf_op jit(solution)/shard_map/ppermute | solution.py:39
  285.1 16.7 %collective-permute-start.74 = (bf16[32,1536]{1,0:T(8,128)(2,1)}, bf16[32,1536]{1,0:T(8,128)(2,1)S(1)}, u32[]{:S(2)}, u32[]{:S(2)}) collective-permute-start(bf16[32,1536]{1,0:T(8,128)(2,1)} %reshape.670), channel_id=1, source_target_pairs={{0,64},{4,68},{64,0},{68,4},{1,65},{5,69},{65,1},{69,5},{2,66},{6,... | collective-permute-start | bytes 294920 | tf_op jit(solution)/shard_map/ppermute | solution.py:39
  310.5 8.1 %collective-permute-start.76 = (bf16[128,1536]{1,0:T(8,128)(2,1)}, bf16[128,1536]{1,0:T(8,128)(2,1)}, u32[]{:S(2)}, u32[]{:S(2)}) collective-permute-start(bf16[128,1536]{1,0:T(8,128)(2,1)} %constant_dynamic-update-slice_fusion.5.dy0_ref.refs_3_), channel_id=1, source_target_pairs={{0,32},{32,0},{1,33},{33,1},{2,34},{34,2},{3,35},{35,3},{4,36},{36... | collective-permute-start | bytes 1179656 | tf_op jit(solution)/shard_map/ppermute | solution.py:35
  311.3 177.6 %reduce-scatter.3.cloned.1.call-start = ((), (), s32[]{:S(2)}) async-start(), calls=%async_computation.7 | async-start | bytes 7520256 | tf_op jit(solution)/shard_map/reduce_scatter | solution.py:665
  356.4 14.4 %collective-permute-start.86 = (bf16[32,1536]{1,0:T(8,128)(2,1)}, bf16[32,1536]{1,0:T(8,128)(2,1)}, u32[]{:S(2)}, u32[]{:S(2)}) collective-permute-start(bf16[32,1536]{1,0:T(8,128)(2,1)} %get-tuple-element.316), channel_id=1, source_target_pairs={{0,4},{4,0},{64,68},{68,64},{1,5},{5,1},{65,69},{69,65},{2,6},{6,2... | collective-permute-start | bytes 294920 | tf_op jit(solution)/shard_map/ppermute | solution.py:51
  357.4 13.5 %collective-permute-start.88 = (bf16[32,1536]{1,0:T(8,128)(2,1)}, bf16[32,1536]{1,0:T(8,128)(2,1)}, u32[]{:S(2)}, u32[]{:S(2)}) collective-permute-start(bf16[32,1536]{1,0:T(8,128)(2,1)} %get-tuple-element.317), channel_id=1, source_target_pairs={{0,68},{4,64},{64,4},{68,0},{1,69},{5,65},{65,5},{69,1},{2,70},{6,... | collective-permute-start | bytes 294920 | tf_op jit(solution)/shard_map/ppermute | solution.py:51
  359.6 11.3 %collective-permute-start.87 = (bf16[32,1536]{1,0:T(8,128)(2,1)}, bf16[32,1536]{1,0:T(8,128)(2,1)}, u32[]{:S(2)}, u32[]{:S(2)}) collective-permute-start(bf16[32,1536]{1,0:T(8,128)(2,1)} %get-tuple-element.318), channel_id=1, source_target_pairs={{0,64},{4,68},{64,0},{68,4},{1,65},{5,69},{65,1},{69,5},{2,66},{6,... | collective-permute-start | bytes 294920 | tf_op jit(solution)/shard_map/ppermute | solution.py:51
  372.7 246.0 %reduce-scatter.5.cloned.1.call-start = ((), (), s32[]{:S(2)}) async-start(), calls=%async_computation.8 | async-start | bytes 11280384 | tf_op jit(solution)/shard_map/reduce_scatter | solution.py:665
  391.1 11.5 %collective-permute-start.99 = (bf16[256,256]{1,0:T(8,128)(2,1)S(1)}, bf16[256,256]{1,0:T(8,128)(2,1)S(1)}, u32[]{:S(2)}, u32[]{:S(2)}) collective-permute-start(bf16[256,256]{1,0:T(8,128)(2,1)S(1)} %get-tuple-element.131.pack_ref.refs_0_), channel_id=1, source_target_pairs={{0,11},{1,10},{2,9},{3,8},{8,3},{9,2},{10,1},{11,0},{4,15},{5,14},... | collective-permute-start | bytes 393224 | tf_op jit(solution)/shard_map/ppermute | solution.py:69
  392.8 18.0 %collective-permute-start.98 = (bf16[256,256]{1,0:T(8,128)(2,1)S(1)}, bf16[256,256]{1,0:T(8,128)(2,1)S(1)}, u32[]{:S(2)}, u32[]{:S(2)}) collective-permute-start(bf16[256,256]{1,0:T(8,128)(2,1)S(1)} %get-tuple-element.131.pack_ref.refs_0_), channel_id=1, source_target_pairs={{0,3},{1,2},{2,1},{3,0},{8,11},{9,10},{10,9},{11,8},{4,7},{5,6},{6... | collective-permute-start | bytes 393224 | tf_op jit(solution)/shard_map/ppermute | solution.py:69
  393.8 23.7 %collective-permute-start.97 = (bf16[256,256]{1,0:T(8,128)(2,1)S(1)}, bf16[256,256]{1,0:T(8,128)(2,1)S(1)}, u32[]{:S(2)}, u32[]{:S(2)}) collective-permute-start(bf16[256,256]{1,0:T(8,128)(2,1)S(1)} %get-tuple-element.131.pack_ref.refs_0_), channel_id=1, source_target_pairs={{0,10},{1,11},{2,8},{3,9},{8,2},{9,3},{10,0},{11,1},{4,14},{5,15},... | collective-permute-start | bytes 393224 | tf_op jit(solution)/shard_map/ppermute | solution.py:69
  395.5 22.1 %collective-permute-start.96 = (bf16[256,256]{1,0:T(8,128)(2,1)S(1)}, bf16[256,256]{1,0:T(8,128)(2,1)S(1)}, u32[]{:S(2)}, u32[]{:S(2)}) collective-permute-start(bf16[256,256]{1,0:T(8,128)(2,1)S(1)} %get-tuple-element.131.pack_ref.refs_0_), channel_id=1, source_target_pairs={{0,2},{1,3},{2,0},{3,1},{8,10},{9,11},{10,8},{11,9},{4,6},{5,7},{6... | collective-permute-start | bytes 393224 | tf_op jit(solution)/shard_map/ppermute | solution.py:69
  397.8 19.8 %collective-permute-start.95 = (bf16[256,256]{1,0:T(8,128)(2,1)S(1)}, bf16[256,256]{1,0:T(8,128)(2,1)S(1)}, u32[]{:S(2)}, u32[]{:S(2)}) collective-permute-start(bf16[256,256]{1,0:T(8,128)(2,1)S(1)} %get-tuple-element.131.pack_ref.refs_0_), channel_id=1, source_target_pairs={{0,9},{1,8},{2,11},{3,10},{8,1},{9,0},{10,3},{11,2},{4,13},{5,12},... | collective-permute-start | bytes 393224 | tf_op jit(solution)/shard_map/ppermute | solution.py:69
  402.7 14.9 %collective-permute-start.94 = (bf16[256,256]{1,0:T(8,128)(2,1)S(1)}, bf16[256,256]{1,0:T(8,128)(2,1)S(1)}, u32[]{:S(2)}, u32[]{:S(2)}) collective-permute-start(bf16[256,256]{1,0:T(8,128)(2,1)S(1)} %get-tuple-element.131.pack_ref.refs_0_), channel_id=1, source_target_pairs={{0,1},{1,0},{2,3},{3,2},{8,9},{9,8},{10,11},{11,10},{4,5},{5,4},{6... | collective-permute-start | bytes 393224 | tf_op jit(solution)/shard_map/ppermute | solution.py:69
  410.8 7.4 %collective-permute-start.93 = (bf16[256,256]{1,0:T(8,128)(2,1)S(1)}, bf16[256,256]{1,0:T(8,128)(2,1)S(1)}, u32[]{:S(2)}, u32[]{:S(2)}) collective-permute-start(bf16[256,256]{1,0:T(8,128)(2,1)S(1)} %get-tuple-element.131.pack_ref.refs_0_), channel_id=1, source_target_pairs={{0,8},{1,9},{2,10},{3,11},{8,0},{9,1},{10,2},{11,3},{4,12},{5,13},... | collective-permute-start | bytes 393224 | tf_op jit(solution)/shard_map/ppermute | solution.py:69
  475.6 11.6 %collective-permute-start.117 = (bf16[32,1536]{1,0:T(8,128)(2,1)S(1)}, bf16[32,1536]{1,0:T(8,128)(2,1)S(1)}, u32[]{:S(2)}, u32[]{:S(2)}) collective-permute-start(bf16[32,1536]{1,0:T(8,128)(2,1)S(1)} %get-tuple-element.307), channel_id=1, source_target_pairs={{0,4},{4,0},{64,68},{68,64},{1,5},{5,1},{65,69},{69,65},{2,6},{6,2... | collective-permute-start | bytes 294920 | tf_op jit(solution)/shard_map/ppermute | solution.py:51
  476.4 10.8 %collective-permute-start.119 = (bf16[32,1536]{1,0:T(8,128)(2,1)S(1)}, bf16[32,1536]{1,0:T(8,128)(2,1)S(1)}, u32[]{:S(2)}, u32[]{:S(2)}) collective-permute-start(bf16[32,1536]{1,0:T(8,128)(2,1)S(1)} %get-tuple-element.308), channel_id=1, source_target_pairs={{0,68},{4,64},{64,4},{68,0},{1,69},{5,65},{65,5},{69,1},{2,70},{6,... | collective-permute-start | bytes 294920 | tf_op jit(solution)/shard_map/ppermute | solution.py:51
  477.6 9.6 %collective-permute-start.118 = (bf16[32,1536]{1,0:T(8,128)(2,1)S(1)}, bf16[32,1536]{1,0:T(8,128)(2,1)}, u32[]{:S(2)}, u32[]{:S(2)}) collective-permute-start(bf16[32,1536]{1,0:T(8,128)(2,1)S(1)} %get-tuple-element.309), channel_id=1, source_target_pairs={{0,64},{4,68},{64,0},{68,4},{1,65},{5,69},{65,1},{69,5},{2,66},{6,... | collective-permute-start | bytes 294920 | tf_op jit(solution)/shard_map/ppermute | solution.py:51
  502.0 9.0 %collective-permute-start.69 = (bf16[4,32,1536]{2,1,0:T(8,128)(2,1)}, bf16[4,32,1536]{2,1,0:T(8,128)(2,1)}, u32[]{:S(2)}, u32[]{:S(2)}) collective-permute-start(bf16[4,32,1536]{2,1,0:T(8,128)(2,1)} %bitcast.60), channel_id=1, source_target_pairs={{0,32},{32,0},{1,33},{33,1},{2,34},{34,2},{3,35},{35,3},{4,36},{36... | collective-permute-start | bytes 1179656 | tf_op jit(solution)/shard_map/ppermute | solution.py:35
  506.7 10.1 %collective-permute-start.130 = (bf16[256,256]{1,0:T(8,128)(2,1)S(1)}, bf16[256,256]{1,0:T(8,128)(2,1)S(1)}, u32[]{:S(2)}, u32[]{:S(2)}) collective-permute-start(bf16[256,256]{1,0:T(8,128)(2,1)S(1)} %get-tuple-element.148.pack_ref.refs_0_), channel_id=1, source_target_pairs={{0,11},{1,10},{2,9},{3,8},{8,3},{9,2},{10,1},{11,0},{4,15},{5,14},... | collective-permute-start | bytes 393224 | tf_op jit(solution)/shard_map/ppermute | solution.py:69
  509.5 19.1 %collective-permute-start.129 = (bf16[256,256]{1,0:T(8,128)(2,1)S(1)}, bf16[256,256]{1,0:T(8,128)(2,1)S(1)}, u32[]{:S(2)}, u32[]{:S(2)}) collective-permute-start(bf16[256,256]{1,0:T(8,128)(2,1)S(1)} %get-tuple-element.148.pack_ref.refs_0_), channel_id=1, source_target_pairs={{0,3},{1,2},{2,1},{3,0},{8,11},{9,10},{10,9},{11,8},{4,7},{5,6},{6... | collective-permute-start | bytes 393224 | tf_op jit(solution)/shard_map/ppermute | solution.py:69
  512.1 19.2 %collective-permute-start.128 = (bf16[256,256]{1,0:T(8,128)(2,1)S(1)}, bf16[256,256]{1,0:T(8,128)(2,1)S(1)}, u32[]{:S(2)}, u32[]{:S(2)}) collective-permute-start(bf16[256,256]{1,0:T(8,128)(2,1)S(1)} %get-tuple-element.148.pack_ref.refs_0_), channel_id=1, source_target_pairs={{0,10},{1,11},{2,8},{3,9},{8,2},{9,3},{10,0},{11,1},{4,14},{5,15},... | collective-permute-start | bytes 393224 | tf_op jit(solution)/shard_map/ppermute | solution.py:69
  512.4 19.7 %collective-permute-start.127 = (bf16[256,256]{1,0:T(8,128)(2,1)S(1)}, bf16[256,256]{1,0:T(8,128)(2,1)S(1)}, u32[]{:S(2)}, u32[]{:S(2)}) collective-permute-start(bf16[256,256]{1,0:T(8,128)(2,1)S(1)} %get-tuple-element.148.pack_ref.refs_0_), channel_id=1, source_target_pairs={{0,2},{1,3},{2,0},{3,1},{8,10},{9,11},{10,8},{11,9},{4,6},{5,7},{6... | collective-permute-start | bytes 393224 | tf_op jit(solution)/shard_map/ppermute | solution.py:69
  514.7 18.7 %collective-permute-start.126 = (bf16[256,256]{1,0:T(8,128)(2,1)S(1)}, bf16[256,256]{1,0:T(8,128)(2,1)S(1)}, u32[]{:S(2)}, u32[]{:S(2)}) collective-permute-start(bf16[256,256]{1,0:T(8,128)(2,1)S(1)} %get-tuple-element.148.pack_ref.refs_0_), channel_id=1, source_target_pairs={{0,9},{1,8},{2,11},{3,10},{8,1},{9,0},{10,3},{11,2},{4,13},{5,12},... | collective-permute-start | bytes 393224 | tf_op jit(solution)/shard_map/ppermute | solution.py:69
  516.8 17.9 %collective-permute-start.125 = (bf16[256,256]{1,0:T(8,128)(2,1)S(1)}, bf16[256,256]{1,0:T(8,128)(2,1)S(1)}, u32[]{:S(2)}, u32[]{:S(2)}) collective-permute-start(bf16[256,256]{1,0:T(8,128)(2,1)S(1)} %get-tuple-element.148.pack_ref.refs_0_), channel_id=1, source_target_pairs={{0,1},{1,0},{2,3},{3,2},{8,9},{9,8},{10,11},{11,10},{4,5},{5,4},{6... | collective-permute-start | bytes 393224 | tf_op jit(solution)/shard_map/ppermute | solution.py:69
  528.6 7.7 %collective-permute-start.124 = (bf16[256,256]{1,0:T(8,128)(2,1)S(1)}, bf16[256,256]{1,0:T(8,128)(2,1)S(1)}, u32[]{:S(2)}, u32[]{:S(2)}) collective-permute-start(bf16[256,256]{1,0:T(8,128)(2,1)S(1)} %get-tuple-element.148.pack_ref.refs_0_), channel_id=1, source_target_pairs={{0,8},{1,9},{2,10},{3,11},{8,0},{9,1},{10,2},{11,3},{4,12},{5,13},... | collective-permute-start | bytes 393224 | tf_op jit(solution)/shard_map/ppermute | solution.py:69
  531.3 16.5 %collective-permute-start.70 = (bf16[32,1536]{1,0:T(8,128)(2,1)S(1)}, bf16[32,1536]{1,0:T(8,128)(2,1)S(1)}, u32[]{:S(2)}, u32[]{:S(2)}) collective-permute-start(bf16[32,1536]{1,0:T(8,128)(2,1)S(1)} %get-tuple-element.322), channel_id=1, source_target_pairs={{0,4},{4,0},{64,68},{68,64},{1,5},{5,1},{65,69},{69,65},{2,6},{6,2... | collective-permute-start | bytes 294920 | tf_op jit(solution)/shard_map/ppermute | solution.py:51
  532.1 15.8 %collective-permute-start.72 = (bf16[32,1536]{1,0:T(8,128)(2,1)S(1)}, bf16[32,1536]{1,0:T(8,128)(2,1)S(1)}, u32[]{:S(2)}, u32[]{:S(2)}) collective-permute-start(bf16[32,1536]{1,0:T(8,128)(2,1)S(1)} %get-tuple-element.323), channel_id=1, source_target_pairs={{0,68},{4,64},{64,4},{68,0},{1,69},{5,65},{65,5},{69,1},{2,70},{6,... | collective-permute-start | bytes 294920 | tf_op jit(solution)/shard_map/ppermute | solution.py:51
  533.4 14.4 %collective-permute-start.71 = (bf16[32,1536]{1,0:T(8,128)(2,1)S(1)}, bf16[32,1536]{1,0:T(8,128)(2,1)S(1)}, u32[]{:S(2)}, u32[]{:S(2)}) collective-permute-start(bf16[32,1536]{1,0:T(8,128)(2,1)S(1)} %get-tuple-element.324), channel_id=1, source_target_pairs={{0,64},{4,68},{64,0},{68,4},{1,65},{5,69},{65,1},{69,5},{2,66},{6,... | collective-permute-start | bytes 294920 | tf_op jit(solution)/shard_map/ppermute | solution.py:51
  550.9 9.8 %collective-permute-start.132 = (bf16[48,1536]{1,0:T(8,128)(2,1)S(1)}, bf16[48,1536]{1,0:T(8,128)(2,1)S(1)}, u32[]{:S(2)}, u32[]{:S(2)}) collective-permute-start(bf16[48,1536]{1,0:T(8,128)(2,1)S(1)} %get-tuple-element.302), channel_id=1, source_target_pairs={{0,4},{4,0},{64,68},{68,64},{1,5},{5,1},{65,69},{69,65},{2,6},{6,2... | collective-permute-start | bytes 442376 | tf_op jit(solution)/shard_map/ppermute | solution.py:51
  551.5 9.2 %collective-permute-start.134 = (bf16[48,1536]{1,0:T(8,128)(2,1)S(1)}, bf16[48,1536]{1,0:T(8,128)(2,1)S(1)}, u32[]{:S(2)}, u32[]{:S(2)}) collective-permute-start(bf16[48,1536]{1,0:T(8,128)(2,1)S(1)} %get-tuple-element.303), channel_id=1, source_target_pairs={{0,68},{4,64},{64,4},{68,0},{1,69},{5,65},{65,5},{69,1},{2,70},{6,... | collective-permute-start | bytes 442376 | tf_op jit(solution)/shard_map/ppermute | solution.py:51
  553.1 7.6 %collective-permute-start.133 = (bf16[48,1536]{1,0:T(8,128)(2,1)S(1)}, bf16[48,1536]{1,0:T(8,128)(2,1)S(1)}, u32[]{:S(2)}, u32[]{:S(2)}) collective-permute-start(bf16[48,1536]{1,0:T(8,128)(2,1)S(1)} %get-tuple-element.304), channel_id=1, source_target_pairs={{0,64},{4,68},{64,0},{68,4},{1,65},{5,69},{65,1},{69,5},{2,66},{6,... | collective-permute-start | bytes 442376 | tf_op jit(solution)/shard_map/ppermute | solution.py:51
  555.2 81.7 %collective-permute-start.141 = (bf16[48,2304]{1,0:T(8,128)(2,1)}, bf16[48,2304]{1,0:T(8,128)(2,1)S(1)}, u32[]{:S(2)}, u32[]{:S(2)}) collective-permute-start(bf16[48,2304]{1,0:T(8,128)(2,1)} %get-tuple-element.305), channel_id=1, source_target_pairs={{0,4},{4,0},{1,5},{5,1},{2,6},{6,2},{3,7},{7,3},{8,12},{12,8},{9,1... | collective-permute-start | bytes 663560 | tf_op jit(solution)/shard_map/ppermute | solution.py:35
  561.5 14.4 %all-to-all-start = ((bf16[16,16,96]{2,1,0:T(8,128)(2,1)}), bf16[16,16,96]{2,1,0:T(8,128)(2,1)S(1)}, u32[]{:S(2)}, u32[]{:S(2)}) async-start(bf16[16,16,96]{2,1,0:T(8,128)(2,1)} %bitcast.318), calls=%async_computation.2 | async-start | bytes 131072 | tf_op jit(solution)/shard_map/all_to_all | solution.py:748
  566.5 11.3 %collective-permute-start.135 = (bf16[16,3072]{1,0:T(8,128)(2,1)S(1)}, bf16[16,3072]{1,0:T(8,128)(2,1)S(1)}, u32[]{:S(2)}, u32[]{:S(2)}) collective-permute-start(bf16[16,3072]{1,0:T(8,128)(2,1)S(1)} %get-tuple-element.342), channel_id=1, source_target_pairs={{0,16},{16,0},{1,17},{17,1},{2,18},{18,2},{3,19},{19,3},{4,20},{20... | collective-permute-start | bytes 294920 | tf_op jit(solution)/shard_map/ppermute | solution.py:35
  572.1 24.8 %collective-permute-start.142 = (bf16[1,4,96,768]{3,2,1,0:T(8,128)(2,1)}, bf16[1,4,96,768]{3,2,1,0:T(8,128)(2,1)}, u32[]{:S(2)}, u32[]{:S(2)}) collective-permute-start(bf16[1,4,96,768]{3,2,1,0:T(8,128)(2,1)} %get-tuple-element.250), channel_id=1, source_target_pairs={{0,1},{1,0},{2,3},{3,2},{4,5},{5,4},{6,7},{7,6},{8,9},{9,8},{10,11... | collective-permute-start | bytes 1769480 | tf_op jit(solution)/shard_map/ppermute | solution.py:112
  573.3 37.8 %collective-permute-start.144 = (bf16[1,4,96,768]{3,2,1,0:T(8,128)(2,1)}, bf16[1,4,96,768]{3,2,1,0:T(8,128)(2,1)}, u32[]{:S(2)}, u32[]{:S(2)}) collective-permute-start(bf16[1,4,96,768]{3,2,1,0:T(8,128)(2,1)} %get-tuple-element.251), channel_id=1, source_target_pairs={{0,2},{1,3},{2,0},{3,1},{4,6},{5,7},{6,4},{7,5},{8,10},{9,11},{10,... | collective-permute-start | bytes 1769480 | tf_op jit(solution)/shard_map/ppermute | solution.py:112
  575.7 35.4 %collective-permute-start.143 = (bf16[1,4,96,768]{3,2,1,0:T(8,128)(2,1)}, bf16[1,4,96,768]{3,2,1,0:T(8,128)(2,1)}, u32[]{:S(2)}, u32[]{:S(2)}) collective-permute-start(bf16[1,4,96,768]{3,2,1,0:T(8,128)(2,1)} %get-tuple-element.252), channel_id=1, source_target_pairs={{0,3},{1,2},{2,1},{3,0},{4,7},{5,6},{6,5},{7,4},{8,11},{9,10},{10,... | collective-permute-start | bytes 1769480 | tf_op jit(solution)/shard_map/ppermute | solution.py:112
  583.0 35.5 %collective-permute-start.137 = (bf16[2,2,16,3072]{3,2,1,0:T(8,128)(2,1)S(1)}, bf16[2,2,16,3072]{3,2,1,0:T(8,128)(2,1)S(1)}, u32[]{:S(2)}, u32[]{:S(2)}) collective-permute-start(bf16[2,2,16,3072]{3,2,1,0:T(8,128)(2,1)S(1)} %reverse_select_fusion.1), channel_id=1, source_target_pairs={{0,64},{64,0},{1,65},{65,1},{2,66},{66,2},{3,67},{67,3},{4,68},{68... | collective-permute-start | bytes 1179656 | tf_op jit(solution)/shard_map/ppermute | solution.py:35
  614.7 6.7 %collective-permute-start.145 = (bf16[1,1,96,768]{3,2,1,0:T(8,128)(2,1)}, bf16[1,1,96,768]{3,2,1,0:T(8,128)(2,1)S(1)}, u32[]{:S(2)}, u32[]{:S(2)}) collective-permute-start(bf16[1,1,96,768]{3,2,1,0:T(8,128)(2,1)} %get-tuple-element.299), channel_id=1, source_target_pairs={{0,8},{8,0},{16,24},{24,16},{1,9},{9,1},{17,25},{25,17},{2,10},{10... | collective-permute-start | bytes 442376 | tf_op jit(solution)/shard_map/ppermute | solution.py:112
  619.8 6.9 %collective-permute-start.138 = (bf16[48,3456]{1,0:T(8,128)(2,1)S(1)}, bf16[48,3456]{1,0:T(8,128)(2,1)S(1)}, u32[]{:S(2)}, u32[]{:S(2)}) collective-permute-start(bf16[48,3456]{1,0:T(8,128)(2,1)S(1)} %get-tuple-element.298), channel_id=1, source_target_pairs={{0,4},{4,0},{1,5},{5,1},{2,6},{6,2},{3,7},{7,3},{8,12},{12,8},{9,1... | collective-permute-start | bytes 995336 | tf_op jit(solution)/shard_map/ppermute | solution.py:35
  (270 other events, 2196.5 us)
Sparse Core Ops, SparseCore 0:
  25.4 69.8 all-gather.4
  98.1 75.9 all-gather.6
  245.3 54.4 all-gather.8
  311.5 34.9 all-gather.10
  372.8 89.5 reduce-scatter.2
  489.1 106.4 reduce-scatter.4

commit v4 on v3

--- a/solution.py
+++ b/solution.py
@@ -477,10 +477,21 @@
     return jnp.swapaxes(parts, -2, -3).reshape(*lead, -1)
 
 
-def width_restored(x):
-    lead = x.shape[:-1]
-    parts = x.reshape(*lead, 4, 8, -1)
-    return jnp.swapaxes(parts, -2, -3).reshape(*lead, -1)
+def shuffled(x, order):
+    size = x.shape[1] // len(order)
+    return jnp.concatenate([x[:, k * size : (k + 1) * size] for k in order], axis=1)
+
+
+def rows_mixed(rows_ref, out_ref):
+    order = [(p % 8) * 4 + p // 8 for p in range(32)]
+    out_ref[...] = shuffled(rows_ref[...].astype(FULL), order).astype(LOW)
+
+
+def rows_restored(last_ref, grad_ref, out_ref):
+    order = [(c % 4) * 8 + c // 4 for c in range(32)]
+    width = last_ref.shape[1]
+    out_ref[:, :width] = shuffled(last_ref[...], order).astype(LOW)
+    out_ref[:, width:] = shuffled(grad_ref[...], order).astype(LOW)
 
 
 def local(
@@ -536,7 +547,7 @@
     send = jnp.where(zh == 0, here[1], here[0])
     own_rows = jnp.concatenate([keep, swapped(send, "zh")], axis=0)
     token_rows = width_mixed(own_rows[:, :width])
-    grad_rows = width_mixed(own_rows[:, width:])
+    grad_rows = kernel_call(rows_mixed, [own_rows[:, width:]], [((32, width), LOW)])[0]
 
     own_0, token_rows, norm_free = tied(own_0, token_rows, turned[0])
     piece_0, token_all = tied(strips_of_all(own_0), jnp.concatenate(rows_of_all(token_rows)))
@@ -748,9 +759,7 @@
             norm_total = lax.all_to_all(jnp.swapaxes(norm_total, 0, 1), SPREAD, 0, 0, tiled=True)
             norm_total = jnp.sum(norm_total.astype(FULL), axis=0)
             grad = grad + unit_back(da[:-16], n_0, r_0, gains[0][0])
-    ends = jnp.concatenate(
-        [width_restored(residual.astype(LOW)), width_restored(grad.astype(LOW))], axis=1
-    )
+    ends = kernel_call(rows_restored, [residual, grad], [((32, 2 * width), LOW)])[0]
     ends = frames_back(ends)
     output, input_grad = ends[:, :, :width], ends[:, :, width:].astype(FULL)
 

time: 657 us -> 648 us (0.986)
  local copies, waits for them, and re-layouts: 81.3 us -> 68.7 us
    unnamed x367 -> x363, local copies, waits for them, and re-layouts: 57.2 us -> 52.9 us
    pallas_call x24 -> x26, Pallas kernels: 69.2 us -> 69.6 us  [kernel_call(): pl.pallas_call(body, grid=(steps,), in_specs=placed, out_specs=out_specs...]
  transfers between devices with their start and end apart: 156 -> 156, of which waited for: 95 -> 96; matrix products, arithmetic and copies ran while one was open for 10% -> 8% of each run, Pallas kernels for 9% -> 9%
where the time goes in v4:
time: 648 us; the launch traced here: 638 us
  waiting for transfers between devices  221 us (34%)
  starting transfers between devices  214 us (33%)
  Pallas kernels  69.6 us (11%)
  local copies, waits for them, and re-layouts  68.7 us (11%)
  other arithmetic  39.9 us (6%)
  between operations  18.9 us (3%)
    ppermute x39, starting transfers between devices, swapped(): return lax.ppermute(x, axis, SWAP)  81.1 us
    pallas_call x26, Pallas kernels, kernel_call(): pl.pallas_call(body, grid=(steps,), in_specs=placed, out_specs=out_specs...  69.6 us
    ppermute x39, waiting for transfers between devices, swapped(): return lax.ppermute(x, axis, SWAP)  57.2 us
    unnamed x363, local copies, waits for them, and re-layouts  52.9 us
    ppermute x36, starting transfers between devices, sum_to_rows(): total = total + lax.ppermute(low[d], CHIPS, flipped(4, d)).astype(FULL)  40.5 us
    ppermute x36, starting transfers between devices, rows_of_all(): lax.ppermute(rows, CHIPS, flipped(4, d))  40.3 us
    ppermute x36, waiting for transfers between devices, sum_to_rows(): total = total + lax.ppermute(low[d], CHIPS, flipped(4, d)).astype(FULL)  32.3 us
    ppermute x36, waiting for transfers between devices, rows_of_all(): lax.ppermute(rows, CHIPS, flipped(4, d))  31.2 us
  transfers between devices with their start and end apart: 156, of which 96 were waited for; matrix products, arithmetic and copies ran while one was open for 8% of the time, Pallas kernels for 9%

profile of v4, /device:TPU:1, one launch (start us, length us, event | category | flops | bytes accessed | tf_op | source)
XLA Modules:
  0.0 638.2 jit_solution(10038727324844174573)
XLA Ops:
  13.1 3.7 collective-permute-start.1
  20.8 3.7 collective-permute-done.22
  25.7 5.3 collective-permute-done.39
  34.0 3.2 collective-permute-start.3
  38.5 2.7 collective-permute-start.9
  48.3 2.7 collective-permute-start.13
  52.9 2.5 collective-permute-start.6
  55.5 2.8 collective-permute-done.11
  58.7 9.5 %collective-permute-start.17 = (bf16[128,1536]{1,0:T(8,128)(2,1)S(1)}, bf16[128,1536]{1,0:T(8,128)(2,1)S(1)}, u32[]{:S(2)}, u32[]{:S(2)}) collective-permute-start(bf16[128,1536]{1,0:T(8,128)(2,1)S(1)} %pad_maximum_fusion.3), channel_id=1, source_target_pairs={{0,32},{32,0},{1,33},{33,1},{2,34},{34,2},{3,35},{35,3},{4,36},{36... | collective-permute-start | bytes 1179656 | tf_op jit(solution)/shard_map/ppermute | solution.py:35
  74.6 8.2 %collective-permute-done.18 = bf16[256,384]{1,0:T(8,128)(2,1)S(1)} collective-permute-done((bf16[256,384]{1,0:T(8,128)(2,1)S(1)}, bf16[256,384]{1,0:T(8,128)(2,1)S(1)}, u32[]{:S(2)}, u32[]{:S(2)}) %collective-permute-start.18) | collective-permute-done | bytes 196640 | tf_op jit(solution)/shard_map/ppermute | solution.py:35
  82.9 3.0 collective-permute-start.20
  87.0 18.1 %collective-permute-done.21.kv3 = bf16[512,384]{1,0:T(8,128)(2,1)S(1)} collective-permute-done((bf16[512,384]{1,0:T(8,128)(2,1)S(1)}, bf16[512,384]{1,0:T(8,128)(2,1)S(1)}, u32[]{:S(2)}, u32[]{:S(2)}) %collective-permute-start.21) | collective-permute-done | bytes 393248 | tf_op jit(solution)/shard_map/ppermute | solution.py:60
  106.7 2.7 copy-done.4
  111.4 5.3 shard_map.230
  135.9 3.3 collective-permute-start.30
  160.2 3.3 collective-permute-start.38
  165.7 8.4 %all-gather.7.cloned.1.call-done.up_ref.down_ref.w_ref.refs_20_ = bf16[1536,3072]{1,0:T(8,128)(2,1)} async-done(((bf16[96,3072]{1,0:T(8,128)(2,1)}), bf16[1536,3072]{1,0:T(8,128)(2,1)}) %all-gather.7.cloned.1.call-update) | async-done | bytes 9437200 | tf_op jit(solution)/shard_map/all_gather | solution.py:527
  174.1 3.7 copy-done
  199.8 3.4 collective-permute-start.47
  207.0 5.1 collective-permute-done.48
  212.9 2.5 collective-permute-start.51
  216.7 3.9 collective-permute-done.52
  221.4 11.0 %collective-permute-done.51.kv3 = bf16[512,384]{1,0:T(8,128)(2,1)} collective-permute-done((bf16[512,384]{1,0:T(8,128)(2,1)}, bf16[512,384]{1,0:T(8,128)(2,1)}, u32[]{:S(2)}, u32[]{:S(2)}) %collective-permute-start.51) | collective-permute-done | bytes 393248 | tf_op jit(solution)/shard_map/ppermute | solution.py:60
  232.6 3.7 copy-done.1
  236.3 6.7 %shard_map.234 = (bf16[256,192]{1,0:T(8,128)(2,1)S(1)}, f32[8,256]{1,0:T(8,128)S(1)}, bf16[256,256]{1,0:T(8,128)(2,1)S(1)}, bf16[256,1536]{1,0:T(8,128)(2,1)S(1)}) custom-call(bf16[256,576]{1,0:T(8,128)(2,1)S(1)} %shard_map.233.q_ref.qkv_ref, bf16[512,384]{1,0:T(8,128)(2,1)} %pad_maximum_fusion.8.kv0, bf16[512,384]{1,0:T(8,128)(2,1)} %collective-permute-done.49.kv1, ...), custom_call_target="tpu_custom_call" | custom-call | tf_op jit(solution)/shard_map/pallas_call | solution.py:168
  246.4 2.4 collective-permute-start.53
  265.5 3.3 collective-permute-start.60
  268.8 2.4 convolution_convert_fusion
  271.3 3.7 copy-done.2
  294.7 3.9 collective-permute-start.68
  299.3 2.8 collective-permute-start.76
  305.3 3.0 shard_map.236
  312.3 3.0 shard_map.238
  332.8 2.9 collective-permute-start.84
  353.7 4.8 shard_map.240
  358.5 2.9 copy-done.9
  371.6 2.5 collective-permute-done.90
  374.2 2.8 collective-permute-start.92
  378.3 3.8 copy-done.3
  389.4 5.4 collective-permute-done.99.refs_7_
  394.9 7.1 %collective-permute-done.98.refs_6_ = bf16[256,256]{1,0:T(8,128)(2,1)S(1)} collective-permute-done((bf16[256,256]{1,0:T(8,128)(2,1)S(1)}, bf16[256,256]{1,0:T(8,128)(2,1)S(1)}, u32[]{:S(2)}, u32[]{:S(2)}) %collective-permute-start.98) | collective-permute-done | bytes 131104 | tf_op jit(solution)/shard_map/ppermute | solution.py:69
  404.4 4.8 shard_map.242
  409.6 4.9 shard_map.243
  433.6 3.4 collective-permute-start.107
  457.0 3.4 collective-permute-start.115
  470.3 8.1 %shard_map.246 = bf16[1536,3456]{1,0:T(8,128)(2,1)} custom-call(bf16[128,1536]{1,0:T(8,128)(2,1)S(1)} %copy-done.26, bf16[128,1536]{1,0:T(8,128)(2,1)S(1)} %copy-done.65, bf16[256,768]{1,0:T(8,128)(2,1)S(1)} %get-tuple-element.139.refs_2_, bf16[128,1536]{1,0:T(8,128)(2,1)S(1)} %pad_maximum_fusion.14.dy0_ref.refs_3_, ...), custom_call_target="tpu_custom_call" | custom-call | tf_op jit(solution)/shard_map/pallas_call | solution.py:168
  490.1 2.4 collective-permute-start.123
  498.2 3.0 collective-permute-start.130
  503.4 2.6 collective-permute-start.127
  508.7 11.4 %collective-permute-done.129.refs_6_ = bf16[256,256]{1,0:T(8,128)(2,1)S(1)} collective-permute-done((bf16[256,256]{1,0:T(8,128)(2,1)S(1)}, bf16[256,256]{1,0:T(8,128)(2,1)S(1)}, u32[]{:S(2)}, u32[]{:S(2)}) %collective-permute-start.129) | collective-permute-done | bytes 131104 | tf_op jit(solution)/shard_map/ppermute | solution.py:69
  520.2 2.6 shard_map.248
  527.6 4.9 shard_map.249
  543.8 3.4 shard_map.251
  549.6 4.6 all-to-all-start
  554.8 2.9 collective-permute-start.135
  557.8 2.7 constant_dynamic-slice_fusion.5
  566.2 3.7 collective-permute-start.136
  572.9 8.4 %collective-permute-done.142 = bf16[1,4,96,768]{3,2,1,0:T(8,128)(2,1)S(1)} collective-permute-done((bf16[1,4,96,768]{3,2,1,0:T(8,128)(2,1)}, bf16[1,4,96,768]{3,2,1,0:T(8,128)(2,1)S(1)}, u32[]{:S(2)}, u32[]{:S(2)}) %collective-permute-start.142) | collective-permute-done | bytes 589856 | tf_op jit(solution)/shard_map/ppermute | solution.py:112
  581.3 17.8 %collective-permute-done.144 = bf16[1,4,96,768]{3,2,1,0:T(8,128)(2,1)} collective-permute-done((bf16[1,4,96,768]{3,2,1,0:T(8,128)(2,1)}, bf16[1,4,96,768]{3,2,1,0:T(8,128)(2,1)}, u32[]{:S(2)}, u32[]{:S(2)}) %collective-permute-start.144) | collective-permute-done | bytes 589856 | tf_op jit(solution)/shard_map/ppermute | solution.py:112
  599.0 3.5 collective-permute-done.143
  602.6 2.9 fusion.124
  606.6 3.5 collective-permute-start.146
  614.7 3.4 collective-permute-done.138.refs_4_
  618.9 3.5 collective-permute-start.139
  (854 shorter events, 322.1 us)
Async XLA Ops:
  7.2 99.5 %all-gather.5.cloned.1.call-start = ((), (), s32[]{:S(2)}) async-start(), calls=%async_computation.3 | async-start | bytes 5013504 | tf_op jit(solution)/shard_map/all_gather | solution.py:527
  9.8 6.9 %collective-permute-start = (bf16[48,640]{1,0:T(8,128)(2,1)S(1)}, bf16[48,640]{1,0:T(8,128)(2,1)S(1)}, u32[]{:S(2)}, u32[]{:S(2)}) collective-permute-start(bf16[48,640]{1,0:T(8,128)(2,1)S(1)} %get-tuple-element.90), channel_id=1, source_target_pairs={{0,4},{4,0},{1,5},{5,1},{2,6},{6,2},{3,7},{7,3},{8,12},{12,8},{9,1... | collective-permute-start | bytes 184328 | tf_op jit(solution)/shard_map/ppermute | solution.py:35
  25.3 148.8 %all-gather.7.cloned.1.call-start = ((), (), s32[]{:S(2)}) async-start(), calls=%async_computation.4 | async-start | bytes 10027008 | tf_op jit(solution)/shard_map/all_gather | solution.py:527
  32.0 271.0 %all-gather.9.cloned.1.call-start = ((), (), s32[]{:S(2)}) async-start(), calls=%async_computation.5 | async-start | bytes 5013504 | tf_op jit(solution)/shard_map/all_gather | solution.py:527
  34.0 14.3 %collective-permute-start.3 = (bf16[1,1,48,640]{3,2,1,0:T(8,128)(2,1)S(1)}, bf16[1,1,48,640]{3,2,1,0:T(8,128)(2,1)S(1)}, u32[]{:S(2)}, u32[]{:S(2)}) collective-permute-start(bf16[1,1,48,640]{3,2,1,0:T(8,128)(2,1)S(1)} %get-tuple-element.349), channel_id=1, source_target_pairs={{0,24},{8,16},{16,8},{24,0},{1,25},{9,17},{17,9},{25,1},{2,26},{10... | collective-permute-start | bytes 184328 | tf_op jit(solution)/shard_map/ppermute | solution.py:86
  37.2 13.8 %collective-permute-start.4 = (bf16[1,1,48,640]{3,2,1,0:T(8,128)(2,1)S(1)}, bf16[1,1,48,640]{3,2,1,0:T(8,128)(2,1)S(1)}, u32[]{:S(2)}, u32[]{:S(2)}) collective-permute-start(bf16[1,1,48,640]{3,2,1,0:T(8,128)(2,1)S(1)} %get-tuple-element.349), channel_id=1, source_target_pairs={{0,16},{8,24},{16,0},{24,8},{1,17},{9,25},{17,1},{25,9},{2,18},{10... | collective-permute-start | bytes 184328 | tf_op jit(solution)/shard_map/ppermute | solution.py:86
  38.5 8.8 %collective-permute-start.9 = (bf16[1,1,48,640]{3,2,0,1:T(8,128)(2,1)S(1)}, bf16[1,1,48,640]{3,2,0,1:T(8,128)(2,1)S(1)}, u32[]{:S(2)}, u32[]{:S(2)}) collective-permute-start(bf16[1,1,48,640]{3,2,0,1:T(8,128)(2,1)S(1)} %get-tuple-element.350), channel_id=1, source_target_pairs={{0,3},{1,2},{2,1},{3,0},{4,7},{5,6},{6,5},{7,4},{8,11},{9,10},{10,... | collective-permute-start | bytes 184328 | tf_op jit(solution)/shard_map/ppermute | solution.py:86
  44.8 8.0 %collective-permute-start.16 = (bf16[32,1536]{1,0:T(8,128)(2,1)S(1)}, bf16[32,1536]{1,0:T(8,128)(2,1)S(1)}, u32[]{:S(2)}, u32[]{:S(2)}) collective-permute-start(bf16[32,1536]{1,0:T(8,128)(2,1)S(1)} %reshape.646), channel_id=1, source_target_pairs={{0,68},{4,64},{64,4},{68,0},{1,69},{5,65},{65,5},{69,1},{2,70},{6,... | collective-permute-start | bytes 294920 | tf_op jit(solution)/shard_map/ppermute | solution.py:39
  48.3 19.9 %collective-permute-start.13 = (bf16[4,1,48,640]{3,2,0,1:T(8,128)(2,1)S(1)}, bf16[4,1,48,640]{3,2,0,1:T(8,128)(2,1)S(1)}, u32[]{:S(2)}, u32[]{:S(2)}) collective-permute-start(bf16[4,1,48,640]{3,2,0,1:T(8,128)(2,1)S(1)} %constant_dynamic-update-slice_fusion.5), channel_id=1, source_target_pairs={{0,16},{8,24},{16,0},{24,8},{1,17},{9,25},{17,1},{25,9},{2,18},{10... | collective-permute-start | bytes 737288 | tf_op jit(solution)/shard_map/ppermute | solution.py:86
  51.1 7.7 %collective-permute-start.12 = (bf16[4,1,48,640]{3,2,0,1:T(8,128)(2,1)S(1)}, bf16[4,1,48,640]{3,2,0,1:T(8,128)(2,1)S(1)}, u32[]{:S(2)}, u32[]{:S(2)}) collective-permute-start(bf16[4,1,48,640]{3,2,0,1:T(8,128)(2,1)S(1)} %constant_dynamic-update-slice_fusion.5), channel_id=1, source_target_pairs={{0,24},{8,16},{16,8},{24,0},{1,25},{9,17},{17,9},{25,1},{2,26},{10... | collective-permute-start | bytes 737288 | tf_op jit(solution)/shard_map/ppermute | solution.py:86
  52.8 15.6 %collective-permute-start.7 = (bf16[1,4,48,640]{3,2,1,0:T(8,128)(2,1)S(1)}, bf16[1,4,48,640]{3,2,1,0:T(8,128)(2,1)S(1)}, u32[]{:S(2)}, u32[]{:S(2)}) collective-permute-start(bf16[1,4,48,640]{3,2,1,0:T(8,128)(2,1)S(1)} %constant_dynamic-update-slice_fusion.9), channel_id=1, source_target_pairs={{0,2},{1,3},{2,0},{3,1},{4,6},{5,7},{6,4},{7,5},{8,10},{9,11},{10,... | collective-permute-start | bytes 737288 | tf_op jit(solution)/shard_map/ppermute | solution.py:86
  52.9 15.4 %collective-permute-start.6 = (bf16[1,4,48,640]{3,2,1,0:T(8,128)(2,1)S(1)}, bf16[1,4,48,640]{3,2,1,0:T(8,128)(2,1)S(1)}, u32[]{:S(2)}, u32[]{:S(2)}) collective-permute-start(bf16[1,4,48,640]{3,2,1,0:T(8,128)(2,1)S(1)} %constant_dynamic-update-slice_fusion.9), channel_id=1, source_target_pairs={{0,3},{1,2},{2,1},{3,0},{4,7},{5,6},{6,5},{7,4},{8,11},{9,10},{10,... | collective-permute-start | bytes 737288 | tf_op jit(solution)/shard_map/ppermute | solution.py:86
  58.4 9.9 %collective-permute-start.5 = (bf16[1,4,48,640]{3,2,1,0:T(8,128)(2,1)S(1)}, bf16[1,4,48,640]{3,2,1,0:T(8,128)(2,1)S(1)}, u32[]{:S(2)}, u32[]{:S(2)}) collective-permute-start(bf16[1,4,48,640]{3,2,1,0:T(8,128)(2,1)S(1)} %constant_dynamic-update-slice_fusion.9), channel_id=1, source_target_pairs={{0,1},{1,0},{2,3},{3,2},{4,5},{5,4},{6,7},{7,6},{8,9},{9,8},{10,11... | collective-permute-start | bytes 737288 | tf_op jit(solution)/shard_map/ppermute | solution.py:86
  58.7 10.8 %collective-permute-start.17 = (bf16[128,1536]{1,0:T(8,128)(2,1)S(1)}, bf16[128,1536]{1,0:T(8,128)(2,1)S(1)}, u32[]{:S(2)}, u32[]{:S(2)}) collective-permute-start(bf16[128,1536]{1,0:T(8,128)(2,1)S(1)} %pad_maximum_fusion.3), channel_id=1, source_target_pairs={{0,32},{32,0},{1,33},{33,1},{2,34},{34,2},{3,35},{35,3},{4,36},{36... | collective-permute-start | bytes 1179656 | tf_op jit(solution)/shard_map/ppermute | solution.py:35
  73.7 9.1 %collective-permute-start.18 = (bf16[256,384]{1,0:T(8,128)(2,1)S(1)}, bf16[256,384]{1,0:T(8,128)(2,1)S(1)}, u32[]{:S(2)}, u32[]{:S(2)}) collective-permute-start(bf16[256,384]{1,0:T(8,128)(2,1)S(1)} %slice.552), channel_id=1, source_target_pairs={{0,8},{8,0},{1,9},{9,1},{2,10},{10,2},{3,11},{11,3},{4,12},{12,4},... | collective-permute-start | bytes 589832 | tf_op jit(solution)/shard_map/ppermute | solution.py:35
  82.8 22.2 %collective-permute-start.21 = (bf16[512,384]{1,0:T(8,128)(2,1)S(1)}, bf16[512,384]{1,0:T(8,128)(2,1)S(1)}, u32[]{:S(2)}, u32[]{:S(2)}) collective-permute-start(bf16[512,384]{1,0:T(8,128)(2,1)S(1)} %pad_maximum_fusion.4.kv0), channel_id=1, source_target_pairs={{0,3},{1,2},{2,1},{3,0},{4,7},{5,6},{6,5},{7,4},{8,11},{9,10},{10,... | collective-permute-start | bytes 1179656 | tf_op jit(solution)/shard_map/ppermute | solution.py:60
  82.9 22.1 %collective-permute-start.20 = (bf16[512,384]{1,0:T(8,128)(2,1)S(1)}, bf16[512,384]{1,0:T(8,128)(2,1)S(1)}, u32[]{:S(2)}, u32[]{:S(2)}) collective-permute-start(bf16[512,384]{1,0:T(8,128)(2,1)S(1)} %pad_maximum_fusion.4.kv0), channel_id=1, source_target_pairs={{0,2},{1,3},{2,0},{3,1},{4,6},{5,7},{6,4},{7,5},{8,10},{9,11},{10,... | collective-permute-start | bytes 1179656 | tf_op jit(solution)/shard_map/ppermute | solution.py:60
  85.9 20.0 %collective-permute-start.19 = (bf16[512,384]{1,0:T(8,128)(2,1)S(1)}, bf16[512,384]{1,0:T(8,128)(2,1)S(1)}, u32[]{:S(2)}, u32[]{:S(2)}) collective-permute-start(bf16[512,384]{1,0:T(8,128)(2,1)S(1)} %pad_maximum_fusion.4.kv0), channel_id=1, source_target_pairs={{0,1},{1,0},{2,3},{3,2},{4,5},{5,4},{6,7},{7,6},{8,9},{9,8},{10,11... | collective-permute-start | bytes 1179656 | tf_op jit(solution)/shard_map/ppermute | solution.py:60
  212.9 19.6 %collective-permute-start.51 = (bf16[512,384]{1,0:T(8,128)(2,1)}, bf16[512,384]{1,0:T(8,128)(2,1)}, u32[]{:S(2)}, u32[]{:S(2)}) collective-permute-start(bf16[512,384]{1,0:T(8,128)(2,1)} %pad_maximum_fusion.8.kv0), channel_id=1, source_target_pairs={{0,3},{1,2},{2,1},{3,0},{4,7},{5,6},{6,5},{7,4},{8,11},{9,10},{10,... | collective-permute-start | bytes 1179656 | tf_op jit(solution)/shard_map/ppermute | solution.py:60
  215.4 17.1 %collective-permute-start.50 = (bf16[512,384]{1,0:T(8,128)(2,1)}, bf16[512,384]{1,0:T(8,128)(2,1)}, u32[]{:S(2)}, u32[]{:S(2)}) collective-permute-start(bf16[512,384]{1,0:T(8,128)(2,1)} %pad_maximum_fusion.8.kv0), channel_id=1, source_target_pairs={{0,2},{1,3},{2,0},{3,1},{4,6},{5,7},{6,4},{7,5},{8,10},{9,11},{10,... | collective-permute-start | bytes 1179656 | tf_op jit(solution)/shard_map/ppermute | solution.py:60
  215.8 16.8 %collective-permute-start.49 = (bf16[512,384]{1,0:T(8,128)(2,1)}, bf16[512,384]{1,0:T(8,128)(2,1)}, u32[]{:S(2)}, u32[]{:S(2)}) collective-permute-start(bf16[512,384]{1,0:T(8,128)(2,1)} %pad_maximum_fusion.8.kv0), channel_id=1, source_target_pairs={{0,1},{1,0},{2,3},{3,2},{4,5},{5,4},{6,7},{7,6},{8,9},{9,8},{10,11... | collective-permute-start | bytes 1179656 | tf_op jit(solution)/shard_map/ppermute | solution.py:60
  245.2 97.8 %all-gather.11.cloned.1.call-start = ((), (), s32[]{:S(2)}) async-start(), calls=%async_computation.6 | async-start | bytes 2359296 | tf_op jit(solution)/shard_map/all_gather | solution.py:667
  290.6 8.0 %collective-permute-start.75 = (bf16[32,1536]{1,0:T(8,128)(2,1)S(1)}, bf16[32,1536]{1,0:T(8,128)(2,1)S(1)}, u32[]{:S(2)}, u32[]{:S(2)}) collective-permute-start(bf16[32,1536]{1,0:T(8,128)(2,1)S(1)} %shard_map.237), channel_id=1, source_target_pairs={{0,68},{4,64},{64,4},{68,0},{1,69},{5,65},{65,5},{69,1},{2,70},{6,... | collective-permute-start | bytes 294920 | tf_op jit(solution)/shard_map/ppermute | solution.py:39
  291.8 6.8 %collective-permute-start.74 = (bf16[32,1536]{1,0:T(8,128)(2,1)S(1)}, bf16[32,1536]{1,0:T(8,128)(2,1)S(1)}, u32[]{:S(2)}, u32[]{:S(2)}) collective-permute-start(bf16[32,1536]{1,0:T(8,128)(2,1)S(1)} %shard_map.237), channel_id=1, source_target_pairs={{0,64},{4,68},{64,0},{68,4},{1,65},{5,69},{65,1},{69,5},{2,66},{6,... | collective-permute-start | bytes 294920 | tf_op jit(solution)/shard_map/ppermute | solution.py:39
  294.7 8.3 %collective-permute-start.68 = (bf16[128,1536]{1,0:T(8,128)(2,1)}, bf16[128,1536]{1,0:T(8,128)(2,1)}, u32[]{:S(2)}, u32[]{:S(2)}) collective-permute-start(bf16[128,1536]{1,0:T(8,128)(2,1)} %pad_maximum_fusion.10.e0_ref.refs_0_), channel_id=1, source_target_pairs={{0,32},{32,0},{1,33},{33,1},{2,34},{34,2},{3,35},{35,3},{4,36},{36... | collective-permute-start | bytes 1179656 | tf_op jit(solution)/shard_map/ppermute | solution.py:35
  299.3 10.6 %collective-permute-start.76 = (bf16[128,1536]{1,0:T(8,128)(2,1)}, bf16[128,1536]{1,0:T(8,128)(2,1)}, u32[]{:S(2)}, u32[]{:S(2)}) collective-permute-start(bf16[128,1536]{1,0:T(8,128)(2,1)} %pad_maximum_fusion.11.dy0_ref.refs_3_), channel_id=1, source_target_pairs={{0,32},{32,0},{1,33},{33,1},{2,34},{34,2},{3,35},{35,3},{4,36},{36... | collective-permute-start | bytes 1179656 | tf_op jit(solution)/shard_map/ppermute | solution.py:35
  302.9 177.3 %reduce-scatter.3.cloned.1.call-start = ((), (), s32[]{:S(2)}) async-start(), calls=%async_computation.7 | async-start | bytes 7520256 | tf_op jit(solution)/shard_map/reduce_scatter | solution.py:676
  347.7 14.4 %collective-permute-start.86 = (bf16[32,1536]{1,0:T(8,128)(2,1)}, bf16[32,1536]{1,0:T(8,128)(2,1)}, u32[]{:S(2)}, u32[]{:S(2)}) collective-permute-start(bf16[32,1536]{1,0:T(8,128)(2,1)} %get-tuple-element.316), channel_id=1, source_target_pairs={{0,4},{4,0},{64,68},{68,64},{1,5},{5,1},{65,69},{69,65},{2,6},{6,2... | collective-permute-start | bytes 294920 | tf_op jit(solution)/shard_map/ppermute | solution.py:51
  348.8 13.3 %collective-permute-start.88 = (bf16[32,1536]{1,0:T(8,128)(2,1)}, bf16[32,1536]{1,0:T(8,128)(2,1)}, u32[]{:S(2)}, u32[]{:S(2)}) collective-permute-start(bf16[32,1536]{1,0:T(8,128)(2,1)} %get-tuple-element.317), channel_id=1, source_target_pairs={{0,68},{4,64},{64,4},{68,0},{1,69},{5,65},{65,5},{69,1},{2,70},{6,... | collective-permute-start | bytes 294920 | tf_op jit(solution)/shard_map/ppermute | solution.py:51
  350.6 11.5 %collective-permute-start.87 = (bf16[32,1536]{1,0:T(8,128)(2,1)}, bf16[32,1536]{1,0:T(8,128)(2,1)}, u32[]{:S(2)}, u32[]{:S(2)}) collective-permute-start(bf16[32,1536]{1,0:T(8,128)(2,1)} %get-tuple-element.318), channel_id=1, source_target_pairs={{0,64},{4,68},{64,0},{68,4},{1,65},{5,69},{65,1},{69,5},{2,66},{6,... | collective-permute-start | bytes 294920 | tf_op jit(solution)/shard_map/ppermute | solution.py:51
  364.0 246.2 %reduce-scatter.5.cloned.1.call-start = ((), (), s32[]{:S(2)}) async-start(), calls=%async_computation.8 | async-start | bytes 11280384 | tf_op jit(solution)/shard_map/reduce_scatter | solution.py:676
  382.8 12.0 %collective-permute-start.99 = (bf16[256,256]{1,0:T(8,128)(2,1)S(1)}, bf16[256,256]{1,0:T(8,128)(2,1)S(1)}, u32[]{:S(2)}, u32[]{:S(2)}) collective-permute-start(bf16[256,256]{1,0:T(8,128)(2,1)S(1)} %get-tuple-element.131.pack_ref.refs_0_), channel_id=1, source_target_pairs={{0,11},{1,10},{2,9},{3,8},{8,3},{9,2},{10,1},{11,0},{4,15},{5,14},... | collective-permute-start | bytes 393224 | tf_op jit(solution)/shard_map/ppermute | solution.py:69
  384.3 17.6 %collective-permute-start.98 = (bf16[256,256]{1,0:T(8,128)(2,1)S(1)}, bf16[256,256]{1,0:T(8,128)(2,1)S(1)}, u32[]{:S(2)}, u32[]{:S(2)}) collective-permute-start(bf16[256,256]{1,0:T(8,128)(2,1)S(1)} %get-tuple-element.131.pack_ref.refs_0_), channel_id=1, source_target_pairs={{0,3},{1,2},{2,1},{3,0},{8,11},{9,10},{10,9},{11,8},{4,7},{5,6},{6... | collective-permute-start | bytes 393224 | tf_op jit(solution)/shard_map/ppermute | solution.py:69
  385.5 23.6 %collective-permute-start.97 = (bf16[256,256]{1,0:T(8,128)(2,1)S(1)}, bf16[256,256]{1,0:T(8,128)(2,1)S(1)}, u32[]{:S(2)}, u32[]{:S(2)}) collective-permute-start(bf16[256,256]{1,0:T(8,128)(2,1)S(1)} %get-tuple-element.131.pack_ref.refs_0_), channel_id=1, source_target_pairs={{0,10},{1,11},{2,8},{3,9},{8,2},{9,3},{10,0},{11,1},{4,14},{5,15},... | collective-permute-start | bytes 393224 | tf_op jit(solution)/shard_map/ppermute | solution.py:69
  387.0 22.2 %collective-permute-start.96 = (bf16[256,256]{1,0:T(8,128)(2,1)S(1)}, bf16[256,256]{1,0:T(8,128)(2,1)S(1)}, u32[]{:S(2)}, u32[]{:S(2)}) collective-permute-start(bf16[256,256]{1,0:T(8,128)(2,1)S(1)} %get-tuple-element.131.pack_ref.refs_0_), channel_id=1, source_target_pairs={{0,2},{1,3},{2,0},{3,1},{8,10},{9,11},{10,8},{11,9},{4,6},{5,7},{6... | collective-permute-start | bytes 393224 | tf_op jit(solution)/shard_map/ppermute | solution.py:69
  389.4 19.7 %collective-permute-start.95 = (bf16[256,256]{1,0:T(8,128)(2,1)S(1)}, bf16[256,256]{1,0:T(8,128)(2,1)S(1)}, u32[]{:S(2)}, u32[]{:S(2)}) collective-permute-start(bf16[256,256]{1,0:T(8,128)(2,1)S(1)} %get-tuple-element.131.pack_ref.refs_0_), channel_id=1, source_target_pairs={{0,9},{1,8},{2,11},{3,10},{8,1},{9,0},{10,3},{11,2},{4,13},{5,12},... | collective-permute-start | bytes 393224 | tf_op jit(solution)/shard_map/ppermute | solution.py:69
  394.9 14.3 %collective-permute-start.94 = (bf16[256,256]{1,0:T(8,128)(2,1)S(1)}, bf16[256,256]{1,0:T(8,128)(2,1)S(1)}, u32[]{:S(2)}, u32[]{:S(2)}) collective-permute-start(bf16[256,256]{1,0:T(8,128)(2,1)S(1)} %get-tuple-element.131.pack_ref.refs_0_), channel_id=1, source_target_pairs={{0,1},{1,0},{2,3},{3,2},{8,9},{9,8},{10,11},{11,10},{4,5},{5,4},{6... | collective-permute-start | bytes 393224 | tf_op jit(solution)/shard_map/ppermute | solution.py:69
  401.9 7.7 %collective-permute-start.93 = (bf16[256,256]{1,0:T(8,128)(2,1)S(1)}, bf16[256,256]{1,0:T(8,128)(2,1)S(1)}, u32[]{:S(2)}, u32[]{:S(2)}) collective-permute-start(bf16[256,256]{1,0:T(8,128)(2,1)S(1)} %get-tuple-element.131.pack_ref.refs_0_), channel_id=1, source_target_pairs={{0,8},{1,9},{2,10},{3,11},{8,0},{9,1},{10,2},{11,3},{4,12},{5,13},... | collective-permute-start | bytes 393224 | tf_op jit(solution)/shard_map/ppermute | solution.py:69
  466.8 11.6 %collective-permute-start.117 = (bf16[32,1536]{1,0:T(8,128)(2,1)S(1)}, bf16[32,1536]{1,0:T(8,128)(2,1)S(1)}, u32[]{:S(2)}, u32[]{:S(2)}) collective-permute-start(bf16[32,1536]{1,0:T(8,128)(2,1)S(1)} %get-tuple-element.307), channel_id=1, source_target_pairs={{0,4},{4,0},{64,68},{68,64},{1,5},{5,1},{65,69},{69,65},{2,6},{6,2... | collective-permute-start | bytes 294920 | tf_op jit(solution)/shard_map/ppermute | solution.py:51
  467.5 10.9 %collective-permute-start.119 = (bf16[32,1536]{1,0:T(8,128)(2,1)S(1)}, bf16[32,1536]{1,0:T(8,128)(2,1)S(1)}, u32[]{:S(2)}, u32[]{:S(2)}) collective-permute-start(bf16[32,1536]{1,0:T(8,128)(2,1)S(1)} %get-tuple-element.308), channel_id=1, source_target_pairs={{0,68},{4,64},{64,4},{68,0},{1,69},{5,65},{65,5},{69,1},{2,70},{6,... | collective-permute-start | bytes 294920 | tf_op jit(solution)/shard_map/ppermute | solution.py:51
  469.0 9.5 %collective-permute-start.118 = (bf16[32,1536]{1,0:T(8,128)(2,1)S(1)}, bf16[32,1536]{1,0:T(8,128)(2,1)}, u32[]{:S(2)}, u32[]{:S(2)}) collective-permute-start(bf16[32,1536]{1,0:T(8,128)(2,1)S(1)} %get-tuple-element.309), channel_id=1, source_target_pairs={{0,64},{4,68},{64,0},{68,4},{1,65},{5,69},{65,1},{69,5},{2,66},{6,... | collective-permute-start | bytes 294920 | tf_op jit(solution)/shard_map/ppermute | solution.py:51
  493.5 8.7 %collective-permute-start.69 = (bf16[4,32,1536]{2,1,0:T(8,128)(2,1)}, bf16[4,32,1536]{2,1,0:T(8,128)(2,1)}, u32[]{:S(2)}, u32[]{:S(2)}) collective-permute-start(bf16[4,32,1536]{2,1,0:T(8,128)(2,1)} %bitcast.60), channel_id=1, source_target_pairs={{0,32},{32,0},{1,33},{33,1},{2,34},{34,2},{3,35},{35,3},{4,36},{36... | collective-permute-start | bytes 1179656 | tf_op jit(solution)/shard_map/ppermute | solution.py:35
  498.2 10.0 %collective-permute-start.130 = (bf16[256,256]{1,0:T(8,128)(2,1)S(1)}, bf16[256,256]{1,0:T(8,128)(2,1)S(1)}, u32[]{:S(2)}, u32[]{:S(2)}) collective-permute-start(bf16[256,256]{1,0:T(8,128)(2,1)S(1)} %get-tuple-element.148.pack_ref.refs_0_), channel_id=1, source_target_pairs={{0,11},{1,10},{2,9},{3,8},{8,3},{9,2},{10,1},{11,0},{4,15},{5,14},... | collective-permute-start | bytes 393224 | tf_op jit(solution)/shard_map/ppermute | solution.py:69
  501.2 18.9 %collective-permute-start.129 = (bf16[256,256]{1,0:T(8,128)(2,1)S(1)}, bf16[256,256]{1,0:T(8,128)(2,1)S(1)}, u32[]{:S(2)}, u32[]{:S(2)}) collective-permute-start(bf16[256,256]{1,0:T(8,128)(2,1)S(1)} %get-tuple-element.148.pack_ref.refs_0_), channel_id=1, source_target_pairs={{0,3},{1,2},{2,1},{3,0},{8,11},{9,10},{10,9},{11,8},{4,7},{5,6},{6... | collective-permute-start | bytes 393224 | tf_op jit(solution)/shard_map/ppermute | solution.py:69
  503.3 19.5 %collective-permute-start.128 = (bf16[256,256]{1,0:T(8,128)(2,1)S(1)}, bf16[256,256]{1,0:T(8,128)(2,1)S(1)}, u32[]{:S(2)}, u32[]{:S(2)}) collective-permute-start(bf16[256,256]{1,0:T(8,128)(2,1)S(1)} %get-tuple-element.148.pack_ref.refs_0_), channel_id=1, source_target_pairs={{0,10},{1,11},{2,8},{3,9},{8,2},{9,3},{10,0},{11,1},{4,14},{5,15},... | collective-permute-start | bytes 393224 | tf_op jit(solution)/shard_map/ppermute | solution.py:69
  503.4 19.9 %collective-permute-start.127 = (bf16[256,256]{1,0:T(8,128)(2,1)S(1)}, bf16[256,256]{1,0:T(8,128)(2,1)S(1)}, u32[]{:S(2)}, u32[]{:S(2)}) collective-permute-start(bf16[256,256]{1,0:T(8,128)(2,1)S(1)} %get-tuple-element.148.pack_ref.refs_0_), channel_id=1, source_target_pairs={{0,2},{1,3},{2,0},{3,1},{8,10},{9,11},{10,8},{11,9},{4,6},{5,7},{6... | collective-permute-start | bytes 393224 | tf_op jit(solution)/shard_map/ppermute | solution.py:69
  506.0 18.8 %collective-permute-start.126 = (bf16[256,256]{1,0:T(8,128)(2,1)S(1)}, bf16[256,256]{1,0:T(8,128)(2,1)S(1)}, u32[]{:S(2)}, u32[]{:S(2)}) collective-permute-start(bf16[256,256]{1,0:T(8,128)(2,1)S(1)} %get-tuple-element.148.pack_ref.refs_0_), channel_id=1, source_target_pairs={{0,9},{1,8},{2,11},{3,10},{8,1},{9,0},{10,3},{11,2},{4,13},{5,12},... | collective-permute-start | bytes 393224 | tf_op jit(solution)/shard_map/ppermute | solution.py:69
  508.1 18.0 %collective-permute-start.125 = (bf16[256,256]{1,0:T(8,128)(2,1)S(1)}, bf16[256,256]{1,0:T(8,128)(2,1)S(1)}, u32[]{:S(2)}, u32[]{:S(2)}) collective-permute-start(bf16[256,256]{1,0:T(8,128)(2,1)S(1)} %get-tuple-element.148.pack_ref.refs_0_), channel_id=1, source_target_pairs={{0,1},{1,0},{2,3},{3,2},{8,9},{9,8},{10,11},{11,10},{4,5},{5,4},{6... | collective-permute-start | bytes 393224 | tf_op jit(solution)/shard_map/ppermute | solution.py:69
  520.1 7.5 %collective-permute-start.124 = (bf16[256,256]{1,0:T(8,128)(2,1)S(1)}, bf16[256,256]{1,0:T(8,128)(2,1)S(1)}, u32[]{:S(2)}, u32[]{:S(2)}) collective-permute-start(bf16[256,256]{1,0:T(8,128)(2,1)S(1)} %get-tuple-element.148.pack_ref.refs_0_), channel_id=1, source_target_pairs={{0,8},{1,9},{2,10},{3,11},{8,0},{9,1},{10,2},{11,3},{4,12},{5,13},... | collective-permute-start | bytes 393224 | tf_op jit(solution)/shard_map/ppermute | solution.py:69
  522.8 14.5 %collective-permute-start.70 = (bf16[32,1536]{1,0:T(8,128)(2,1)S(1)}, bf16[32,1536]{1,0:T(8,128)(2,1)S(1)}, u32[]{:S(2)}, u32[]{:S(2)}) collective-permute-start(bf16[32,1536]{1,0:T(8,128)(2,1)S(1)} %get-tuple-element.322), channel_id=1, source_target_pairs={{0,4},{4,0},{64,68},{68,64},{1,5},{5,1},{65,69},{69,65},{2,6},{6,2... | collective-permute-start | bytes 294920 | tf_op jit(solution)/shard_map/ppermute | solution.py:51
  523.2 14.1 %collective-permute-start.72 = (bf16[32,1536]{1,0:T(8,128)(2,1)S(1)}, bf16[32,1536]{1,0:T(8,128)(2,1)S(1)}, u32[]{:S(2)}, u32[]{:S(2)}) collective-permute-start(bf16[32,1536]{1,0:T(8,128)(2,1)S(1)} %get-tuple-element.323), channel_id=1, source_target_pairs={{0,68},{4,64},{64,4},{68,0},{1,69},{5,65},{65,5},{69,1},{2,70},{6,... | collective-permute-start | bytes 294920 | tf_op jit(solution)/shard_map/ppermute | solution.py:51
  524.8 12.5 %collective-permute-start.71 = (bf16[32,1536]{1,0:T(8,128)(2,1)S(1)}, bf16[32,1536]{1,0:T(8,128)(2,1)S(1)}, u32[]{:S(2)}, u32[]{:S(2)}) collective-permute-start(bf16[32,1536]{1,0:T(8,128)(2,1)S(1)} %get-tuple-element.324), channel_id=1, source_target_pairs={{0,64},{4,68},{64,0},{68,4},{1,65},{5,69},{65,1},{69,5},{2,66},{6,... | collective-permute-start | bytes 294920 | tf_op jit(solution)/shard_map/ppermute | solution.py:51
  539.2 9.4 %collective-permute-start.132 = (bf16[48,1536]{1,0:T(8,128)(2,1)S(1)}, bf16[48,1536]{1,0:T(8,128)(2,1)S(1)}, u32[]{:S(2)}, u32[]{:S(2)}) collective-permute-start(bf16[48,1536]{1,0:T(8,128)(2,1)S(1)} %get-tuple-element.302), channel_id=1, source_target_pairs={{0,4},{4,0},{64,68},{68,64},{1,5},{5,1},{65,69},{69,65},{2,6},{6,2... | collective-permute-start | bytes 442376 | tf_op jit(solution)/shard_map/ppermute | solution.py:51
  539.6 9.0 %collective-permute-start.134 = (bf16[48,1536]{1,0:T(8,128)(2,1)S(1)}, bf16[48,1536]{1,0:T(8,128)(2,1)S(1)}, u32[]{:S(2)}, u32[]{:S(2)}) collective-permute-start(bf16[48,1536]{1,0:T(8,128)(2,1)S(1)} %get-tuple-element.303), channel_id=1, source_target_pairs={{0,68},{4,64},{64,4},{68,0},{1,69},{5,65},{65,5},{69,1},{2,70},{6,... | collective-permute-start | bytes 442376 | tf_op jit(solution)/shard_map/ppermute | solution.py:51
  541.2 7.5 %collective-permute-start.133 = (bf16[48,1536]{1,0:T(8,128)(2,1)S(1)}, bf16[48,1536]{1,0:T(8,128)(2,1)S(1)}, u32[]{:S(2)}, u32[]{:S(2)}) collective-permute-start(bf16[48,1536]{1,0:T(8,128)(2,1)S(1)} %get-tuple-element.304), channel_id=1, source_target_pairs={{0,64},{4,68},{64,0},{68,4},{1,65},{5,69},{65,1},{69,5},{2,66},{6,... | collective-permute-start | bytes 442376 | tf_op jit(solution)/shard_map/ppermute | solution.py:51
  543.2 84.6 %collective-permute-start.141 = (bf16[48,2304]{1,0:T(8,128)(2,1)}, bf16[48,2304]{1,0:T(8,128)(2,1)S(1)}, u32[]{:S(2)}, u32[]{:S(2)}) collective-permute-start(bf16[48,2304]{1,0:T(8,128)(2,1)} %get-tuple-element.305), channel_id=1, source_target_pairs={{0,4},{4,0},{1,5},{5,1},{2,6},{6,2},{3,7},{7,3},{8,12},{12,8},{9,1... | collective-permute-start | bytes 663560 | tf_op jit(solution)/shard_map/ppermute | solution.py:35
  549.6 14.7 %all-to-all-start = ((bf16[16,16,96]{2,1,0:T(8,128)(2,1)}), bf16[16,16,96]{2,1,0:T(8,128)(2,1)S(1)}, u32[]{:S(2)}, u32[]{:S(2)}) async-start(bf16[16,16,96]{2,1,0:T(8,128)(2,1)} %bitcast.305), calls=%async_computation.2 | async-start | bytes 131072 | tf_op jit(solution)/shard_map/all_to_all | solution.py:759
  554.8 11.3 %collective-permute-start.135 = (bf16[16,3072]{1,0:T(8,128)(2,1)S(1)}, bf16[16,3072]{1,0:T(8,128)(2,1)S(1)}, u32[]{:S(2)}, u32[]{:S(2)}) collective-permute-start(bf16[16,3072]{1,0:T(8,128)(2,1)S(1)} %get-tuple-element.342), channel_id=1, source_target_pairs={{0,16},{16,0},{1,17},{17,1},{2,18},{18,2},{3,19},{19,3},{4,20},{20... | collective-permute-start | bytes 294920 | tf_op jit(solution)/shard_map/ppermute | solution.py:35
  560.4 20.8 %collective-permute-start.142 = (bf16[1,4,96,768]{3,2,1,0:T(8,128)(2,1)}, bf16[1,4,96,768]{3,2,1,0:T(8,128)(2,1)S(1)}, u32[]{:S(2)}, u32[]{:S(2)}) collective-permute-start(bf16[1,4,96,768]{3,2,1,0:T(8,128)(2,1)} %get-tuple-element.250), channel_id=1, source_target_pairs={{0,1},{1,0},{2,3},{3,2},{4,5},{5,4},{6,7},{7,6},{8,9},{9,8},{10,11... | collective-permute-start | bytes 1769480 | tf_op jit(solution)/shard_map/ppermute | solution.py:112
  561.6 37.4 %collective-permute-start.144 = (bf16[1,4,96,768]{3,2,1,0:T(8,128)(2,1)}, bf16[1,4,96,768]{3,2,1,0:T(8,128)(2,1)}, u32[]{:S(2)}, u32[]{:S(2)}) collective-permute-start(bf16[1,4,96,768]{3,2,1,0:T(8,128)(2,1)} %get-tuple-element.251), channel_id=1, source_target_pairs={{0,2},{1,3},{2,0},{3,1},{4,6},{5,7},{6,4},{7,5},{8,10},{9,11},{10,... | collective-permute-start | bytes 1769480 | tf_op jit(solution)/shard_map/ppermute | solution.py:112
  564.0 38.6 %collective-permute-start.143 = (bf16[1,4,96,768]{3,2,1,0:T(8,128)(2,1)}, bf16[1,4,96,768]{3,2,1,0:T(8,128)(2,1)}, u32[]{:S(2)}, u32[]{:S(2)}) collective-permute-start(bf16[1,4,96,768]{3,2,1,0:T(8,128)(2,1)} %get-tuple-element.252), channel_id=1, source_target_pairs={{0,3},{1,2},{2,1},{3,0},{4,7},{5,6},{6,5},{7,4},{8,11},{9,10},{10,... | collective-permute-start | bytes 1769480 | tf_op jit(solution)/shard_map/ppermute | solution.py:112
  571.0 39.0 %collective-permute-start.137 = (bf16[2,2,16,3072]{3,2,1,0:T(8,128)(2,1)S(1)}, bf16[2,2,16,3072]{3,2,1,0:T(8,128)(2,1)S(1)}, u32[]{:S(2)}, u32[]{:S(2)}) collective-permute-start(bf16[2,2,16,3072]{3,2,1,0:T(8,128)(2,1)S(1)} %reverse_select_fusion.1), channel_id=1, source_target_pairs={{0,64},{64,0},{1,65},{65,1},{2,66},{66,2},{3,67},{67,3},{4,68},{68... | collective-permute-start | bytes 1179656 | tf_op jit(solution)/shard_map/ppermute | solution.py:35
  606.6 7.1 %collective-permute-start.146 = (bf16[1,1,96,768]{3,2,1,0:T(8,128)(2,1)S(1)}, bf16[1,1,96,768]{3,2,1,0:T(8,128)(2,1)S(1)}, u32[]{:S(2)}, u32[]{:S(2)}) collective-permute-start(bf16[1,1,96,768]{3,2,1,0:T(8,128)(2,1)S(1)} %get-tuple-element.301), channel_id=1, source_target_pairs={{0,24},{8,16},{16,8},{24,0},{1,25},{9,17},{17,9},{25,1},{2,26},{10... | collective-permute-start | bytes 442376 | tf_op jit(solution)/shard_map/ppermute | solution.py:112
  611.3 6.8 %collective-permute-start.138 = (bf16[48,3456]{1,0:T(8,128)(2,1)S(1)}, bf16[48,3456]{1,0:T(8,128)(2,1)S(1)}, u32[]{:S(2)}, u32[]{:S(2)}) collective-permute-start(bf16[48,3456]{1,0:T(8,128)(2,1)S(1)} %get-tuple-element.298), channel_id=1, source_target_pairs={{0,4},{4,0},{1,5},{5,1},{2,6},{6,2},{3,7},{7,3},{8,12},{12,8},{9,1... | collective-permute-start | bytes 995336 | tf_op jit(solution)/shard_map/ppermute | solution.py:35
  (270 other events, 2190.7 us)
Sparse Core Ops, SparseCore 0:
  25.4 69.8 all-gather.4
  98.1 75.9 all-gather.6
  245.3 54.4 all-gather.8
  303.0 34.8 all-gather.10
  364.1 88.9 reduce-scatter.2
  480.3 109.4 reduce-scatter.4
